TPU v7x, 256 devices: a whole 4x4x8 slice. The times are simulated.
256 devices in a mesh: cand: 32 (over x, z_hi, core), tp: 8 (over y, z_lo).
Axes of the slice: x: 4, y: 4, z: 8 (z_hi: 4, z_lo: 2; z = z_hi * 2 + z_lo), core: 2. Of those that a mesh axis runs over, the one named last changes fastest.
Arguments:
- hidden_in: bfloat16 [256, 2, 8192], P('cand'), may hold values from -4 to 4
- queries: bfloat16 [256, 2, 32, 128], P('cand', None, 'tp'), may hold values from -128 to 128
- new_kv: bfloat16 [256, 2, 8, 2, 128], P('cand', None, 'tp'), may hold values from -5 to 5
- kv_cache: bfloat16 [256, 8, 2, 512, 128], P('cand', 'tp'), may hold values from -6 to 6
- lengths: int32 [256], P('cand'), may hold values from 128 to 512, as said below
- winner: int32 [8], replicated, may hold values from 0 to 31
- out_values: bfloat16 [4096, 8192], P('tp'), may hold values from -4 to 4
- out_scales: float32 [32, 64], P('tp'), may hold values from 0.008 to 0.032
Outputs:
- mixed: bfloat16 [256, 2, 8192], P('cand')
Inputs may be any that keep to these rules, and one draw needn't show every extreme that they name: `lengths`: every draw has some row with exactly 512 live slots.
All inputs are finite; a program needn't handle non-finite values.
Results may differ from a plain program's by a relative error of at most 0.013.
Values may be sent and summed in bfloat16 or wider, within the bound.
No kernel may reach another device: no remote copies, remote signals or barrier semaphores. Data moves between devices by JAX's collectives and lax.ppermute only.
A program may use at most 64 MiB of HBM per device.

v0:
```python
import math

import jax
import jax.numpy as jnp
from jax import lax
from jax.sharding import PartitionSpec as P

BLOCK = 64
KB = 256


def from_root(block, axis, holder):
    block = jnp.where(lax.axis_index(axis) == holder, block, jnp.zeros_like(block))
    return lax.psum(block, axis)


def own_blocks(cache_rows, row_lengths):

    def take_block(cache_row, row_length):
        return lax.dynamic_slice_in_dim(cache_row, row_length - BLOCK, BLOCK, 2)

    return jax.vmap(take_block)(cache_rows, row_lengths)


def local(hidden_in, queries, new_kv, kv_cache, lengths, winner, out_values, out_scales):
    problems = kv_cache.shape[0]
    kv_here = kv_cache.shape[1]
    steps_count = queries.shape[1]
    heads_here = queries.shape[2]
    head_dim = queries.shape[3]
    group = heads_here // kv_here
    blocks = own_blocks(kv_cache, lengths)

    def send_one(problem, forked_now):
        piece = lax.dynamic_index_in_dim(blocks, problem, 0, keepdims=False)
        piece = from_root(piece, "cand", winner[problem])
        return lax.dynamic_update_index_in_dim(forked_now, piece, problem, 0)

    forked = lax.fori_loop(0, problems, send_one, jnp.zeros_like(blocks))
    grouped = queries.reshape(problems, steps_count, kv_here, group, head_dim)
    factor = 1.0 / math.sqrt(head_dim)

    def scores_of(keys):
        return (
            jnp.einsum("ptkgd,pkjd->ptkgj", grouped, keys, preferred_element_type=jnp.float32)
            * factor
        )

    def combine_values(weights, values):
        return jnp.einsum("ptkgj,pkjd->ptkgd", weights, values, preferred_element_type=jnp.float32)

    fresh = jnp.transpose(new_kv, (0, 2, 3, 1, 4))
    fork_scores = scores_of(forked[:, :, 0])
    new_scores = scores_of(fresh[:, :, 0])
    causal = jnp.arange(steps_count)[None, :] <= jnp.arange(steps_count)[:, None]
    new_scores = jnp.where(causal[None, :, None, None, :], new_scores, -jnp.inf)
    live = lengths - BLOCK
    count = kv_cache.shape[3] // KB

    def block_scores(index):
        piece = lax.dynamic_slice_in_dim(kv_cache, index * KB, KB, 3)
        scores = scores_of(piece[:, :, 0])
        slots = index * KB + jnp.arange(KB, dtype=jnp.int32)
        valid = slots[None, :] < live[:, None]
        scores = jnp.where(valid[:, None, None, None, :], scores, -jnp.inf)
        return (scores, piece[:, :, 1])

    peak = jnp.maximum(jnp.max(fork_scores, -1), jnp.max(new_scores, -1))
    total = jnp.sum(jnp.exp(fork_scores - peak[..., None]), -1) + jnp.sum(
        jnp.exp(new_scores - peak[..., None]), -1
    )

    def first_pass(index, carry):
        peak_now, total_now = carry
        scores, unused_values = block_scores(index)
        higher = jnp.maximum(peak_now, jnp.max(scores, -1))
        total_now = total_now * jnp.exp(peak_now - higher) + jnp.sum(
            jnp.exp(scores - higher[..., None]), -1
        )
        return (higher, total_now)

    peak, total = lax.fori_loop(0, count, first_pass, (peak, total))

    def weigh(scores):
        return (jnp.exp(scores - peak[..., None]) / total[..., None]).astype(jnp.bfloat16)

    summed = combine_values(weigh(fork_scores), forked[:, :, 1]) + combine_values(
        weigh(new_scores), fresh[:, :, 1]
    )

    def second_pass(index, summed_now):
        scores, values = block_scores(index)
        return summed_now + combine_values(weigh(scores), values)

    summed = lax.fori_loop(0, count, second_pass, summed)
    attended = summed.astype(jnp.bfloat16).reshape(problems * steps_count, heads_here * head_dim)
    blocks_here = out_scales.shape[0]
    side = out_values.shape[0] // blocks_here
    width = out_values.shape[1]
    partial_terms = jnp.einsum(
        "rbk,bkn->rbn",
        attended.reshape(-1, blocks_here, side),
        out_values.reshape(blocks_here, side, width),
        preferred_element_type=jnp.float32,
    )
    spread = jnp.repeat(out_scales, side, axis=1)
    term = jnp.sum(partial_terms * spread[None], axis=1)
    residual = hidden_in.reshape(problems * steps_count, width)
    totals = lax.psum(term.astype(jnp.bfloat16), "tp").astype(jnp.float32)
    result = (residual.astype(jnp.float32) + totals).astype(jnp.bfloat16)
    return result.reshape(hidden_in.shape)


def solution(mesh):
    placed = (
        P("cand", None, None),
        P("cand", None, "tp", None),
        P("cand", None, "tp", None, None),
        P("cand", "tp", None, None, None),
        P("cand"),
        P(),
        P("tp", None),
        P("tp", None),
    )
    return jax.shard_map(
        local, mesh=mesh, in_specs=placed, out_specs=P("cand", None, None), check_vma=False
    )
```

profile of v0, /device:TPU:6, one launch (start us, length us, event | category | flops | bytes accessed | tf_op | source)
XLA Modules:
  0.0 1232.5 jit_solution(9146878500982959980)
XLA Ops:
  6.6 0.7 copy.110
  7.3 1.0 convolution_multiply_fusion.4
  8.4 3.8 copy.75
  12.2 1.3 gather_fusion
  13.4 1105.0 %while.41 = (s32[]{:T(128)}, bf16[8,1,2,64,128]{4,3,0,2,1:T(8,128)(2,1)S(1)}, s32[8]{0:T(128)S(1)}, bf16[8,1,2,64,128]{4,2,3,0,1:T(2,128)(2,1)S(1)}, s32[]{:T(128)}, /*index=5*/u32[]{:T(128)}, u32[]{:T(128)}) while((s32[]{:T(128)}, bf16[8,1,2,64,128]{4,3,0,2,1:T(8,128)(2,1)S(1)}, s32[8]{0:T(128)S(1)}, ...), condition=%wide.region_2.3_spmd, body=%wide.region_0.2_spmd.sunk | while | flops 32774 | bytes 262283 | solution.py:39
  13.5 0.7 dynamic_slice.33
  14.9 126.2 %psum.20 = bf16[1,1,2,64,128]{4,3,2,1,0:T(8,128)(2,1)S(1)} all-reduce(bf16[1,1,2,64,128]{4,3,2,1,0:T(8,128)(2,1)S(1)} %copy_select_fusion.2), channel_id=1, replica_groups=mesh['cand'=32,'tp'=8] {'cand'}, use_global_device_ids=true, to_apply=%region_1.1 | all-reduce | flops 16384 | bytes 65536 | tf_op jit(solution)/shard_map/while/body/eval_jaxpr/psum | solution.py:14
  141.1 0.7 dynamic_slice.33
  142.5 138.2 %psum.20 = bf16[1,1,2,64,128]{4,3,2,1,0:T(8,128)(2,1)S(1)} all-reduce(bf16[1,1,2,64,128]{4,3,2,1,0:T(8,128)(2,1)S(1)} %copy_select_fusion.2), channel_id=1, replica_groups=mesh['cand'=32,'tp'=8] {'cand'}, use_global_device_ids=true, to_apply=%region_1.1 | all-reduce | flops 16384 | bytes 65536 | tf_op jit(solution)/shard_map/while/body/eval_jaxpr/psum | solution.py:14
  282.2 138.2 %psum.20 = bf16[1,1,2,64,128]{4,3,2,1,0:T(8,128)(2,1)S(1)} all-reduce(bf16[1,1,2,64,128]{4,3,2,1,0:T(8,128)(2,1)S(1)} %copy_select_fusion.2), channel_id=1, replica_groups=mesh['cand'=32,'tp'=8] {'cand'}, use_global_device_ids=true, to_apply=%region_1.1 | all-reduce | flops 16384 | bytes 65536 | tf_op jit(solution)/shard_map/while/body/eval_jaxpr/psum | solution.py:14
  421.8 138.2 %psum.20 = bf16[1,1,2,64,128]{4,3,2,1,0:T(8,128)(2,1)S(1)} all-reduce(bf16[1,1,2,64,128]{4,3,2,1,0:T(8,128)(2,1)S(1)} %copy_select_fusion.2), channel_id=1, replica_groups=mesh['cand'=32,'tp'=8] {'cand'}, use_global_device_ids=true, to_apply=%region_1.1 | all-reduce | flops 16384 | bytes 65536 | tf_op jit(solution)/shard_map/while/body/eval_jaxpr/psum | solution.py:14
  560.0 0.7 dynamic_slice.33
  561.4 138.2 %psum.20 = bf16[1,1,2,64,128]{4,3,2,1,0:T(8,128)(2,1)S(1)} all-reduce(bf16[1,1,2,64,128]{4,3,2,1,0:T(8,128)(2,1)S(1)} %copy_select_fusion.2), channel_id=1, replica_groups=mesh['cand'=32,'tp'=8] {'cand'}, use_global_device_ids=true, to_apply=%region_1.1 | all-reduce | flops 16384 | bytes 65536 | tf_op jit(solution)/shard_map/while/body/eval_jaxpr/psum | solution.py:14
  699.6 0.7 dynamic_slice.33
  701.0 138.2 %psum.20 = bf16[1,1,2,64,128]{4,3,2,1,0:T(8,128)(2,1)S(1)} all-reduce(bf16[1,1,2,64,128]{4,3,2,1,0:T(8,128)(2,1)S(1)} %copy_select_fusion.2), channel_id=1, replica_groups=mesh['cand'=32,'tp'=8] {'cand'}, use_global_device_ids=true, to_apply=%region_1.1 | all-reduce | flops 16384 | bytes 65536 | tf_op jit(solution)/shard_map/while/body/eval_jaxpr/psum | solution.py:14
  840.6 138.2 %psum.20 = bf16[1,1,2,64,128]{4,3,2,1,0:T(8,128)(2,1)S(1)} all-reduce(bf16[1,1,2,64,128]{4,3,2,1,0:T(8,128)(2,1)S(1)} %copy_select_fusion.2), channel_id=1, replica_groups=mesh['cand'=32,'tp'=8] {'cand'}, use_global_device_ids=true, to_apply=%region_1.1 | all-reduce | flops 16384 | bytes 65536 | tf_op jit(solution)/shard_map/while/body/eval_jaxpr/psum | solution.py:14
  980.3 138.2 %psum.20 = bf16[1,1,2,64,128]{4,3,2,1,0:T(8,128)(2,1)S(1)} all-reduce(bf16[1,1,2,64,128]{4,3,2,1,0:T(8,128)(2,1)S(1)} %copy_select_fusion.2), channel_id=1, replica_groups=mesh['cand'=32,'tp'=8] {'cand'}, use_global_device_ids=true, to_apply=%region_1.1 | all-reduce | flops 16384 | bytes 65536 | tf_op jit(solution)/shard_map/while/body/eval_jaxpr/psum | solution.py:14
  1119.1 1.7 copy.84
  1121.2 1.9 while.42
  1123.9 1.3 while.43
  1125.5 5.4 fusion.24
  1131.0 92.8 %all-reduce.2.cloned.1.call-done = bf16[16,8192]{1,0:T(8,128)(2,1)} async-done(((bf16[16,8192]{1,0:T(8,128)(2,1)}), bf16[16,8192]{1,0:T(8,128)(2,1)}) %all-reduce.2.cloned.1.call-update) | async-done | bytes 262160 | tf_op jit(solution)/shard_map/psum | solution.py:109
  1223.8 1.0 add_convert_fusion
  1224.8 0.9 reshape.271
  (94 shorter events, 8.3 us)
Async XLA Ops:
  6.5 1118.7 %copy-start = (f32[4,64]{1,0:T(4,128)S(1)}, f32[4,64]{1,0:T(4,128)}, u32[]{:S(2)}) copy-start(f32[4,64]{1,0:T(4,128)} %param.21) | copy-start | bytes 3076
  6.5 1217.3 %all-reduce.2.cloned.1.call-start = ((), (), s32[]{:S(2)}) async-start(), calls=%async_computation | async-start | bytes 524288 | tf_op jit(solution)/shard_map/psum | solution.py:109
  8.3 3.8 copy-start.4
  8.3 5.1 copy-start.3
  8.3 1110.1 %copy-start.1 = (bf16[8,2,4,128]{3,2,1,0:T(4,128)(2,1)S(1)}, bf16[8,2,4,128]{3,2,1,0:T(4,128)(2,1)}, u32[]{:S(2)}) copy-start(bf16[8,2,4,128]{3,2,1,0:T(4,128)(2,1)} %param.15) | copy-start | bytes 49156
  1125.4 5.5 copy-start.2
Sparse Core Ops, SparseCore 0:
  1131.0 92.7 all-reduce.1
where the time goes:
time: 1230 us
  blocking collectives  1090 us (89%)
  waiting for transfers between devices  92.8 us (8%)
  local copies, waits for them, and re-layouts  15.9 us (1%)
  between operations  13.6 us (1%)
    psum x8, blocking collectives, from_root(): return lax.psum(block, axis)  1090 us
    psum x1, waiting for transfers between devices, local(): totals = lax.psum(term.astype(jnp.bfloat16), 'tp').astype(jnp.float32)  92.8 us
  transfers between devices with their start and end apart: 1, of which 1 were waited for; matrix products, arithmetic and copies ran while one was open for 0% of the time, Pallas kernels for 0%

commit v1 on v0

v1 whole, which is shorter than its diff:
```python
import functools
import math

import jax
import jax.numpy as jnp
from jax import lax
from jax.experimental import pallas as pl
from jax.experimental.pallas import tpu as pltpu
from jax.sharding import PartitionSpec as P

BLOCK = 64
WINDOW = 80
CHUNK = 1024
VMEM = pl.BlockSpec(memory_space=pltpu.VMEM)
SMEM = pl.BlockSpec(memory_space=pltpu.SMEM)
ANY = pl.BlockSpec(memory_space=pl.ANY)
NT = (((1,), (1,)), ((), ()))


def exchange(x, axis, size, bit):
    return lax.ppermute(x, axis, [(i, i ^ bit) for i in range(size)])


def extract_kernel(lengths, winner, place, cache, keep, send, window, sems):
    problems = cache.shape[0]
    half = problems // 2

    def start_of(p):
        first = lengths[p] - BLOCK
        start = jnp.minimum((first // 16) * 16, cache.shape[3] - WINDOW)
        return pl.multiple_of(start, 16), first - start

    copies = []
    for p in range(problems):
        start, _ = start_of(p)
        copies.append(
            pltpu.make_async_copy(cache.at[p, 0, :, pl.ds(start, WINDOW), :], window.at[p], sems.at[p])
        )
        copies[-1].start()
    for p in range(problems):
        copies[p].wait()
    rows = lax.broadcasted_iota(jnp.int32, (16, 128), 0)
    for j in range(problems):
        p = j ^ (place[1] * half)
        _, offset = start_of(p)
        mine = winner[p] == place[0]
        where = (keep if j < half else send, j % half)
        for kv in range(2):
            head = jnp.where(
                rows < offset,
                window[p, kv, 64:80, :].astype(jnp.float32),
                window[p, kv, 0:16, :].astype(jnp.float32),
            )
            head = jnp.where(mine, head, 0.0).astype(jnp.bfloat16)
            tail = window[p, kv, 16:64, :].astype(jnp.float32)
            tail = jnp.where(mine, tail, 0.0).astype(jnp.bfloat16)
            base = where[1] * BLOCK
            where[0][kv, base : base + 16, :] = head
            where[0][kv, base + 16 : base + BLOCK, :] = tail


def old_kernel(lengths, queries, new_keys, new_values, cache, out, peak, total, held, sems, *, factor):
    problems = cache.shape[0]
    group = queries.shape[1] // 2
    copies = []
    for p in range(problems):
        copies.append(pltpu.make_async_copy(cache.at[p, 0], held.at[p], sems.at[p]))
        copies[-1].start()
    slots = lax.broadcasted_iota(jnp.int32, (queries.shape[1], cache.shape[3]), 1)
    later = lax.broadcasted_iota(jnp.int32, (queries.shape[1], 1), 0) >= group
    for p in range(problems):
        query = queries[p]
        wide = query.astype(jnp.float32)
        keys = [new_keys[p, u : u + 1, :].astype(jnp.float32) for u in range(2)]
        fresh = [jnp.sum(wide * key, -1, keepdims=True) * factor for key in keys]
        fresh[1] = jnp.where(later, fresh[1], -jnp.inf)
        copies[p].wait()
        scores = lax.dot_general(query, held[p, 0], NT, preferred_element_type=jnp.float32) * factor
        scores = jnp.where(slots < lengths[p] - BLOCK, scores, -jnp.inf)
        top = jnp.maximum(jnp.max(scores, -1, keepdims=True), jnp.maximum(fresh[0], fresh[1]))
        weights = jnp.exp(scores - top)
        sums = jnp.sum(weights, -1, keepdims=True)
        mixed = jnp.dot(weights.astype(jnp.bfloat16), held[p, 1], preferred_element_type=jnp.float32)
        for u in range(2):
            weight = jnp.exp(fresh[u] - top)
            sums = sums + weight
            mixed = mixed + weight * new_values[p, u : u + 1, :].astype(jnp.float32)
        out[p] = mixed
        peak[p] = jnp.broadcast_to(top, mixed.shape)
        total[p] = jnp.broadcast_to(sums, mixed.shape)


def start_weights(weights, held, sems, base):
    chunks = held.shape[1] // CHUNK
    copies = []
    for c in range(chunks):
        columns = pl.multiple_of(base + c * CHUNK, CHUNK)
        copies.append(
            pltpu.make_async_copy(
                weights.at[:, pl.ds(columns, CHUNK)], held.at[:, c * CHUNK : (c + 1) * CHUNK], sems.at[c]
            )
        )
        copies[-1].start()
    return copies


def project(attended, scales, held, copies, base, out):
    blocks, side = scales.shape[0], held.shape[0] // scales.shape[0]
    parts = [attended[pl.ds(b, 16, stride=blocks), :].astype(jnp.bfloat16) for b in range(blocks)]
    first = base // 128
    for c, copy in enumerate(copies):
        copy.wait()
        columns = slice(c * CHUNK, (c + 1) * CHUNK)
        terms = [
            jnp.dot(parts[b], held[b * side : (b + 1) * side, columns], preferred_element_type=jnp.float32)
            for b in range(blocks)
        ]
        for n in range(CHUNK // 128):
            block = first + c * (CHUNK // 128) + n
            sums = 0.0
            for b in range(blocks):
                sums = sums + terms[b][:, n * 128 : (n + 1) * 128] * scales[b, block]
            out[:, c * CHUNK + n * 128 : c * CHUNK + (n + 1) * 128] = sums.astype(out.dtype)


def fork_kernel(place, queries, mine, other, old, peak, total, scales, weights, attended, out, held, sems, *, factor):
    width = held.shape[1]
    base = (1 - place[2]) * width
    copies = start_weights(weights, held, sems, base)
    rows, keys_here = queries.shape[0], mine.shape[1]
    per_row = rows // (2 * keys_here // BLOCK)
    halves = []
    for half, ref in ((place[1], mine), (1 - place[1], other)):
        scores = lax.dot_general(queries[...], ref[0], NT, preferred_element_type=jnp.float32) * factor
        row = lax.broadcasted_iota(jnp.int32, scores.shape, 0) // per_row
        owner = lax.broadcasted_iota(jnp.int32, scores.shape, 1) // BLOCK + half * (keys_here // BLOCK)
        halves.append(jnp.where(row == owner, scores, -jnp.inf))
    top = jnp.maximum(jnp.max(halves[0], -1, keepdims=True), jnp.max(halves[1], -1, keepdims=True))
    top = jnp.maximum(peak[...], top)
    kept = jnp.exp(peak[...] - top)
    sums = total[...] * kept
    mixed = old[...] * kept
    for scores, ref in zip(halves, (mine, other)):
        share = jnp.exp(scores - top[:, :1])
        sums = sums + jnp.sum(share, -1, keepdims=True)
        mixed = mixed + jnp.dot(share.astype(jnp.bfloat16), ref[1], preferred_element_type=jnp.float32)
    attended[...] = (mixed / sums).astype(jnp.bfloat16).astype(jnp.float32)
    project(attended, scales, held, copies, base, out)


def project_kernel(place, attended, scales, weights, out, held, sems):
    base = place[2] * held.shape[1]
    copies = start_weights(weights, held, sems, base)
    project(attended, scales, held, copies, base, out)


def params(mib, flops, size):
    return dict(
        compiler_params=pltpu.CompilerParams(vmem_limit_bytes=mib * 2**20),
        cost_estimate=pl.CostEstimate(flops=flops, bytes_accessed=size, transcendentals=0),
    )


def local(hidden_in, queries, new_kv, kv_cache, lengths, winner, out_values, out_scales):
    problems, _, _, slots, head_dim = kv_cache.shape
    steps, heads = queries.shape[1], queries.shape[2]
    width = out_values.shape[1]
    factor = 1.0 / math.sqrt(head_dim)
    cand, tp = lax.axis_index("cand"), lax.axis_index("tp")
    place = jnp.stack([cand, cand % 2, tp % 2]).astype(jnp.int32)
    half = width // 2
    bf16, f32 = jnp.bfloat16, jnp.float32

    fork_shape = jax.ShapeDtypeStruct((2, problems // 2 * BLOCK, head_dim), bf16)
    keep, send = pl.pallas_call(
        extract_kernel,
        out_shape=(fork_shape, fork_shape),
        in_specs=[SMEM, SMEM, SMEM, ANY],
        out_specs=(VMEM, VMEM),
        scratch_shapes=[
            pltpu.VMEM((problems, 2, WINDOW, head_dim), bf16),
            pltpu.SemaphoreType.DMA((problems,)),
        ],
        **params(4, 0, 2**19),
    )(lengths, winner, place, kv_cache)

    grouped = queries.reshape(problems, steps * heads, head_dim)
    rows = problems * steps * heads
    partial = jax.ShapeDtypeStruct((problems, steps * heads, head_dim), f32)
    old, peak, total = pl.pallas_call(
        functools.partial(old_kernel, factor=factor),
        out_shape=(partial,) * 3,
        in_specs=[SMEM, VMEM, VMEM, VMEM, ANY],
        out_specs=(VMEM,) * 3,
        scratch_shapes=[
            pltpu.VMEM((problems, 2, slots, head_dim), bf16),
            pltpu.SemaphoreType.DMA((problems,)),
        ],
        **params(8, 2**24, 2**21),
    )(lengths, grouped, new_kv[:, :, 0, 0], new_kv[:, :, 0, 1], kv_cache)

    block = keep + exchange(send, "cand", 32, 1)
    for bit in (8, 16, 2, 4):
        block = block + exchange(block, "cand", 32, bit)
    other = exchange(block, "cand", 32, 1)

    flat = (rows, head_dim)
    half_shape = jax.ShapeDtypeStruct((problems * steps, half), bf16)
    scratch = [pltpu.VMEM((out_values.shape[0], half), bf16), pltpu.SemaphoreType.DMA((half // CHUNK,))]
    attended, away = pl.pallas_call(
        functools.partial(fork_kernel, factor=factor),
        out_shape=(jax.ShapeDtypeStruct(flat, f32), half_shape),
        in_specs=[SMEM] + [VMEM] * 6 + [SMEM, ANY],
        out_specs=(VMEM, VMEM),
        scratch_shapes=scratch,
        **params(12, 2**26, 2**22),
    )(
        place,
        grouped.reshape(flat),
        block,
        other,
        old.reshape(flat),
        peak.reshape(flat),
        total.reshape(flat),
        out_scales,
        out_values,
    )
    arrived = exchange(away, "tp", 8, 1)
    home = pl.pallas_call(
        project_kernel,
        out_shape=half_shape,
        in_specs=[SMEM, VMEM, SMEM, ANY],
        out_specs=VMEM,
        scratch_shapes=scratch,
        **params(12, 2**26, 2**22),
    )(place, attended, out_scales, out_values)

    sums = home + arrived
    for bit in (2, 4):
        sums = sums + exchange(sums, "tp", 8, bit)
    residual = hidden_in.reshape(problems * steps, width)
    residual = lax.dynamic_slice_in_dim(residual, (tp % 2) * half, half, 1)
    mixed = (residual.astype(f32) + sums.astype(f32)).astype(bf16)
    neighbour = exchange(mixed, "tp", 8, 1)
    first = tp % 2 == 0
    result = jnp.concatenate(
        [jnp.where(first, mixed, neighbour), jnp.where(first, neighbour, mixed)], axis=1
    )
    return result.reshape(hidden_in.shape)


def solution(mesh):
    placed = (
        P("cand", None, None),
        P("cand", None, "tp", None),
        P("cand", None, "tp", None, None),
        P("cand", "tp", None, None, None),
        P("cand"),
        P(),
        P("tp", None),
        P("tp", None),
    )
    return jax.shard_map(
        local, mesh=mesh, in_specs=placed, out_specs=P("cand", None, None), check_vma=False
    )
```

time: 1230 us -> 74.7 us (0.06)
  blocking collectives: 1090 us -> 0 us
  waiting for transfers between devices: 92.8 us -> 32.2 us
  starting transfers between devices: 0.01 us -> 18.8 us
  between operations: 13.6 us -> 0.16 us
    psum x8 -> x0, blocking collectives: 1090 us -> none  [from_root(): return lax.psum(block, axis)]
    psum x1 -> x0, waiting for transfers between devices: 92.8 us -> none  [local(): totals = lax.psum(term.astype(jnp.bfloat16), 'tp').astype(jnp.float32)]
    ppermute x0 -> x10, waiting for transfers between devices: none -> 32.2 us  [exchange(): return lax.ppermute(x, axis, [(i, i ^ bit) for i in range(size)])]
    ppermute x0 -> x10, starting transfers between devices: none -> 18.8 us  [exchange(): return lax.ppermute(x, axis, [(i, i ^ bit) for i in range(size)])]
  transfers between devices with their start and end apart: 1 -> 10, of which waited for: 1 -> 9; matrix products, arithmetic and copies ran while one was open for 0% -> 1% of each run, Pallas kernels for 0% -> 8%
where the time goes in v1:
time: 74.7 us; the launch traced here: 74.2 us
  waiting for transfers between devices  32.2 us (43%)
  starting transfers between devices  18.8 us (25%)
  local copies, waits for them, and re-layouts  13 us (17%)
  Pallas kernels  9.61 us (13%)
    ppermute x10, waiting for transfers between devices, exchange(): return lax.ppermute(x, axis, [(i, i ^ bit) for i in range(size)])  32.2 us
    ppermute x10, starting transfers between devices, exchange(): return lax.ppermute(x, axis, [(i, i ^ bit) for i in range(size)])  18.8 us
    unnamed x22, local copies, waits for them, and re-layouts  11.2 us
    pallas_call x1, Pallas kernels, local(): pl.pallas_call(functools.partial(old_kernel, factor=factor), out_shape=(p...  3.7 us
    pallas_call x1, Pallas kernels, local(): pl.pallas_call(functools.partial(fork_kernel, factor=factor), out_shape=(...  2.69 us
    pallas_call x1, Pallas kernels, local(): pl.pallas_call(project_kernel, out_shape=half_shape, in_specs=[SMEM, VMEM...  2.2 us
  transfers between devices with their start and end apart: 10, of which 9 were waited for; matrix products, arithmetic and copies ran while one was open for 1% of the time, Pallas kernels for 8%

profile of v1, /device:TPU:6, one launch (start us, length us, event | category | flops | bytes accessed | tf_op | source)
XLA Modules:
  0.0 74.2 jit_solution(11227876113478403686)
XLA Ops:
  0.1 1.6 %copy-done.2 = bf16[8,1,2,512,128]{4,3,2,1,0:T(8,128)(2,1)S(1)} copy-done((bf16[8,1,2,512,128]{4,3,2,1,0:T(8,128)(2,1)S(1)}, bf16[8,1,2,512,128]{4,3,2,1,0:T(8,128)(2,1)}, u32[]{:S(2)}) %copy-start.2) | copy-done | bytes 2097176
  3.0 1.0 %shard_map.82 = (bf16[2,256,128]{2,1,0:T(8,128)(2,1)S(1)}, bf16[2,256,128]{2,1,0:T(8,128)(2,1)S(1)}) custom-call(s32[8]{0:T(128)S(1)} %copy-done.7, s32[8]{0:T(128)S(1)} %copy-done.9, s32[3]{0:T(128)S(1)} %pad_add_fusion.place, bf16[8,1,2,512,128]{4,3,2,1,0:T(8,128)(2,1)S(1)} %copy-done.2), custom_call_target="tpu_custom_call" | custom-call | bytes 524288 | tf_op jit(solution)/shard_map/pallas_call | solution.py:175
  4.1 1.3 %collective-permute-done = bf16[2,256,128]{2,1,0:T(8,128)(2,1)S(1)} collective-permute-done((bf16[2,256,128]{2,1,0:T(8,128)(2,1)S(1)}, bf16[2,256,128]{2,1,0:T(8,128)(2,1)S(1)}, u32[]{:S(2)}, u32[]{:S(2)}) %collective-permute-start) | collective-permute-done | bytes 131104 | tf_op jit(solution)/shard_map/ppermute | solution.py:21
  5.5 0.9 %collective-permute-start.1 = (bf16[2,256,128]{2,1,0:T(8,128)(2,1)S(1)}, bf16[2,256,128]{2,1,0:T(8,128)(2,1)S(1)}, u32[]{:S(2)}, u32[]{:S(2)}) collective-permute-start(bf16[2,256,128]{2,1,0:T(8,128)(2,1)S(1)} %add.42), channel_id=1, source_target_pairs={{0,64},{8,72},{16,80},{24,88},{32,96},{40,104},{48,112},{56,120},{... | collective-permute-start | bytes 393224 | tf_op jit(solution)/shard_map/ppermute | solution.py:21
  6.4 4.7 %collective-permute-done.1 = bf16[2,256,128]{2,1,0:T(8,128)(2,1)S(1)} collective-permute-done((bf16[2,256,128]{2,1,0:T(8,128)(2,1)S(1)}, bf16[2,256,128]{2,1,0:T(8,128)(2,1)S(1)}, u32[]{:S(2)}, u32[]{:S(2)}) %collective-permute-start.1) | collective-permute-done | bytes 131104 | tf_op jit(solution)/shard_map/ppermute | solution.py:21
  11.2 2.0 %collective-permute-start.2 = (bf16[2,256,128]{2,1,0:T(8,128)(2,1)S(1)}, bf16[2,256,128]{2,1,0:T(8,128)(2,1)S(1)}, u32[]{:S(2)}, u32[]{:S(2)}) collective-permute-start(bf16[2,256,128]{2,1,0:T(8,128)(2,1)S(1)} %add.43), channel_id=1, source_target_pairs={{0,128},{8,136},{16,144},{24,152},{32,160},{40,168},{48,176},{56,1... | collective-permute-start | bytes 393224 | tf_op jit(solution)/shard_map/ppermute | solution.py:21
  13.2 4.5 %collective-permute-done.2 = bf16[2,256,128]{2,1,0:T(8,128)(2,1)S(1)} collective-permute-done((bf16[2,256,128]{2,1,0:T(8,128)(2,1)S(1)}, bf16[2,256,128]{2,1,0:T(8,128)(2,1)S(1)}, u32[]{:S(2)}, u32[]{:S(2)}) %collective-permute-start.2) | collective-permute-done | bytes 131104 | tf_op jit(solution)/shard_map/ppermute | solution.py:21
  17.8 3.4 %collective-permute-start.3 = (bf16[2,256,128]{2,1,0:T(8,128)(2,1)S(1)}, bf16[2,256,128]{2,1,0:T(8,128)(2,1)S(1)}, u32[]{:S(2)}, u32[]{:S(2)}) collective-permute-start(bf16[2,256,128]{2,1,0:T(8,128)(2,1)S(1)} %add.44), channel_id=1, source_target_pairs={{0,16},{8,24},{16,0},{24,8},{32,48},{40,56},{48,32},{56,40},{64,80... | collective-permute-start | bytes 393224 | tf_op jit(solution)/shard_map/ppermute | solution.py:21
  21.1 4.6 %collective-permute-done.3 = bf16[2,256,128]{2,1,0:T(8,128)(2,1)S(1)} collective-permute-done((bf16[2,256,128]{2,1,0:T(8,128)(2,1)S(1)}, bf16[2,256,128]{2,1,0:T(8,128)(2,1)S(1)}, u32[]{:S(2)}, u32[]{:S(2)}) %collective-permute-start.3) | collective-permute-done | bytes 131104 | tf_op jit(solution)/shard_map/ppermute | solution.py:21
  25.8 6.7 %collective-permute-start.4 = (bf16[2,256,128]{2,1,0:T(8,128)(2,1)S(1)}, bf16[2,256,128]{2,1,0:T(8,128)(2,1)S(1)}, u32[]{:S(2)}, u32[]{:S(2)}) collective-permute-start(bf16[2,256,128]{2,1,0:T(8,128)(2,1)S(1)} %add.45), channel_id=1, source_target_pairs={{0,32},{8,40},{16,48},{24,56},{32,0},{40,8},{48,16},{56,24},{64,96... | collective-permute-start | bytes 393224 | tf_op jit(solution)/shard_map/ppermute | solution.py:21
  32.6 0.8 %fusion = (bf16[8,2,1,1,128]{4,3,2,1,0:T(2,128)(2,1)S(1)}, bf16[8,2,1,1,128]{4,3,2,1,0:T(2,128)(2,1)S(1)}) fusion(bf16[8,2,1,2,128]{4,3,2,1,0:T(2,128)(2,1)} %param.10), kind=kLoop, calls=%fused_computation.7 | loop fusion | bytes 16384 | tf_op jit(solution)/shard_map/slice | solution.py:200
  33.3 2.7 %collective-permute-done.4 = bf16[2,256,128]{2,1,0:T(8,128)(2,1)S(1)} collective-permute-done((bf16[2,256,128]{2,1,0:T(8,128)(2,1)S(1)}, bf16[2,256,128]{2,1,0:T(8,128)(2,1)S(1)}, u32[]{:S(2)}, u32[]{:S(2)}) %collective-permute-start.4) | collective-permute-done | bytes 131104 | tf_op jit(solution)/shard_map/ppermute | solution.py:21
  36.2 1.6 %copy-done.3 = bf16[8,1,2,512,128]{4,3,2,1,0:T(8,128)(2,1)S(1)} copy-done((bf16[8,1,2,512,128]{4,3,2,1,0:T(8,128)(2,1)S(1)}, bf16[8,1,2,512,128]{4,3,2,1,0:T(8,128)(2,1)}, u32[]{:S(2)}) %copy-start.3) | copy-done | bytes 2097176
  39.1 3.7 %shard_map.83 = (f32[8,8,128]{2,1,0:T(8,128)S(1)}, f32[8,8,128]{2,1,0:T(8,128)S(1)}, f32[8,8,128]{2,1,0:T(8,128)S(1)}) custom-call(s32[8]{0:T(128)S(1)} %copy-done.8, bf16[8,8,128]{2,1,0:T(8,128)(2,1)S(1)} %bitcast.12, bf16[8,2,128]{2,1,0:T(2,128)(2,1)S(1)} %get-tuple-element.24.new_keys, bf16[8,2,128]{2,1,0:T(2,128)(2,1)S(1)} %get-tuple-element.23.new_values, ...), custom_call_target="tpu_custom_call" | custom-call | flops 16777216 | bytes 2097152 | tf_op jit(solution)/shard_map/pallas_call | solution.py:190
  42.9 3.4 %copy-done = bf16[512,8192]{1,0:T(8,128)(2,1)S(1)} copy-done((bf16[512,8192]{1,0:T(8,128)(2,1)S(1)}, bf16[512,8192]{1,0:T(8,128)(2,1)}, u32[]{:S(2)}) %copy-start) | copy-done | bytes 8388632
  47.7 2.7 %shard_map.84 = (f32[64,128]{1,0:T(8,128)S(1)}, bf16[16,4096]{1,0:T(8,128)(2,1)S(1)}) custom-call(s32[3]{0:T(128)S(1)} %pad_add_fusion.place, bf16[64,128]{1,0:T(8,128)(2,1)S(1)} %bitcast.13, bf16[2,256,128]{2,1,0:T(8,128)(2,1)S(1)} %add.46.mine, bf16[2,256,128]{2,1,0:T(8,128)(2,1)S(1)} %collective-permute-done.5.other, f32[64,128]{1,0:T(8,128)S(1)} %bitcast.14, ...), custom_call_target="tpu_custom_call" | custom-call | flops 67108864 | bytes 4194304 | tf_op jit(solution)/shard_map/pallas_call | solution.py:210
  51.0 2.2 %shard_map.85 = bf16[16,4096]{1,0:T(8,128)(2,1)S(1)} custom-call(s32[3]{0:T(128)S(1)} %pad_add_fusion.place, f32[64,128]{1,0:T(8,128)S(1)} %get-tuple-element.17.attended, f32[4,64]{1,0:T(4,128)S(1)} %copy-done.6, bf16[512,8192]{1,0:T(8,128)(2,1)S(1)} %copy-done.1), custom_call_target="tpu_custom_call" | custom-call | flops 67108864 | bytes 4194304 | tf_op jit(solution)/shard_map/pallas_call | solution.py:229
  53.2 3.1 %collective-permute-done.6 = bf16[16,4096]{1,0:T(8,128)(2,1)S(1)} collective-permute-done((bf16[16,4096]{1,0:T(8,128)(2,1)S(1)}, bf16[16,4096]{1,0:T(8,128)(2,1)S(1)}, u32[]{:S(2)}, u32[]{:S(2)}) %collective-permute-start.6) | collective-permute-done | bytes 131104 | tf_op jit(solution)/shard_map/ppermute | solution.py:21
  56.4 1.7 %collective-permute-start.7 = (bf16[16,4096]{1,0:T(8,128)(2,1)S(1)}, bf16[16,4096]{1,0:T(8,128)(2,1)S(1)}, u32[]{:S(2)}, u32[]{:S(2)}) collective-permute-start(bf16[16,4096]{1,0:T(8,128)(2,1)S(1)} %add.47), channel_id=1, source_target_pairs={{0,2},{1,3},{2,0},{3,1},{4,6},{5,7},{6,4},{7,5},{8,10},{9,11},{10,... | collective-permute-start | bytes 393224 | tf_op jit(solution)/shard_map/ppermute | solution.py:21
  58.0 3.5 %collective-permute-done.7 = bf16[16,4096]{1,0:T(8,128)(2,1)S(1)} collective-permute-done((bf16[16,4096]{1,0:T(8,128)(2,1)S(1)}, bf16[16,4096]{1,0:T(8,128)(2,1)S(1)}, u32[]{:S(2)}, u32[]{:S(2)}) %collective-permute-start.7) | collective-permute-done | bytes 131104 | tf_op jit(solution)/shard_map/ppermute | solution.py:21
  61.6 3.3 %collective-permute-start.8 = (bf16[16,4096]{1,0:T(8,128)(2,1)S(1)}, bf16[16,4096]{1,0:T(8,128)(2,1)S(1)}, u32[]{:S(2)}, u32[]{:S(2)}) collective-permute-start(bf16[16,4096]{1,0:T(8,128)(2,1)S(1)} %add.48), channel_id=1, source_target_pairs={{0,4},{1,5},{2,6},{3,7},{4,0},{5,1},{6,2},{7,3},{8,12},{9,13},{10,... | collective-permute-start | bytes 393224 | tf_op jit(solution)/shard_map/ppermute | solution.py:21
  65.0 3.2 %collective-permute-done.8 = bf16[16,4096]{1,0:T(8,128)(2,1)S(1)} collective-permute-done((bf16[16,4096]{1,0:T(8,128)(2,1)S(1)}, bf16[16,4096]{1,0:T(8,128)(2,1)S(1)}, u32[]{:S(2)}, u32[]{:S(2)}) %collective-permute-start.8) | collective-permute-done | bytes 131104 | tf_op jit(solution)/shard_map/ppermute | solution.py:21
  68.8 4.5 %collective-permute-done.9 = bf16[16,4096]{1,0:T(8,128)(2,1)S(1)} collective-permute-done((bf16[16,4096]{1,0:T(8,128)(2,1)S(1)}, bf16[16,4096]{1,0:T(8,128)(2,1)S(1)}, u32[]{:S(2)}, u32[]{:S(2)}) %collective-permute-start.9) | collective-permute-done | bytes 131104 | tf_op jit(solution)/shard_map/ppermute | solution.py:21
  73.3 0.9 %reshape.23 = bf16[8,2,8192]{2,1,0:T(2,128)(2,1)} reshape(bf16[16,8192]{1,0:T(8,128)(2,1)S(1)} %pad_maximum_fusion) | data formatting | bytes 524288 | tf_op jit(solution)/shard_map/reshape | solution.py:249
  (37 shorter events, 6.1 us)
Async XLA Ops:
  0.1 1.6 %copy-start.2 = (bf16[8,1,2,512,128]{4,3,2,1,0:T(8,128)(2,1)S(1)}, bf16[8,1,2,512,128]{4,3,2,1,0:T(8,128)(2,1)}, u32[]{:S(2)}) copy-start(bf16[8,1,2,512,128]{4,3,2,1,0:T(8,128)(2,1)} %cache.3) | copy-start | bytes 6291460
  1.7 0.7 copy-start.7
  2.3 0.7 copy-start.9
  4.0 1.4 %collective-permute-start = (bf16[2,256,128]{2,1,0:T(8,128)(2,1)S(1)}, bf16[2,256,128]{2,1,0:T(8,128)(2,1)S(1)}, u32[]{:S(2)}, u32[]{:S(2)}) collective-permute-start(bf16[2,256,128]{2,1,0:T(8,128)(2,1)S(1)} %get-tuple-element.13), channel_id=1, source_target_pairs={{0,8},{8,0},{16,24},{24,16},{32,40},{40,32},{48,56},{56,48},{64,72... | collective-permute-start | bytes 393224 | tf_op jit(solution)/shard_map/ppermute | solution.py:21
  5.5 5.6 %collective-permute-start.1 = (bf16[2,256,128]{2,1,0:T(8,128)(2,1)S(1)}, bf16[2,256,128]{2,1,0:T(8,128)(2,1)S(1)}, u32[]{:S(2)}, u32[]{:S(2)}) collective-permute-start(bf16[2,256,128]{2,1,0:T(8,128)(2,1)S(1)} %add.42), channel_id=1, source_target_pairs={{0,64},{8,72},{16,80},{24,88},{32,96},{40,104},{48,112},{56,120},{... | collective-permute-start | bytes 393224 | tf_op jit(solution)/shard_map/ppermute | solution.py:21
  11.2 6.6 %collective-permute-start.2 = (bf16[2,256,128]{2,1,0:T(8,128)(2,1)S(1)}, bf16[2,256,128]{2,1,0:T(8,128)(2,1)S(1)}, u32[]{:S(2)}, u32[]{:S(2)}) collective-permute-start(bf16[2,256,128]{2,1,0:T(8,128)(2,1)S(1)} %add.43), channel_id=1, source_target_pairs={{0,128},{8,136},{16,144},{24,152},{32,160},{40,168},{48,176},{56,1... | collective-permute-start | bytes 393224 | tf_op jit(solution)/shard_map/ppermute | solution.py:21
  17.8 8.0 %collective-permute-start.3 = (bf16[2,256,128]{2,1,0:T(8,128)(2,1)S(1)}, bf16[2,256,128]{2,1,0:T(8,128)(2,1)S(1)}, u32[]{:S(2)}, u32[]{:S(2)}) collective-permute-start(bf16[2,256,128]{2,1,0:T(8,128)(2,1)S(1)} %add.44), channel_id=1, source_target_pairs={{0,16},{8,24},{16,0},{24,8},{32,48},{40,56},{48,32},{56,40},{64,80... | collective-permute-start | bytes 393224 | tf_op jit(solution)/shard_map/ppermute | solution.py:21
  25.8 10.2 %collective-permute-start.4 = (bf16[2,256,128]{2,1,0:T(8,128)(2,1)S(1)}, bf16[2,256,128]{2,1,0:T(8,128)(2,1)S(1)}, u32[]{:S(2)}, u32[]{:S(2)}) collective-permute-start(bf16[2,256,128]{2,1,0:T(8,128)(2,1)S(1)} %add.45), channel_id=1, source_target_pairs={{0,32},{8,40},{16,48},{24,56},{32,0},{40,8},{48,16},{56,24},{64,96... | collective-permute-start | bytes 393224 | tf_op jit(solution)/shard_map/ppermute | solution.py:21
  36.1 6.8 %collective-permute-start.5 = (bf16[2,256,128]{2,1,0:T(8,128)(2,1)S(1)}, bf16[2,256,128]{2,1,0:T(8,128)(2,1)S(1)}, u32[]{:S(2)}, u32[]{:S(2)}) collective-permute-start(bf16[2,256,128]{2,1,0:T(8,128)(2,1)S(1)} %add.46.mine), channel_id=1, source_target_pairs={{0,8},{8,0},{16,24},{24,16},{32,40},{40,32},{48,56},{56,48},{64,72... | collective-permute-start | bytes 393224 | tf_op jit(solution)/shard_map/ppermute | solution.py:21
  36.2 1.6 %copy-start.3 = (bf16[8,1,2,512,128]{4,3,2,1,0:T(8,128)(2,1)S(1)}, bf16[8,1,2,512,128]{4,3,2,1,0:T(8,128)(2,1)}, u32[]{:S(2)}) copy-start(bf16[8,1,2,512,128]{4,3,2,1,0:T(8,128)(2,1)} %cache.3) | copy-start | bytes 6291460
  37.8 0.7 copy-start.4
  38.5 0.7 copy-start.8
  42.9 3.4 %copy-start = (bf16[512,8192]{1,0:T(8,128)(2,1)S(1)}, bf16[512,8192]{1,0:T(8,128)(2,1)}, u32[]{:S(2)}) copy-start(bf16[512,8192]{1,0:T(8,128)(2,1)} %weights.3) | copy-start | bytes 25165828
  46.3 0.7 copy-start.5
  47.0 0.7 copy-start.6
  47.7 3.4 %copy-start.1 = (bf16[512,8192]{1,0:T(8,128)(2,1)S(1)}, bf16[512,8192]{1,0:T(8,128)(2,1)}, u32[]{:S(2)}) copy-start(bf16[512,8192]{1,0:T(8,128)(2,1)} %weights.3) | copy-start | bytes 25165828
  47.7 17.2 %copy-start.10 = (bf16[8,2,8192]{2,1,0:T(2,128)(2,1)S(1)}, bf16[8,2,8192]{2,1,0:T(2,128)(2,1)}, u32[]{:S(2)}) copy-start(bf16[8,2,8192]{2,1,0:T(2,128)(2,1)} %param.8) | copy-start | bytes 786436
  50.3 6.0 %collective-permute-start.6 = (bf16[16,4096]{1,0:T(8,128)(2,1)S(1)}, bf16[16,4096]{1,0:T(8,128)(2,1)S(1)}, u32[]{:S(2)}, u32[]{:S(2)}) collective-permute-start(bf16[16,4096]{1,0:T(8,128)(2,1)S(1)} %get-tuple-element.18), channel_id=1, source_target_pairs={{0,1},{1,0},{2,3},{3,2},{4,5},{5,4},{6,7},{7,6},{8,9},{9,8},{10,11... | collective-permute-start | bytes 393224 | tf_op jit(solution)/shard_map/ppermute | solution.py:21
  56.4 5.2 %collective-permute-start.7 = (bf16[16,4096]{1,0:T(8,128)(2,1)S(1)}, bf16[16,4096]{1,0:T(8,128)(2,1)S(1)}, u32[]{:S(2)}, u32[]{:S(2)}) collective-permute-start(bf16[16,4096]{1,0:T(8,128)(2,1)S(1)} %add.47), channel_id=1, source_target_pairs={{0,2},{1,3},{2,0},{3,1},{4,6},{5,7},{6,4},{7,5},{8,10},{9,11},{10,... | collective-permute-start | bytes 393224 | tf_op jit(solution)/shard_map/ppermute | solution.py:21
  61.6 6.6 %collective-permute-start.8 = (bf16[16,4096]{1,0:T(8,128)(2,1)S(1)}, bf16[16,4096]{1,0:T(8,128)(2,1)S(1)}, u32[]{:S(2)}, u32[]{:S(2)}) collective-permute-start(bf16[16,4096]{1,0:T(8,128)(2,1)S(1)} %add.48), channel_id=1, source_target_pairs={{0,4},{1,5},{2,6},{3,7},{4,0},{5,1},{6,2},{7,3},{8,12},{9,13},{10,... | collective-permute-start | bytes 393224 | tf_op jit(solution)/shard_map/ppermute | solution.py:21
  68.2 5.1 %collective-permute-start.9 = (bf16[16,4096]{1,0:T(8,128)(2,1)S(1)}, bf16[16,4096]{1,0:T(8,128)(2,1)S(1)}, u32[]{:S(2)}, u32[]{:S(2)}) collective-permute-start(bf16[16,4096]{1,0:T(8,128)(2,1)S(1)} %add_convert_fusion), channel_id=1, source_target_pairs={{0,1},{1,0},{2,3},{3,2},{4,5},{5,4},{6,7},{7,6},{8,9},{9,8},{10,11... | collective-permute-start | bytes 393224 | tf_op jit(solution)/shard_map/ppermute | solution.py:21

commit v2 on v1

--- a/solution.py
+++ b/solution.py
@@ -13,7 +13,7 @@
 CHUNK = 1024
 VMEM = pl.BlockSpec(memory_space=pltpu.VMEM)
 SMEM = pl.BlockSpec(memory_space=pltpu.SMEM)
-ANY = pl.BlockSpec(memory_space=pl.ANY)
+HBM = pl.BlockSpec(memory_space=pltpu.HBM)
 NT = (((1,), (1,)), ((), ()))
 
 
@@ -21,9 +21,17 @@
     return lax.ppermute(x, axis, [(i, i ^ bit) for i in range(size)])
 
 
-def extract_kernel(lengths, winner, place, cache, keep, send, window, sems):
+def extract_kernel(place, lengths_in, winner_in, cache, keep, send, lengths, winner, window, sems):
     problems = cache.shape[0]
     half = problems // 2
+    small = [
+        pltpu.make_async_copy(lengths_in, lengths, sems.at[problems]),
+        pltpu.make_async_copy(winner_in, winner, sems.at[problems + 1]),
+    ]
+    for copy in small:
+        copy.start()
+    for copy in small:
+        copy.wait()
 
     def start_of(p):
         first = lengths[p] - BLOCK
@@ -59,7 +67,7 @@
             where[0][kv, base + 16 : base + BLOCK, :] = tail
 
 
-def old_kernel(lengths, queries, new_keys, new_values, cache, out, peak, total, held, sems, *, factor):
+def old_kernel(lengths, queries, new_keys, new_values, cache, out, peak, total, passed, held, sems, *, factor):
     problems = cache.shape[0]
     group = queries.shape[1] // 2
     copies = []
@@ -85,14 +93,16 @@
             weight = jnp.exp(fresh[u] - top)
             sums = sums + weight
             mixed = mixed + weight * new_values[p, u : u + 1, :].astype(jnp.float32)
+        passed[p] = query
         out[p] = mixed
         peak[p] = jnp.broadcast_to(top, mixed.shape)
         total[p] = jnp.broadcast_to(sums, mixed.shape)
 
 
-def start_weights(weights, held, sems, base):
+def start_weights(scales_in, scales, weights, held, sems, base):
     chunks = held.shape[1] // CHUNK
-    copies = []
+    copies = [pltpu.make_async_copy(scales_in, scales, sems.at[chunks])]
+    copies[0].start()
     for c in range(chunks):
         columns = pl.multiple_of(base + c * CHUNK, CHUNK)
         copies.append(
@@ -108,7 +118,8 @@
     blocks, side = scales.shape[0], held.shape[0] // scales.shape[0]
     parts = [attended[pl.ds(b, 16, stride=blocks), :].astype(jnp.bfloat16) for b in range(blocks)]
     first = base // 128
-    for c, copy in enumerate(copies):
+    copies[0].wait()
+    for c, copy in enumerate(copies[1:]):
         copy.wait()
         columns = slice(c * CHUNK, (c + 1) * CHUNK)
         terms = [
@@ -123,10 +134,12 @@
             out[:, c * CHUNK + n * 128 : c * CHUNK + (n + 1) * 128] = sums.astype(out.dtype)
 
 
-def fork_kernel(place, queries, mine, other, old, peak, total, scales, weights, attended, out, held, sems, *, factor):
+def fork_kernel(
+    place, queries, mine, other, old, peak, total, scales_in, weights, attended, out, scales, held, sems, *, factor
+):
     width = held.shape[1]
     base = (1 - place[2]) * width
-    copies = start_weights(weights, held, sems, base)
+    copies = start_weights(scales_in, scales, weights, held, sems, base)
     rows, keys_here = queries.shape[0], mine.shape[1]
     per_row = rows // (2 * keys_here // BLOCK)
     halves = []
@@ -148,9 +161,9 @@
     project(attended, scales, held, copies, base, out)
 
 
-def project_kernel(place, attended, scales, weights, out, held, sems):
+def project_kernel(place, attended, scales_in, weights, out, scales, held, sems):
     base = place[2] * held.shape[1]
-    copies = start_weights(weights, held, sems, base)
+    copies = start_weights(scales_in, scales, weights, held, sems, base)
     project(attended, scales, held, copies, base, out)
 
 
@@ -167,6 +180,9 @@
     width = out_values.shape[1]
     factor = 1.0 / math.sqrt(head_dim)
     cand, tp = lax.axis_index("cand"), lax.axis_index("tp")
+    kv_cache, lengths_far, winner, out_values, out_scales = (
+        pltpu.with_memory_space_constraint(x, pltpu.HBM) for x in (kv_cache, lengths, winner, out_values, out_scales)
+    )
     place = jnp.stack([cand, cand % 2, tp % 2]).astype(jnp.int32)
     half = width // 2
     bf16, f32 = jnp.bfloat16, jnp.float32
@@ -175,23 +191,25 @@
     keep, send = pl.pallas_call(
         extract_kernel,
         out_shape=(fork_shape, fork_shape),
-        in_specs=[SMEM, SMEM, SMEM, ANY],
+        in_specs=[SMEM, HBM, HBM, HBM],
         out_specs=(VMEM, VMEM),
         scratch_shapes=[
+            pltpu.SMEM((problems,), jnp.int32),
+            pltpu.SMEM((problems,), jnp.int32),
             pltpu.VMEM((problems, 2, WINDOW, head_dim), bf16),
-            pltpu.SemaphoreType.DMA((problems,)),
+            pltpu.SemaphoreType.DMA((problems + 2,)),
         ],
         **params(4, 0, 2**19),
-    )(lengths, winner, place, kv_cache)
+    )(place, lengths_far, winner, kv_cache)
 
     grouped = queries.reshape(problems, steps * heads, head_dim)
     rows = problems * steps * heads
     partial = jax.ShapeDtypeStruct((problems, steps * heads, head_dim), f32)
-    old, peak, total = pl.pallas_call(
+    partials = pl.pallas_call(
         functools.partial(old_kernel, factor=factor),
-        out_shape=(partial,) * 3,
-        in_specs=[SMEM, VMEM, VMEM, VMEM, ANY],
-        out_specs=(VMEM,) * 3,
+        out_shape=(partial,) * 3 + (jax.ShapeDtypeStruct(partial.shape, bf16),),
+        in_specs=[SMEM, VMEM, VMEM, VMEM, HBM],
+        out_specs=(VMEM,) * 4,
         scratch_shapes=[
             pltpu.VMEM((problems, 2, slots, head_dim), bf16),
             pltpu.SemaphoreType.DMA((problems,)),
@@ -200,17 +218,25 @@
     )(lengths, grouped, new_kv[:, :, 0, 0], new_kv[:, :, 0, 1], kv_cache)
 
     block = keep + exchange(send, "cand", 32, 1)
-    for bit in (8, 16, 2, 4):
-        block = block + exchange(block, "cand", 32, bit)
+    for bit in (8, 24, 2, 6):
+        received = exchange(block, "cand", 32, bit)
+        if bit == 8:
+            received, partials = lax.optimization_barrier((received, partials))
+        block = block + received
+    old, peak, total, grouped = partials
     other = exchange(block, "cand", 32, 1)
 
     flat = (rows, head_dim)
     half_shape = jax.ShapeDtypeStruct((problems * steps, half), bf16)
-    scratch = [pltpu.VMEM((out_values.shape[0], half), bf16), pltpu.SemaphoreType.DMA((half // CHUNK,))]
+    scratch = [
+        pltpu.SMEM(out_scales.shape, f32),
+        pltpu.VMEM((out_values.shape[0], half), bf16),
+        pltpu.SemaphoreType.DMA((half // CHUNK + 1,)),
+    ]
     attended, away = pl.pallas_call(
         functools.partial(fork_kernel, factor=factor),
         out_shape=(jax.ShapeDtypeStruct(flat, f32), half_shape),
-        in_specs=[SMEM] + [VMEM] * 6 + [SMEM, ANY],
+        in_specs=[SMEM] + [VMEM] * 6 + [HBM, HBM],
         out_specs=(VMEM, VMEM),
         scratch_shapes=scratch,
         **params(12, 2**26, 2**22),
@@ -229,18 +255,18 @@
     home = pl.pallas_call(
         project_kernel,
         out_shape=half_shape,
-        in_specs=[SMEM, VMEM, SMEM, ANY],
+        in_specs=[SMEM, VMEM, HBM, HBM],
         out_specs=VMEM,
         scratch_shapes=scratch,
         **params(12, 2**26, 2**22),
     )(place, attended, out_scales, out_values)
 
     sums = home + arrived
-    for bit in (2, 4):
-        sums = sums + exchange(sums, "tp", 8, bit)
+    ahead, back, across = (exchange(sums, "tp", 8, bit) for bit in (2, 6, 4))
     residual = hidden_in.reshape(problems * steps, width)
     residual = lax.dynamic_slice_in_dim(residual, (tp % 2) * half, half, 1)
-    mixed = (residual.astype(f32) + sums.astype(f32)).astype(bf16)
+    pairs = (sums.astype(f32) + ahead.astype(f32)) + (back.astype(f32) + across.astype(f32))
+    mixed = (residual.astype(f32) + pairs).astype(bf16)
     neighbour = exchange(mixed, "tp", 8, 1)
     first = tp % 2 == 0
     result = jnp.concatenate(

time: 74.7 us -> 64.2 us (0.86)
  local copies, waits for them, and re-layouts: 13 us -> 3.15 us
  waiting for transfers between devices: 32.2 us -> 27.7 us
  Pallas kernels: 9.61 us -> 13 us
    unnamed x22 -> x6, local copies, waits for them, and re-layouts: 11.2 us -> 1.37 us
    ppermute x10 -> x11, waiting for transfers between devices: 32.2 us -> 27.7 us  [exchange(): return lax.ppermute(x, axis, [(i, i ^ bit) for i in range(size)])]
    pallas_call x1, Pallas kernels: 1.02 us -> 2.31 us  [local(): pl.pallas_call(extract_kernel, out_shape=(fork_shape, fork_shape), in_spe...]
    pallas_call x1, Pallas kernels: 2.2 us -> 3.03 us  [local(): pl.pallas_call(project_kernel, out_shape=half_shape, in_specs=[SMEM, VMEM...]
    ppermute x10 -> x11, starting transfers between devices: 18.8 us -> 18.8 us  [exchange(): return lax.ppermute(x, axis, [(i, i ^ bit) for i in range(size)])]
  transfers between devices with their start and end apart: 10 -> 11, of which waited for: 9 -> 9; matrix products, arithmetic and copies ran while one was open for 1% -> 1% of each run, Pallas kernels for 8% -> 12%
where the time goes in v2:
time: 64.2 us; the launch traced here: 63.3 us
  waiting for transfers between devices  27.7 us (43%)
  starting transfers between devices  18.8 us (29%)
  Pallas kernels  13 us (20%)
  local copies, waits for them, and re-layouts  3.15 us (5%)
    ppermute x11, waiting for transfers between devices, exchange(): return lax.ppermute(x, axis, [(i, i ^ bit) for i in range(size)])  27.7 us
    ppermute x11, starting transfers between devices, exchange(): return lax.ppermute(x, axis, [(i, i ^ bit) for i in range(size)])  18.8 us
    pallas_call x1, Pallas kernels, local(): pl.pallas_call(functools.partial(old_kernel, factor=factor), out_shape=(p...  4.42 us
    pallas_call x1, Pallas kernels, local(): pl.pallas_call(functools.partial(fork_kernel, factor=factor), out_shape=(...  3.29 us
    pallas_call x1, Pallas kernels, local(): pl.pallas_call(project_kernel, out_shape=half_shape, in_specs=[SMEM, VMEM...  3.03 us
    pallas_call x1, Pallas kernels, local(): pl.pallas_call(extract_kernel, out_shape=(fork_shape, fork_shape), in_spe...  2.31 us
    unnamed x6, local copies, waits for them, and re-layouts  1.37 us
  transfers between devices with their start and end apart: 11, of which 9 were waited for; matrix products, arithmetic and copies ran while one was open for 1% of the time, Pallas kernels for 12%

profile of v2, /device:TPU:6, one launch (start us, length us, event | category | flops | bytes accessed | tf_op | source)
XLA Modules:
  0.0 63.3 jit_solution(12838631312725347361)
XLA Ops:
  0.1 2.3 %shard_map.82 = (bf16[2,256,128]{2,1,0:T(8,128)(2,1)S(1)}, bf16[2,256,128]{2,1,0:T(8,128)(2,1)S(1)}) custom-call(s32[3]{0:T(128)S(1)} %pad_add_fusion.place, s32[8]{0:T(128)} %lengths.1, s32[8]{0:T(128)} %winner_in.1, bf16[8,1,2,512,128]{4,3,2,1,0:T(8,128)(2,1)} %cache.3), custom_call_target="tpu_custom_call" | custom-call | bytes 524288 | tf_op jit(solution)/shard_map/pallas_call | solution.py:191
  2.5 0.8 %fusion = (bf16[8,2,1,1,128]{4,3,2,1,0:T(2,128)(2,1)S(1)}, bf16[8,2,1,1,128]{4,3,2,1,0:T(2,128)(2,1)S(1)}) fusion(bf16[8,2,1,2,128]{4,3,2,1,0:T(2,128)(2,1)} %param.10), kind=kLoop, calls=%fused_computation.7 | loop fusion | bytes 16384 | tf_op jit(solution)/shard_map/slice | solution.py:218
  3.9 0.9 %collective-permute-start.1 = (bf16[2,256,128]{2,1,0:T(8,128)(2,1)S(1)}, bf16[2,256,128]{2,1,0:T(8,128)(2,1)S(1)}, u32[]{:S(2)}, u32[]{:S(2)}) collective-permute-start(bf16[2,256,128]{2,1,0:T(8,128)(2,1)S(1)} %add.45), channel_id=1, source_target_pairs={{0,64},{8,72},{16,80},{24,88},{32,96},{40,104},{48,112},{56,120},{... | collective-permute-start | bytes 393224 | tf_op jit(solution)/shard_map/ppermute | solution.py:21
  4.8 0.7 %copy-done = bf16[8,2,4,128]{3,2,1,0:T(4,128)(2,1)S(1)} copy-done((bf16[8,2,4,128]{3,2,1,0:T(4,128)(2,1)S(1)}, bf16[8,2,4,128]{3,2,1,0:T(4,128)(2,1)}, u32[]{:S(2)}) %copy-start) | copy-done | bytes 16408
  5.5 0.7 %copy-done.1 = s32[8]{0:T(128)S(1)} copy-done((s32[8]{0:T(128)S(1)}, s32[8]{0:T(128)}, u32[]{:S(2)}) %copy-start.1) | copy-done | bytes 56
  6.2 4.4 %shard_map.83 = (f32[8,8,128]{2,1,0:T(8,128)S(1)}, f32[8,8,128]{2,1,0:T(8,128)S(1)}, f32[8,8,128]{2,1,0:T(8,128)S(1)}, bf16[8,8,128]{2,1,0:T(8,128)(2,1)S(1)}) custom-call(s32[8]{0:T(128)S(1)} %copy-done.1, bf16[8,8,128]{2,1,0:T(8,128)(2,1)S(1)} %bitcast.15, bf16[8,2,128]{2,1,0:T(2,128)(2,1)S(1)} %get-tuple-element.36.new_keys, ...), custom_call_target="tpu_custom_call" | custom-call | flops 16777216 | bytes 2097152 | tf_op jit(solution)/shard_map/pallas_call | solution.py:208
  10.7 1.5 %collective-permute-start.2 = (bf16[2,256,128]{2,1,0:T(8,128)(2,1)S(1)}, bf16[2,256,128]{2,1,0:T(8,128)(2,1)S(1)}, u32[]{:S(2)}, u32[]{:S(2)}) collective-permute-start(bf16[2,256,128]{2,1,0:T(8,128)(2,1)S(1)} %add.46), channel_id=1, source_target_pairs={{0,192},{8,200},{16,208},{24,216},{32,224},{40,232},{48,240},{56,2... | collective-permute-start | bytes 393224 | tf_op jit(solution)/shard_map/ppermute | solution.py:21
  12.2 5.1 %collective-permute-done.2 = bf16[2,256,128]{2,1,0:T(8,128)(2,1)S(1)} collective-permute-done((bf16[2,256,128]{2,1,0:T(8,128)(2,1)S(1)}, bf16[2,256,128]{2,1,0:T(8,128)(2,1)S(1)}, u32[]{:S(2)}, u32[]{:S(2)}) %collective-permute-start.2) | collective-permute-done | bytes 131104 | tf_op jit(solution)/shard_map/ppermute | solution.py:21
  17.3 3.4 %collective-permute-start.3 = (bf16[2,256,128]{2,1,0:T(8,128)(2,1)S(1)}, bf16[2,256,128]{2,1,0:T(8,128)(2,1)S(1)}, u32[]{:S(2)}, u32[]{:S(2)}) collective-permute-start(bf16[2,256,128]{2,1,0:T(8,128)(2,1)S(1)} %add.47), channel_id=1, source_target_pairs={{0,16},{8,24},{16,0},{24,8},{32,48},{40,56},{48,32},{56,40},{64,80... | collective-permute-start | bytes 393224 | tf_op jit(solution)/shard_map/ppermute | solution.py:21
  20.6 5.5 %collective-permute-done.3 = bf16[2,256,128]{2,1,0:T(8,128)(2,1)S(1)} collective-permute-done((bf16[2,256,128]{2,1,0:T(8,128)(2,1)S(1)}, bf16[2,256,128]{2,1,0:T(8,128)(2,1)S(1)}, u32[]{:S(2)}, u32[]{:S(2)}) %collective-permute-start.3) | collective-permute-done | bytes 131104 | tf_op jit(solution)/shard_map/ppermute | solution.py:21
  26.1 3.8 %collective-permute-start.4 = (bf16[2,256,128]{2,1,0:T(8,128)(2,1)S(1)}, bf16[2,256,128]{2,1,0:T(8,128)(2,1)S(1)}, u32[]{:S(2)}, u32[]{:S(2)}) collective-permute-start(bf16[2,256,128]{2,1,0:T(8,128)(2,1)S(1)} %add.48), channel_id=1, source_target_pairs={{0,48},{8,56},{16,32},{24,40},{32,16},{40,24},{48,0},{56,8},{64,11... | collective-permute-start | bytes 393224 | tf_op jit(solution)/shard_map/ppermute | solution.py:21
  30.0 5.3 %collective-permute-done.4 = bf16[2,256,128]{2,1,0:T(8,128)(2,1)S(1)} collective-permute-done((bf16[2,256,128]{2,1,0:T(8,128)(2,1)S(1)}, bf16[2,256,128]{2,1,0:T(8,128)(2,1)S(1)}, u32[]{:S(2)}, u32[]{:S(2)}) %collective-permute-start.4) | collective-permute-done | bytes 131104 | tf_op jit(solution)/shard_map/ppermute | solution.py:21
  35.4 1.3 %collective-permute-done.5.other = bf16[2,256,128]{2,1,0:T(8,128)(2,1)S(1)} collective-permute-done((bf16[2,256,128]{2,1,0:T(8,128)(2,1)S(1)}, bf16[2,256,128]{2,1,0:T(8,128)(2,1)S(1)}, u32[]{:S(2)}, u32[]{:S(2)}) %collective-permute-start.5) | collective-permute-done | bytes 131104 | tf_op jit(solution)/shard_map/ppermute | solution.py:21
  36.8 3.3 %shard_map.84 = (f32[64,128]{1,0:T(8,128)S(1)}, bf16[16,4096]{1,0:T(8,128)(2,1)S(1)}) custom-call(s32[3]{0:T(128)S(1)} %pad_add_fusion.place, bf16[64,128]{1,0:T(8,128)(2,1)S(1)} %bitcast.16, bf16[2,256,128]{2,1,0:T(8,128)(2,1)S(1)} %add.49.mine, bf16[2,256,128]{2,1,0:T(8,128)(2,1)S(1)} %collective-permute-done.5.other, f32[64,128]{1,0:T(8,128)S(1)} %bitcast.12, ...), custom_call_target="tpu_custom_call" | custom-call | flops 67108864 | bytes 4194304 | tf_op jit(solution)/shard_map/pallas_call | solution.py:236
  40.1 2.6 %collective-permute-start.6 = (bf16[16,4096]{1,0:T(8,128)(2,1)S(1)}, bf16[16,4096]{1,0:T(8,128)(2,1)S(1)}, u32[]{:S(2)}, u32[]{:S(2)}) collective-permute-start(bf16[16,4096]{1,0:T(8,128)(2,1)S(1)} %get-tuple-element.30), channel_id=1, source_target_pairs={{0,1},{1,0},{2,3},{3,2},{4,5},{5,4},{6,7},{7,6},{8,9},{9,8},{10,11... | collective-permute-start | bytes 393224 | tf_op jit(solution)/shard_map/ppermute | solution.py:21
  42.7 3.0 %shard_map.85 = bf16[16,4096]{1,0:T(8,128)(2,1)S(1)} custom-call(s32[3]{0:T(128)S(1)} %pad_add_fusion.place, f32[64,128]{1,0:T(8,128)S(1)} %get-tuple-element.29.attended, f32[4,64]{1,0:T(4,128)} %scales_in.3, bf16[512,8192]{1,0:T(8,128)(2,1)} %weights.3), custom_call_target="tpu_custom_call" | custom-call | flops 67108864 | bytes 4194304 | tf_op jit(solution)/shard_map/pallas_call | solution.py:255
  45.7 0.8 %collective-permute-done.6 = bf16[16,4096]{1,0:T(8,128)(2,1)S(1)} collective-permute-done((bf16[16,4096]{1,0:T(8,128)(2,1)S(1)}, bf16[16,4096]{1,0:T(8,128)(2,1)S(1)}, u32[]{:S(2)}, u32[]{:S(2)}) %collective-permute-start.6) | collective-permute-done | bytes 131104 | tf_op jit(solution)/shard_map/ppermute | solution.py:21
  46.6 1.7 %collective-permute-start.7 = (bf16[16,4096]{1,0:T(8,128)(2,1)S(1)}, bf16[16,4096]{1,0:T(8,128)(2,1)S(1)}, u32[]{:S(2)}, u32[]{:S(2)}) collective-permute-start(bf16[16,4096]{1,0:T(8,128)(2,1)S(1)} %add.50), channel_id=1, source_target_pairs={{0,2},{1,3},{2,0},{3,1},{4,6},{5,7},{6,4},{7,5},{8,10},{9,11},{10,... | collective-permute-start | bytes 393224 | tf_op jit(solution)/shard_map/ppermute | solution.py:21
  48.2 2.2 %collective-permute-start.8 = (bf16[16,4096]{1,0:T(8,128)(2,1)S(1)}, bf16[16,4096]{1,0:T(8,128)(2,1)S(1)}, u32[]{:S(2)}, u32[]{:S(2)}) collective-permute-start(bf16[16,4096]{1,0:T(8,128)(2,1)S(1)} %add.50), channel_id=1, source_target_pairs={{0,6},{1,7},{2,4},{3,5},{4,2},{5,3},{6,0},{7,1},{8,14},{9,15},{10,... | collective-permute-start | bytes 393224 | tf_op jit(solution)/shard_map/ppermute | solution.py:21
  50.4 0.7 %collective-permute-start.9 = (bf16[16,4096]{1,0:T(8,128)(2,1)S(1)}, bf16[16,4096]{1,0:T(8,128)(2,1)S(1)}, u32[]{:S(2)}, u32[]{:S(2)}) collective-permute-start(bf16[16,4096]{1,0:T(8,128)(2,1)S(1)} %add.50), channel_id=1, source_target_pairs={{0,4},{1,5},{2,6},{3,7},{4,0},{5,1},{6,2},{7,3},{8,12},{9,13},{10,... | collective-permute-start | bytes 393224 | tf_op jit(solution)/shard_map/ppermute | solution.py:21
  51.7 5.5 %collective-permute-done.8 = bf16[16,4096]{1,0:T(8,128)(2,1)S(1)} collective-permute-done((bf16[16,4096]{1,0:T(8,128)(2,1)S(1)}, bf16[16,4096]{1,0:T(8,128)(2,1)S(1)}, u32[]{:S(2)}, u32[]{:S(2)}) %collective-permute-start.8) | collective-permute-done | bytes 131104 | tf_op jit(solution)/shard_map/ppermute | solution.py:21
  57.3 1.8 %collective-permute-start.10 = (bf16[16,4096]{1,0:T(8,128)(2,1)S(1)}, bf16[16,4096]{1,0:T(8,128)(2,1)S(1)}, u32[]{:S(2)}, u32[]{:S(2)}) collective-permute-start(bf16[16,4096]{1,0:T(8,128)(2,1)S(1)} %add_convert_fusion), channel_id=1, source_target_pairs={{0,1},{1,0},{2,3},{3,2},{4,5},{5,4},{6,7},{7,6},{8,9},{9,8},{10,11... | collective-permute-start | bytes 393224 | tf_op jit(solution)/shard_map/ppermute | solution.py:21
  59.1 3.2 %collective-permute-done.10 = bf16[16,4096]{1,0:T(8,128)(2,1)S(1)} collective-permute-done((bf16[16,4096]{1,0:T(8,128)(2,1)S(1)}, bf16[16,4096]{1,0:T(8,128)(2,1)S(1)}, u32[]{:S(2)}, u32[]{:S(2)}) %collective-permute-start.10) | collective-permute-done | bytes 131104 | tf_op jit(solution)/shard_map/ppermute | solution.py:21
  62.4 0.9 %reshape.27 = bf16[8,2,8192]{2,1,0:T(2,128)(2,1)} reshape(bf16[16,8192]{1,0:T(8,128)(2,1)S(1)} %pad_maximum_fusion) | data formatting | bytes 524288 | tf_op jit(solution)/shard_map/reshape | solution.py:275
  (22 shorter events, 1.7 us)
Async XLA Ops:
  2.4 1.4 %collective-permute-start = (bf16[2,256,128]{2,1,0:T(8,128)(2,1)S(1)}, bf16[2,256,128]{2,1,0:T(8,128)(2,1)S(1)}, u32[]{:S(2)}, u32[]{:S(2)}) collective-permute-start(bf16[2,256,128]{2,1,0:T(8,128)(2,1)S(1)} %get-tuple-element.19), channel_id=1, source_target_pairs={{0,8},{8,0},{16,24},{24,16},{32,40},{40,32},{48,56},{56,48},{64,72... | collective-permute-start | bytes 393224 | tf_op jit(solution)/shard_map/ppermute | solution.py:21
  3.9 6.7 %collective-permute-start.1 = (bf16[2,256,128]{2,1,0:T(8,128)(2,1)S(1)}, bf16[2,256,128]{2,1,0:T(8,128)(2,1)S(1)}, u32[]{:S(2)}, u32[]{:S(2)}) collective-permute-start(bf16[2,256,128]{2,1,0:T(8,128)(2,1)S(1)} %add.45), channel_id=1, source_target_pairs={{0,64},{8,72},{16,80},{24,88},{32,96},{40,104},{48,112},{56,120},{... | collective-permute-start | bytes 393224 | tf_op jit(solution)/shard_map/ppermute | solution.py:21
  4.8 0.7 %copy-start = (bf16[8,2,4,128]{3,2,1,0:T(4,128)(2,1)S(1)}, bf16[8,2,4,128]{3,2,1,0:T(4,128)(2,1)}, u32[]{:S(2)}) copy-start(bf16[8,2,4,128]{3,2,1,0:T(4,128)(2,1)} %param.9) | copy-start | bytes 49156
  5.5 0.7 %copy-start.1 = (s32[8]{0:T(128)S(1)}, s32[8]{0:T(128)}, u32[]{:S(2)}) copy-start(s32[8]{0:T(128)} %lengths.1) | copy-start | bytes 100
  10.7 6.6 %collective-permute-start.2 = (bf16[2,256,128]{2,1,0:T(8,128)(2,1)S(1)}, bf16[2,256,128]{2,1,0:T(8,128)(2,1)S(1)}, u32[]{:S(2)}, u32[]{:S(2)}) collective-permute-start(bf16[2,256,128]{2,1,0:T(8,128)(2,1)S(1)} %add.46), channel_id=1, source_target_pairs={{0,192},{8,200},{16,208},{24,216},{32,224},{40,232},{48,240},{56,2... | collective-permute-start | bytes 393224 | tf_op jit(solution)/shard_map/ppermute | solution.py:21
  17.3 8.8 %collective-permute-start.3 = (bf16[2,256,128]{2,1,0:T(8,128)(2,1)S(1)}, bf16[2,256,128]{2,1,0:T(8,128)(2,1)S(1)}, u32[]{:S(2)}, u32[]{:S(2)}) collective-permute-start(bf16[2,256,128]{2,1,0:T(8,128)(2,1)S(1)} %add.47), channel_id=1, source_target_pairs={{0,16},{8,24},{16,0},{24,8},{32,48},{40,56},{48,32},{56,40},{64,80... | collective-permute-start | bytes 393224 | tf_op jit(solution)/shard_map/ppermute | solution.py:21
  26.1 9.2 %collective-permute-start.4 = (bf16[2,256,128]{2,1,0:T(8,128)(2,1)S(1)}, bf16[2,256,128]{2,1,0:T(8,128)(2,1)S(1)}, u32[]{:S(2)}, u32[]{:S(2)}) collective-permute-start(bf16[2,256,128]{2,1,0:T(8,128)(2,1)S(1)} %add.48), channel_id=1, source_target_pairs={{0,48},{8,56},{16,32},{24,40},{32,16},{40,24},{48,0},{56,8},{64,11... | collective-permute-start | bytes 393224 | tf_op jit(solution)/shard_map/ppermute | solution.py:21
  35.3 1.4 %collective-permute-start.5 = (bf16[2,256,128]{2,1,0:T(8,128)(2,1)S(1)}, bf16[2,256,128]{2,1,0:T(8,128)(2,1)S(1)}, u32[]{:S(2)}, u32[]{:S(2)}) collective-permute-start(bf16[2,256,128]{2,1,0:T(8,128)(2,1)S(1)} %add.49.mine), channel_id=1, source_target_pairs={{0,8},{8,0},{16,24},{24,16},{32,40},{40,32},{48,56},{56,48},{64,72... | collective-permute-start | bytes 393224 | tf_op jit(solution)/shard_map/ppermute | solution.py:21
  36.8 14.4 %copy-start.2 = (bf16[8,2,8192]{2,1,0:T(2,128)(2,1)S(1)}, bf16[8,2,8192]{2,1,0:T(2,128)(2,1)}, u32[]{:S(2)}) copy-start(bf16[8,2,8192]{2,1,0:T(2,128)(2,1)} %param.8) | copy-start | bytes 786436
  40.1 6.4 %collective-permute-start.6 = (bf16[16,4096]{1,0:T(8,128)(2,1)S(1)}, bf16[16,4096]{1,0:T(8,128)(2,1)S(1)}, u32[]{:S(2)}, u32[]{:S(2)}) collective-permute-start(bf16[16,4096]{1,0:T(8,128)(2,1)S(1)} %get-tuple-element.30), channel_id=1, source_target_pairs={{0,1},{1,0},{2,3},{3,2},{4,5},{5,4},{6,7},{7,6},{8,9},{9,8},{10,11... | collective-permute-start | bytes 393224 | tf_op jit(solution)/shard_map/ppermute | solution.py:21
  46.6 5.1 %collective-permute-start.7 = (bf16[16,4096]{1,0:T(8,128)(2,1)S(1)}, bf16[16,4096]{1,0:T(8,128)(2,1)S(1)}, u32[]{:S(2)}, u32[]{:S(2)}) collective-permute-start(bf16[16,4096]{1,0:T(8,128)(2,1)S(1)} %add.50), channel_id=1, source_target_pairs={{0,2},{1,3},{2,0},{3,1},{4,6},{5,7},{6,4},{7,5},{8,10},{9,11},{10,... | collective-permute-start | bytes 393224 | tf_op jit(solution)/shard_map/ppermute | solution.py:21
  48.2 9.0 %collective-permute-start.8 = (bf16[16,4096]{1,0:T(8,128)(2,1)S(1)}, bf16[16,4096]{1,0:T(8,128)(2,1)S(1)}, u32[]{:S(2)}, u32[]{:S(2)}) collective-permute-start(bf16[16,4096]{1,0:T(8,128)(2,1)S(1)} %add.50), channel_id=1, source_target_pairs={{0,6},{1,7},{2,4},{3,5},{4,2},{5,3},{6,0},{7,1},{8,14},{9,15},{10,... | collective-permute-start | bytes 393224 | tf_op jit(solution)/shard_map/ppermute | solution.py:21
  50.4 6.8 %collective-permute-start.9 = (bf16[16,4096]{1,0:T(8,128)(2,1)S(1)}, bf16[16,4096]{1,0:T(8,128)(2,1)S(1)}, u32[]{:S(2)}, u32[]{:S(2)}) collective-permute-start(bf16[16,4096]{1,0:T(8,128)(2,1)S(1)} %add.50), channel_id=1, source_target_pairs={{0,4},{1,5},{2,6},{3,7},{4,0},{5,1},{6,2},{7,3},{8,12},{9,13},{10,... | collective-permute-start | bytes 393224 | tf_op jit(solution)/shard_map/ppermute | solution.py:21
  57.3 5.1 %collective-permute-start.10 = (bf16[16,4096]{1,0:T(8,128)(2,1)S(1)}, bf16[16,4096]{1,0:T(8,128)(2,1)S(1)}, u32[]{:S(2)}, u32[]{:S(2)}) collective-permute-start(bf16[16,4096]{1,0:T(8,128)(2,1)S(1)} %add_convert_fusion), channel_id=1, source_target_pairs={{0,1},{1,0},{2,3},{3,2},{4,5},{5,4},{6,7},{7,6},{8,9},{9,8},{10,11... | collective-permute-start | bytes 393224 | tf_op jit(solution)/shard_map/ppermute | solution.py:21

commit v3 on v2

--- a/solution.py
+++ b/solution.py
@@ -99,47 +99,40 @@
         total[p] = jnp.broadcast_to(sums, mixed.shape)
 
 
-def start_weights(scales_in, scales, weights, held, sems, base):
-    chunks = held.shape[1] // CHUNK
-    copies = [pltpu.make_async_copy(scales_in, scales, sems.at[chunks])]
-    copies[0].start()
-    for c in range(chunks):
-        columns = pl.multiple_of(base + c * CHUNK, CHUNK)
-        copies.append(
-            pltpu.make_async_copy(
-                weights.at[:, pl.ds(columns, CHUNK)], held.at[:, c * CHUNK : (c + 1) * CHUNK], sems.at[c]
-            )
-        )
-        copies[-1].start()
-    return copies
-
-
-def project(attended, scales, held, copies, base, out):
-    blocks, side = scales.shape[0], held.shape[0] // scales.shape[0]
+def fetch_kernel(far, near, sems):
+    rows = far.shape[0] // sems.shape[0]
+    copies = [
+        pltpu.make_async_copy(far.at[pl.ds(i * rows, rows)], near.at[pl.ds(i * rows, rows)], sems.at[i])
+        for i in range(sems.shape[0])
+    ]
+    for copy in copies:
+        copy.start()
+    for copy in copies:
+        copy.wait()
+
+
+def project(attended, scales, weights, base, out):
+    blocks, side = scales.shape[0], weights.shape[0] // scales.shape[0]
     parts = [attended[pl.ds(b, 16, stride=blocks), :].astype(jnp.bfloat16) for b in range(blocks)]
-    first = base // 128
-    copies[0].wait()
-    for c, copy in enumerate(copies[1:]):
-        copy.wait()
-        columns = slice(c * CHUNK, (c + 1) * CHUNK)
+    for c in range(out.shape[1] // CHUNK):
+        columns = pl.ds(pl.multiple_of(base + c * CHUNK, CHUNK), CHUNK)
         terms = [
-            jnp.dot(parts[b], held[b * side : (b + 1) * side, columns], preferred_element_type=jnp.float32)
+            jnp.dot(parts[b], weights[b * side : (b + 1) * side, columns], preferred_element_type=jnp.float32)
             for b in range(blocks)
         ]
         for n in range(CHUNK // 128):
-            block = first + c * (CHUNK // 128) + n
-            sums = 0.0
-            for b in range(blocks):
+            block = base // 128 + c * (CHUNK // 128) + n
+            sums = terms[0][:, n * 128 : (n + 1) * 128] * scales[0, block]
+            for b in range(1, blocks):
                 sums = sums + terms[b][:, n * 128 : (n + 1) * 128] * scales[b, block]
             out[:, c * CHUNK + n * 128 : c * CHUNK + (n + 1) * 128] = sums.astype(out.dtype)
 
 
 def fork_kernel(
-    place, queries, mine, other, old, peak, total, scales_in, weights, attended, out, scales, held, sems, *, factor
+    place, queries, mine, other, old, peak, total, scales_in, weights, attended, out, scales, sem, *, factor
 ):
-    width = held.shape[1]
-    base = (1 - place[2]) * width
-    copies = start_weights(scales_in, scales, weights, held, sems, base)
+    scales_copy = pltpu.make_async_copy(scales_in, scales, sem)
+    scales_copy.start()
     rows, keys_here = queries.shape[0], mine.shape[1]
     per_row = rows // (2 * keys_here // BLOCK)
     halves = []
@@ -158,13 +151,15 @@
         sums = sums + jnp.sum(share, -1, keepdims=True)
         mixed = mixed + jnp.dot(share.astype(jnp.bfloat16), ref[1], preferred_element_type=jnp.float32)
     attended[...] = (mixed / sums).astype(jnp.bfloat16).astype(jnp.float32)
-    project(attended, scales, held, copies, base, out)
-
-
-def project_kernel(place, attended, scales_in, weights, out, scales, held, sems):
-    base = place[2] * held.shape[1]
-    copies = start_weights(scales_in, scales, weights, held, sems, base)
-    project(attended, scales, held, copies, base, out)
+    scales_copy.wait()
+    project(attended, scales, weights, (1 - place[2]) * out.shape[1], out)
+
+
+def project_kernel(place, attended, scales_in, weights, out, scales, sem):
+    scales_copy = pltpu.make_async_copy(scales_in, scales, sem)
+    scales_copy.start()
+    scales_copy.wait()
+    project(attended, scales, weights, place[2] * out.shape[1], out)
 
 
 def params(mib, flops, size):
@@ -180,7 +175,7 @@
     width = out_values.shape[1]
     factor = 1.0 / math.sqrt(head_dim)
     cand, tp = lax.axis_index("cand"), lax.axis_index("tp")
-    kv_cache, lengths_far, winner, out_values, out_scales = (
+    far_cache, far_lengths, winner, far_values, far_scales = (
         pltpu.with_memory_space_constraint(x, pltpu.HBM) for x in (kv_cache, lengths, winner, out_values, out_scales)
     )
     place = jnp.stack([cand, cand % 2, tp % 2]).astype(jnp.int32)
@@ -200,46 +195,58 @@
             pltpu.SemaphoreType.DMA((problems + 2,)),
         ],
         **params(4, 0, 2**19),
-    )(place, lengths_far, winner, kv_cache)
-
-    grouped = queries.reshape(problems, steps * heads, head_dim)
-    rows = problems * steps * heads
-    partial = jax.ShapeDtypeStruct((problems, steps * heads, head_dim), f32)
-    partials = pl.pallas_call(
-        functools.partial(old_kernel, factor=factor),
-        out_shape=(partial,) * 3 + (jax.ShapeDtypeStruct(partial.shape, bf16),),
-        in_specs=[SMEM, VMEM, VMEM, VMEM, HBM],
-        out_specs=(VMEM,) * 4,
-        scratch_shapes=[
-            pltpu.VMEM((problems, 2, slots, head_dim), bf16),
-            pltpu.SemaphoreType.DMA((problems,)),
-        ],
-        **params(8, 2**24, 2**21),
-    )(lengths, grouped, new_kv[:, :, 0, 0], new_kv[:, :, 0, 1], kv_cache)
+    )(place, far_lengths, winner, far_cache)
+
+    def attend_old(queries, new_kv, lengths):
+        grouped = queries.reshape(problems, steps * heads, head_dim)
+        partial = jax.ShapeDtypeStruct(grouped.shape, f32)
+        return pl.pallas_call(
+            functools.partial(old_kernel, factor=factor),
+            out_shape=(partial,) * 3 + (jax.ShapeDtypeStruct(partial.shape, bf16),),
+            in_specs=[SMEM, VMEM, VMEM, VMEM, HBM],
+            out_specs=(VMEM,) * 4,
+            scratch_shapes=[
+                pltpu.VMEM((problems, 2, slots, head_dim), bf16),
+                pltpu.SemaphoreType.DMA((problems,)),
+            ],
+            **params(8, 2**24, 2**21),
+        )(lengths, grouped, new_kv[:, :, 0, 0], new_kv[:, :, 0, 1], far_cache)
+
+    def fetch_weights(weights):
+        return pl.pallas_call(
+            fetch_kernel,
+            out_shape=jax.ShapeDtypeStruct(weights.shape, bf16),
+            in_specs=[HBM],
+            out_specs=VMEM,
+            scratch_shapes=[pltpu.SemaphoreType.DMA((8,))],
+            **params(12, 0, 2**24),
+        )(weights)
 
     block = keep + exchange(send, "cand", 32, 1)
-    for bit in (8, 24, 2, 6):
-        received = exchange(block, "cand", 32, bit)
-        if bit == 8:
-            received, partials = lax.optimization_barrier((received, partials))
-        block = block + received
+    block = block + exchange(block, "cand", 32, 8)
+    far_values, block = lax.optimization_barrier((far_values, block))
+    received, weights = lax.optimization_barrier((exchange(block, "cand", 32, 24), fetch_weights(far_values)))
+    block = block + received
+    queries, new_kv, lengths, block = lax.optimization_barrier((queries, new_kv, lengths, block))
+    received, partials = lax.optimization_barrier(
+        (exchange(block, "cand", 32, 2), attend_old(queries, new_kv, lengths))
+    )
+    block = block + received
+    block = block + exchange(block, "cand", 32, 6)
     old, peak, total, grouped = partials
     other = exchange(block, "cand", 32, 1)
 
-    flat = (rows, head_dim)
+    weights = pltpu.with_memory_space_constraint(weights, pltpu.VMEM)
+    flat = (problems * steps * heads, head_dim)
     half_shape = jax.ShapeDtypeStruct((problems * steps, half), bf16)
-    scratch = [
-        pltpu.SMEM(out_scales.shape, f32),
-        pltpu.VMEM((out_values.shape[0], half), bf16),
-        pltpu.SemaphoreType.DMA((half // CHUNK + 1,)),
-    ]
+    scratch = [pltpu.SMEM(out_scales.shape, f32), pltpu.SemaphoreType.DMA]
     attended, away = pl.pallas_call(
         functools.partial(fork_kernel, factor=factor),
         out_shape=(jax.ShapeDtypeStruct(flat, f32), half_shape),
-        in_specs=[SMEM] + [VMEM] * 6 + [HBM, HBM],
+        in_specs=[SMEM] + [VMEM] * 6 + [HBM, VMEM],
         out_specs=(VMEM, VMEM),
         scratch_shapes=scratch,
-        **params(12, 2**26, 2**22),
+        **params(14, 2**26, 2**22),
     )(
         place,
         grouped.reshape(flat),
@@ -248,18 +255,18 @@
         old.reshape(flat),
         peak.reshape(flat),
         total.reshape(flat),
-        out_scales,
-        out_values,
+        far_scales,
+        weights,
     )
     arrived = exchange(away, "tp", 8, 1)
     home = pl.pallas_call(
         project_kernel,
         out_shape=half_shape,
-        in_specs=[SMEM, VMEM, HBM, HBM],
+        in_specs=[SMEM, VMEM, HBM, VMEM],
         out_specs=VMEM,
         scratch_shapes=scratch,
-        **params(12, 2**26, 2**22),
-    )(place, attended, out_scales, out_values)
+        **params(14, 2**26, 2**22),
+    )(place, attended, far_scales, weights)
 
     sums = home + arrived
     ahead, back, across = (exchange(sums, "tp", 8, bit) for bit in (2, 6, 4))

time: 64.2 us -> 61.1 us (0.952)
  the two profiles are of different devices: /device:TPU:6 before, /device:TPU:64 now
where the time goes in v3:
time: 61.1 us; the launch traced here: 60.9 us
  waiting for transfers between devices  27.1 us (44%)
  starting transfers between devices  17.9 us (29%)
  Pallas kernels  14.3 us (23%)
  local copies, waits for them, and re-layouts  1.02 us (2%)
    ppermute x11, waiting for transfers between devices, exchange(): return lax.ppermute(x, axis, [(i, i ^ bit) for i in range(size)])  27.1 us
    ppermute x11, starting transfers between devices, exchange(): return lax.ppermute(x, axis, [(i, i ^ bit) for i in range(size)])  17.9 us
    pallas_call x1, Pallas kernels, attend_old(): pl.pallas_call(functools.partial(old_kernel, factor=factor), out_shape=(p...  4.43 us
    pallas_call x1, Pallas kernels, fetch_weights(): pl.pallas_call(fetch_kernel, out_shape=jax.ShapeDtypeStruct(weights.shape...  3.47 us
    pallas_call x1, Pallas kernels, local(): pl.pallas_call(extract_kernel, out_shape=(fork_shape, fork_shape), in_spe...  2.31 us
    pallas_call x1, Pallas kernels, local(): pl.pallas_call(functools.partial(fork_kernel, factor=factor), out_shape=(...  2.17 us
    pallas_call x1, Pallas kernels, local(): pl.pallas_call(project_kernel, out_shape=half_shape, in_specs=[SMEM, VMEM...  1.91 us
  transfers between devices with their start and end apart: 11, of which 9 were waited for; matrix products, arithmetic and copies ran while one was open for 0% of the time, Pallas kernels for 16%

profile of v3, /device:TPU:64, one launch (start us, length us, event | category | flops | bytes accessed | tf_op | source)
XLA Modules:
  0.0 60.9 jit_solution(4112153031523439301)
XLA Ops:
  0.1 2.3 %shard_map.82 = (bf16[2,256,128]{2,1,0:T(8,128)(2,1)S(1)}, bf16[2,256,128]{2,1,0:T(8,128)(2,1)S(1)}) custom-call(s32[3]{0:T(128)S(1)} %pad_add_fusion.place, s32[8]{0:T(128)} %lengths, s32[8]{0:T(128)} %winner_in.1, bf16[8,1,2,512,128]{4,3,2,1,0:T(8,128)(2,1)} %cache.3), custom_call_target="tpu_custom_call" | custom-call | bytes 524288 | tf_op jit(solution)/shard_map/pallas_call | solution.py:186
  2.5 1.3 %collective-permute-done = bf16[2,256,128]{2,1,0:T(8,128)(2,1)S(1)} collective-permute-done((bf16[2,256,128]{2,1,0:T(8,128)(2,1)S(1)}, bf16[2,256,128]{2,1,0:T(8,128)(2,1)S(1)}, u32[]{:S(2)}, u32[]{:S(2)}) %collective-permute-start) | collective-permute-done | bytes 131104 | tf_op jit(solution)/shard_map/ppermute | solution.py:21
  3.9 1.6 %collective-permute-start.1 = (bf16[2,256,128]{2,1,0:T(8,128)(2,1)S(1)}, bf16[2,256,128]{2,1,0:T(8,128)(2,1)S(1)}, u32[]{:S(2)}, u32[]{:S(2)}) collective-permute-start(bf16[2,256,128]{2,1,0:T(8,128)(2,1)S(1)} %add.45), channel_id=1, source_target_pairs={{0,64},{8,72},{16,80},{24,88},{32,96},{40,104},{48,112},{56,120},{... | collective-permute-start | bytes 393224 | tf_op jit(solution)/shard_map/ppermute | solution.py:21
  5.4 4.1 %collective-permute-done.1 = bf16[2,256,128]{2,1,0:T(8,128)(2,1)S(1)} collective-permute-done((bf16[2,256,128]{2,1,0:T(8,128)(2,1)S(1)}, bf16[2,256,128]{2,1,0:T(8,128)(2,1)S(1)}, u32[]{:S(2)}, u32[]{:S(2)}) %collective-permute-start.1) | collective-permute-done | bytes 131104 | tf_op jit(solution)/shard_map/ppermute | solution.py:21
  9.6 2.8 %collective-permute-start.2 = (bf16[2,256,128]{2,1,0:T(8,128)(2,1)S(1)}, bf16[2,256,128]{2,1,0:T(8,128)(2,1)S(1)}, u32[]{:S(2)}, u32[]{:S(2)}) collective-permute-start(bf16[2,256,128]{2,1,0:T(8,128)(2,1)S(1)} %add.46), channel_id=1, source_target_pairs={{0,192},{8,200},{16,208},{24,216},{32,224},{40,232},{48,240},{56,2... | collective-permute-start | bytes 393224 | tf_op jit(solution)/shard_map/ppermute | solution.py:21
  12.4 3.5 %shard_map.83.weights = bf16[512,8192]{1,0:T(8,128)(2,1)S(1)} custom-call(bf16[512,8192]{1,0:T(8,128)(2,1)} %far), custom_call_target="tpu_custom_call" | custom-call | bytes 16777216 | tf_op jit(solution)/shard_map/pallas_call | solution.py:216
  16.0 1.4 %collective-permute-start.3 = (bf16[2,256,128]{2,1,0:T(8,128)(2,1)S(1)}, bf16[2,256,128]{2,1,0:T(8,128)(2,1)S(1)}, u32[]{:S(2)}, u32[]{:S(2)}) collective-permute-start(bf16[2,256,128]{2,1,0:T(8,128)(2,1)S(1)} %add.47), channel_id=1, source_target_pairs={{0,16},{8,24},{16,0},{24,8},{32,48},{40,56},{48,32},{56,40},{64,80... | collective-permute-start | bytes 393224 | tf_op jit(solution)/shard_map/ppermute | solution.py:21
  17.4 4.4 %shard_map.84 = (f32[8,8,128]{2,1,0:T(8,128)S(1)}, f32[8,8,128]{2,1,0:T(8,128)S(1)}, f32[8,8,128]{2,1,0:T(8,128)S(1)}, bf16[8,8,128]{2,1,0:T(8,128)(2,1)S(1)}) custom-call(s32[8]{0:T(128)S(1)} %copy-done.1, bf16[8,8,128]{2,1,0:T(8,128)(2,1)S(1)} %bitcast.15, bf16[8,2,128]{2,1,0:T(2,128)(2,1)S(1)} %get-tuple-element.50.new_keys, ...), custom_call_target="tpu_custom_call" | custom-call | flops 16777216 | bytes 2097152 | tf_op jit(solution)/shard_map/pallas_call | solution.py:203
  22.0 6.9 %collective-permute-start.4 = (bf16[2,256,128]{2,1,0:T(8,128)(2,1)S(1)}, bf16[2,256,128]{2,1,0:T(8,128)(2,1)S(1)}, u32[]{:S(2)}, u32[]{:S(2)}) collective-permute-start(bf16[2,256,128]{2,1,0:T(8,128)(2,1)S(1)} %add.48), channel_id=1, source_target_pairs={{0,48},{8,56},{16,32},{24,40},{32,16},{40,24},{48,0},{56,8},{64,11... | collective-permute-start | bytes 393224 | tf_op jit(solution)/shard_map/ppermute | solution.py:21
  28.8 6.0 %collective-permute-done.4 = bf16[2,256,128]{2,1,0:T(8,128)(2,1)S(1)} collective-permute-done((bf16[2,256,128]{2,1,0:T(8,128)(2,1)S(1)}, bf16[2,256,128]{2,1,0:T(8,128)(2,1)S(1)}, u32[]{:S(2)}, u32[]{:S(2)}) %collective-permute-start.4) | collective-permute-done | bytes 131104 | tf_op jit(solution)/shard_map/ppermute | solution.py:21
  34.9 0.1 collective-permute-start.5
  35.0 1.3 %collective-permute-done.5.other = bf16[2,256,128]{2,1,0:T(8,128)(2,1)S(1)} collective-permute-done((bf16[2,256,128]{2,1,0:T(8,128)(2,1)S(1)}, bf16[2,256,128]{2,1,0:T(8,128)(2,1)S(1)}, u32[]{:S(2)}, u32[]{:S(2)}) %collective-permute-start.5) | collective-permute-done | bytes 131104 | tf_op jit(solution)/shard_map/ppermute | solution.py:21
  36.3 2.2 %shard_map.85 = (f32[64,128]{1,0:T(8,128)S(1)}, bf16[16,4096]{1,0:T(8,128)(2,1)S(1)}) custom-call(s32[3]{0:T(128)S(1)} %pad_add_fusion.place, bf16[64,128]{1,0:T(8,128)(2,1)S(1)} %bitcast.16, bf16[2,256,128]{2,1,0:T(8,128)(2,1)S(1)} %add.49.mine, bf16[2,256,128]{2,1,0:T(8,128)(2,1)S(1)} %collective-permute-done.5.other, f32[64,128]{1,0:T(8,128)S(1)} %bitcast.12, ...), custom_call_target="tpu_custom_call" | custom-call | flops 67108864 | bytes 4194304 | tf_op jit(solution)/shard_map/pallas_call | solution.py:243
  38.6 1.9 %shard_map.86 = bf16[16,4096]{1,0:T(8,128)(2,1)S(1)} custom-call(s32[3]{0:T(128)S(1)} %pad_add_fusion.place, f32[64,128]{1,0:T(8,128)S(1)} %get-tuple-element.45.attended, f32[4,64]{1,0:T(4,128)} %scales_in.3, bf16[512,8192]{1,0:T(8,128)(2,1)S(1)} %shard_map.83.weights), custom_call_target="tpu_custom_call" | custom-call | flops 67108864 | bytes 4194304 | tf_op jit(solution)/shard_map/pallas_call | solution.py:262
  40.5 3.6 %collective-permute-done.6 = bf16[16,4096]{1,0:T(8,128)(2,1)S(1)} collective-permute-done((bf16[16,4096]{1,0:T(8,128)(2,1)S(1)}, bf16[16,4096]{1,0:T(8,128)(2,1)S(1)}, u32[]{:S(2)}, u32[]{:S(2)}) %collective-permute-start.6) | collective-permute-done | bytes 131104 | tf_op jit(solution)/shard_map/ppermute | solution.py:21
  44.1 1.7 %collective-permute-start.7 = (bf16[16,4096]{1,0:T(8,128)(2,1)S(1)}, bf16[16,4096]{1,0:T(8,128)(2,1)S(1)}, u32[]{:S(2)}, u32[]{:S(2)}) collective-permute-start(bf16[16,4096]{1,0:T(8,128)(2,1)S(1)} %add.50), channel_id=1, source_target_pairs={{0,2},{1,3},{2,0},{3,1},{4,6},{5,7},{6,4},{7,5},{8,10},{9,11},{10,... | collective-permute-start | bytes 393224 | tf_op jit(solution)/shard_map/ppermute | solution.py:21
  45.8 2.2 %collective-permute-start.8 = (bf16[16,4096]{1,0:T(8,128)(2,1)S(1)}, bf16[16,4096]{1,0:T(8,128)(2,1)S(1)}, u32[]{:S(2)}, u32[]{:S(2)}) collective-permute-start(bf16[16,4096]{1,0:T(8,128)(2,1)S(1)} %add.50), channel_id=1, source_target_pairs={{0,6},{1,7},{2,4},{3,5},{4,2},{5,3},{6,0},{7,1},{8,14},{9,15},{10,... | collective-permute-start | bytes 393224 | tf_op jit(solution)/shard_map/ppermute | solution.py:21
  48.0 0.7 %collective-permute-start.9 = (bf16[16,4096]{1,0:T(8,128)(2,1)S(1)}, bf16[16,4096]{1,0:T(8,128)(2,1)S(1)}, u32[]{:S(2)}, u32[]{:S(2)}) collective-permute-start(bf16[16,4096]{1,0:T(8,128)(2,1)S(1)} %add.50), channel_id=1, source_target_pairs={{0,4},{1,5},{2,6},{3,7},{4,0},{5,1},{6,2},{7,3},{8,12},{9,13},{10,... | collective-permute-start | bytes 393224 | tf_op jit(solution)/shard_map/ppermute | solution.py:21
  48.7 0.1 reshape.21
  48.8 0.4 collective-permute-done.7
  49.2 5.6 %collective-permute-done.8 = bf16[16,4096]{1,0:T(8,128)(2,1)S(1)} collective-permute-done((bf16[16,4096]{1,0:T(8,128)(2,1)S(1)}, bf16[16,4096]{1,0:T(8,128)(2,1)S(1)}, u32[]{:S(2)}, u32[]{:S(2)}) %collective-permute-start.8) | collective-permute-done | bytes 131104 | tf_op jit(solution)/shard_map/ppermute | solution.py:21
  54.9 0.4 collective-permute-start.10
  55.3 4.7 %collective-permute-done.10 = bf16[16,4096]{1,0:T(8,128)(2,1)S(1)} collective-permute-done((bf16[16,4096]{1,0:T(8,128)(2,1)S(1)}, bf16[16,4096]{1,0:T(8,128)(2,1)S(1)}, u32[]{:S(2)}, u32[]{:S(2)}) %collective-permute-start.10) | collective-permute-done | bytes 131104 | tf_op jit(solution)/shard_map/ppermute | solution.py:21
  60.0 0.9 %reshape.27 = bf16[8,2,8192]{2,1,0:T(2,128)(2,1)} reshape(bf16[16,8192]{1,0:T(8,128)(2,1)S(1)} %pad_maximum_fusion) | data formatting | bytes 524288 | tf_op jit(solution)/shard_map/reshape | solution.py:282
  (25 shorter events, 0.7 us)
Async XLA Ops:
  2.4 1.4 %collective-permute-start = (bf16[2,256,128]{2,1,0:T(8,128)(2,1)S(1)}, bf16[2,256,128]{2,1,0:T(8,128)(2,1)S(1)}, u32[]{:S(2)}, u32[]{:S(2)}) collective-permute-start(bf16[2,256,128]{2,1,0:T(8,128)(2,1)S(1)} %get-tuple-element.27), channel_id=1, source_target_pairs={{0,8},{8,0},{16,24},{24,16},{32,40},{40,32},{48,56},{56,48},{64,72... | collective-permute-start | bytes 393224 | tf_op jit(solution)/shard_map/ppermute | solution.py:21
  3.9 5.6 %collective-permute-start.1 = (bf16[2,256,128]{2,1,0:T(8,128)(2,1)S(1)}, bf16[2,256,128]{2,1,0:T(8,128)(2,1)S(1)}, u32[]{:S(2)}, u32[]{:S(2)}) collective-permute-start(bf16[2,256,128]{2,1,0:T(8,128)(2,1)S(1)} %add.45), channel_id=1, source_target_pairs={{0,64},{8,72},{16,80},{24,88},{32,96},{40,104},{48,112},{56,120},{... | collective-permute-start | bytes 393224 | tf_op jit(solution)/shard_map/ppermute | solution.py:21
  9.5 6.4 %copy-start.3 = (bf16[8,2,1,2,128]{4,3,2,1,0:T(2,128)(2,1)S(1)}, bf16[8,2,1,2,128]{4,3,2,1,0:T(2,128)(2,1)}, u32[]{:S(2)}) copy-start(bf16[8,2,1,2,128]{4,3,2,1,0:T(2,128)(2,1)} %param.10) | copy-start | bytes 24580
  9.6 7.8 %copy-start = (bf16[8,2,4,128]{3,2,1,0:T(4,128)(2,1)S(1)}, bf16[8,2,4,128]{3,2,1,0:T(4,128)(2,1)}, u32[]{:S(2)}) copy-start(bf16[8,2,4,128]{3,2,1,0:T(4,128)(2,1)} %param.9) | copy-start | bytes 49156
  9.6 7.8 %copy-start.1 = (s32[8]{0:T(128)S(1)}, s32[8]{0:T(128)}, u32[]{:S(2)}) copy-start(s32[8]{0:T(128)} %lengths) | copy-start | bytes 100
  9.6 6.3 %collective-permute-start.2 = (bf16[2,256,128]{2,1,0:T(8,128)(2,1)S(1)}, bf16[2,256,128]{2,1,0:T(8,128)(2,1)S(1)}, u32[]{:S(2)}, u32[]{:S(2)}) collective-permute-start(bf16[2,256,128]{2,1,0:T(8,128)(2,1)S(1)} %add.46), channel_id=1, source_target_pairs={{0,192},{8,200},{16,208},{24,216},{32,224},{40,232},{48,240},{56,2... | collective-permute-start | bytes 393224 | tf_op jit(solution)/shard_map/ppermute | solution.py:21
  16.0 6.0 %collective-permute-start.3 = (bf16[2,256,128]{2,1,0:T(8,128)(2,1)S(1)}, bf16[2,256,128]{2,1,0:T(8,128)(2,1)S(1)}, u32[]{:S(2)}, u32[]{:S(2)}) collective-permute-start(bf16[2,256,128]{2,1,0:T(8,128)(2,1)S(1)} %add.47), channel_id=1, source_target_pairs={{0,16},{8,24},{16,0},{24,8},{32,48},{40,56},{48,32},{56,40},{64,80... | collective-permute-start | bytes 393224 | tf_op jit(solution)/shard_map/ppermute | solution.py:21
  22.0 12.8 %collective-permute-start.4 = (bf16[2,256,128]{2,1,0:T(8,128)(2,1)S(1)}, bf16[2,256,128]{2,1,0:T(8,128)(2,1)S(1)}, u32[]{:S(2)}, u32[]{:S(2)}) collective-permute-start(bf16[2,256,128]{2,1,0:T(8,128)(2,1)S(1)} %add.48), channel_id=1, source_target_pairs={{0,48},{8,56},{16,32},{24,40},{32,16},{40,24},{48,0},{56,8},{64,11... | collective-permute-start | bytes 393224 | tf_op jit(solution)/shard_map/ppermute | solution.py:21
  34.9 1.4 %collective-permute-start.5 = (bf16[2,256,128]{2,1,0:T(8,128)(2,1)S(1)}, bf16[2,256,128]{2,1,0:T(8,128)(2,1)S(1)}, u32[]{:S(2)}, u32[]{:S(2)}) collective-permute-start(bf16[2,256,128]{2,1,0:T(8,128)(2,1)S(1)} %add.49.mine), channel_id=1, source_target_pairs={{0,8},{8,0},{16,24},{24,16},{32,40},{40,32},{48,56},{56,48},{64,72... | collective-permute-start | bytes 393224 | tf_op jit(solution)/shard_map/ppermute | solution.py:21
  36.3 12.4 %copy-start.2 = (bf16[8,2,8192]{2,1,0:T(2,128)(2,1)S(1)}, bf16[8,2,8192]{2,1,0:T(2,128)(2,1)}, u32[]{:S(2)}) copy-start(bf16[8,2,8192]{2,1,0:T(2,128)(2,1)} %param.8) | copy-start | bytes 786436
  38.5 5.6 %collective-permute-start.6 = (bf16[16,4096]{1,0:T(8,128)(2,1)S(1)}, bf16[16,4096]{1,0:T(8,128)(2,1)S(1)}, u32[]{:S(2)}, u32[]{:S(2)}) collective-permute-start(bf16[16,4096]{1,0:T(8,128)(2,1)S(1)} %get-tuple-element.46), channel_id=1, source_target_pairs={{0,1},{1,0},{2,3},{3,2},{4,5},{5,4},{6,7},{7,6},{8,9},{9,8},{10,11... | collective-permute-start | bytes 393224 | tf_op jit(solution)/shard_map/ppermute | solution.py:21
  44.1 5.1 %collective-permute-start.7 = (bf16[16,4096]{1,0:T(8,128)(2,1)S(1)}, bf16[16,4096]{1,0:T(8,128)(2,1)S(1)}, u32[]{:S(2)}, u32[]{:S(2)}) collective-permute-start(bf16[16,4096]{1,0:T(8,128)(2,1)S(1)} %add.50), channel_id=1, source_target_pairs={{0,2},{1,3},{2,0},{3,1},{4,6},{5,7},{6,4},{7,5},{8,10},{9,11},{10,... | collective-permute-start | bytes 393224 | tf_op jit(solution)/shard_map/ppermute | solution.py:21
  45.8 9.0 %collective-permute-start.8 = (bf16[16,4096]{1,0:T(8,128)(2,1)S(1)}, bf16[16,4096]{1,0:T(8,128)(2,1)S(1)}, u32[]{:S(2)}, u32[]{:S(2)}) collective-permute-start(bf16[16,4096]{1,0:T(8,128)(2,1)S(1)} %add.50), channel_id=1, source_target_pairs={{0,6},{1,7},{2,4},{3,5},{4,2},{5,3},{6,0},{7,1},{8,14},{9,15},{10,... | collective-permute-start | bytes 393224 | tf_op jit(solution)/shard_map/ppermute | solution.py:21
  48.0 6.8 %collective-permute-start.9 = (bf16[16,4096]{1,0:T(8,128)(2,1)S(1)}, bf16[16,4096]{1,0:T(8,128)(2,1)S(1)}, u32[]{:S(2)}, u32[]{:S(2)}) collective-permute-start(bf16[16,4096]{1,0:T(8,128)(2,1)S(1)} %add.50), channel_id=1, source_target_pairs={{0,4},{1,5},{2,6},{3,7},{4,0},{5,1},{6,2},{7,3},{8,12},{9,13},{10,... | collective-permute-start | bytes 393224 | tf_op jit(solution)/shard_map/ppermute | solution.py:21
  54.9 5.1 %collective-permute-start.10 = (bf16[16,4096]{1,0:T(8,128)(2,1)S(1)}, bf16[16,4096]{1,0:T(8,128)(2,1)S(1)}, u32[]{:S(2)}, u32[]{:S(2)}) collective-permute-start(bf16[16,4096]{1,0:T(8,128)(2,1)S(1)} %add_convert_fusion), channel_id=1, source_target_pairs={{0,1},{1,0},{2,3},{3,2},{4,5},{5,4},{6,7},{7,6},{8,9},{9,8},{10,11... | collective-permute-start | bytes 393224 | tf_op jit(solution)/shard_map/ppermute | solution.py:21

commit v4 on v3

--- a/solution.py
+++ b/solution.py
@@ -67,42 +67,53 @@
             where[0][kv, base + 16 : base + BLOCK, :] = tail
 
 
-def old_kernel(lengths, queries, new_keys, new_values, cache, out, peak, total, passed, held, sems, *, factor):
-    problems = cache.shape[0]
-    group = queries.shape[1] // 2
-    copies = []
-    for p in range(problems):
-        copies.append(pltpu.make_async_copy(cache.at[p, 0], held.at[p], sems.at[p]))
+def old_kernel(
+    lengths_in, queries_in, fresh_in, cache, out, peak, total, passed, lengths, fresh, held, sems, *, first, factor
+):
+    problems = out.shape[0]
+    group = passed.shape[1] // 2
+    copies = [
+        pltpu.make_async_copy(lengths_in, lengths, sems.at[problems]),
+        pltpu.make_async_copy(queries_in.at[first : first + problems], passed, sems.at[problems + 1]),
+        pltpu.make_async_copy(fresh_in.at[first : first + problems], fresh, sems.at[problems + 2]),
+    ]
+    for copy in copies:
+        copy.start()
+    for i in range(problems):
+        copies.append(pltpu.make_async_copy(cache.at[first + i, 0], held.at[i], sems.at[i]))
         copies[-1].start()
-    slots = lax.broadcasted_iota(jnp.int32, (queries.shape[1], cache.shape[3]), 1)
-    later = lax.broadcasted_iota(jnp.int32, (queries.shape[1], 1), 0) >= group
-    for p in range(problems):
-        query = queries[p]
+    slots = lax.broadcasted_iota(jnp.int32, (2 * group, cache.shape[3]), 1)
+    later = lax.broadcasted_iota(jnp.int32, (2 * group, 1), 0) >= group
+    for copy in copies:
+        copy.wait()
+    for i in range(problems):
+        query = passed[i]
         wide = query.astype(jnp.float32)
-        keys = [new_keys[p, u : u + 1, :].astype(jnp.float32) for u in range(2)]
-        fresh = [jnp.sum(wide * key, -1, keepdims=True) * factor for key in keys]
-        fresh[1] = jnp.where(later, fresh[1], -jnp.inf)
-        copies[p].wait()
-        scores = lax.dot_general(query, held[p, 0], NT, preferred_element_type=jnp.float32) * factor
-        scores = jnp.where(slots < lengths[p] - BLOCK, scores, -jnp.inf)
-        top = jnp.maximum(jnp.max(scores, -1, keepdims=True), jnp.maximum(fresh[0], fresh[1]))
+        keys = [fresh[i, 2 * u : 2 * u + 1, :].astype(jnp.float32) for u in range(2)]
+        values = [fresh[i, 2 * u + 1 : 2 * u + 2, :].astype(jnp.float32) for u in range(2)]
+        new = [jnp.sum(wide * key, -1, keepdims=True) * factor for key in keys]
+        new[1] = jnp.where(later, new[1], -jnp.inf)
+        scores = lax.dot_general(query, held[i, 0], NT, preferred_element_type=jnp.float32) * factor
+        scores = jnp.where(slots < lengths[first + i] - BLOCK, scores, -jnp.inf)
+        top = jnp.maximum(jnp.max(scores, -1, keepdims=True), jnp.maximum(new[0], new[1]))
         weights = jnp.exp(scores - top)
         sums = jnp.sum(weights, -1, keepdims=True)
-        mixed = jnp.dot(weights.astype(jnp.bfloat16), held[p, 1], preferred_element_type=jnp.float32)
+        mixed = jnp.dot(weights.astype(jnp.bfloat16), held[i, 1], preferred_element_type=jnp.float32)
         for u in range(2):
-            weight = jnp.exp(fresh[u] - top)
+            weight = jnp.exp(new[u] - top)
             sums = sums + weight
-            mixed = mixed + weight * new_values[p, u : u + 1, :].astype(jnp.float32)
-        passed[p] = query
-        out[p] = mixed
-        peak[p] = jnp.broadcast_to(top, mixed.shape)
-        total[p] = jnp.broadcast_to(sums, mixed.shape)
-
-
-def fetch_kernel(far, near, sems):
+            mixed = mixed + weight * values[u]
+        out[i] = mixed
+        peak[i] = jnp.broadcast_to(top, mixed.shape)
+        total[i] = jnp.broadcast_to(sums, mixed.shape)
+
+
+def fetch_kernel(place, far, near, sems, *, own):
     rows = far.shape[0] // sems.shape[0]
+    half = place[2] if own else 1 - place[2]
+    columns = pl.ds(pl.multiple_of(half * near.shape[1], 128), near.shape[1])
     copies = [
-        pltpu.make_async_copy(far.at[pl.ds(i * rows, rows)], near.at[pl.ds(i * rows, rows)], sems.at[i])
+        pltpu.make_async_copy(far.at[pl.ds(i * rows, rows), columns], near.at[pl.ds(i * rows, rows)], sems.at[i])
         for i in range(sems.shape[0])
     ]
     for copy in copies:
@@ -115,7 +126,7 @@
     blocks, side = scales.shape[0], weights.shape[0] // scales.shape[0]
     parts = [attended[pl.ds(b, 16, stride=blocks), :].astype(jnp.bfloat16) for b in range(blocks)]
     for c in range(out.shape[1] // CHUNK):
-        columns = pl.ds(pl.multiple_of(base + c * CHUNK, CHUNK), CHUNK)
+        columns = slice(c * CHUNK, (c + 1) * CHUNK)
         terms = [
             jnp.dot(parts[b], weights[b * side : (b + 1) * side, columns], preferred_element_type=jnp.float32)
             for b in range(blocks)
@@ -128,24 +139,24 @@
             out[:, c * CHUNK + n * 128 : c * CHUNK + (n + 1) * 128] = sums.astype(out.dtype)
 
 
-def fork_kernel(
-    place, queries, mine, other, old, peak, total, scales_in, weights, attended, out, scales, sem, *, factor
-):
+def fork_kernel(place, mine, other, *refs, factor):
+    parts, (scales_in, weights, attended, out, scales, sem) = refs[:8], refs[8:]
     scales_copy = pltpu.make_async_copy(scales_in, scales, sem)
     scales_copy.start()
+    old, peak, total, queries = (jnp.concatenate([parts[i][...], parts[i + 4][...]], 0) for i in range(4))
     rows, keys_here = queries.shape[0], mine.shape[1]
     per_row = rows // (2 * keys_here // BLOCK)
     halves = []
     for half, ref in ((place[1], mine), (1 - place[1], other)):
-        scores = lax.dot_general(queries[...], ref[0], NT, preferred_element_type=jnp.float32) * factor
+        scores = lax.dot_general(queries, ref[0], NT, preferred_element_type=jnp.float32) * factor
         row = lax.broadcasted_iota(jnp.int32, scores.shape, 0) // per_row
         owner = lax.broadcasted_iota(jnp.int32, scores.shape, 1) // BLOCK + half * (keys_here // BLOCK)
         halves.append(jnp.where(row == owner, scores, -jnp.inf))
     top = jnp.maximum(jnp.max(halves[0], -1, keepdims=True), jnp.max(halves[1], -1, keepdims=True))
-    top = jnp.maximum(peak[...], top)
-    kept = jnp.exp(peak[...] - top)
-    sums = total[...] * kept
-    mixed = old[...] * kept
+    top = jnp.maximum(peak, top)
+    kept = jnp.exp(peak - top)
+    sums = total * kept
+    mixed = old * kept
     for scores, ref in zip(halves, (mine, other)):
         share = jnp.exp(scores - top[:, :1])
         sums = sums + jnp.sum(share, -1, keepdims=True)
@@ -197,66 +208,80 @@
         **params(4, 0, 2**19),
     )(place, far_lengths, winner, far_cache)
 
-    def attend_old(queries, new_kv, lengths):
-        grouped = queries.reshape(problems, steps * heads, head_dim)
-        partial = jax.ShapeDtypeStruct(grouped.shape, f32)
+    def attend_old(queries, fresh, lengths, first):
+        queries, fresh, lengths = (
+            pltpu.with_memory_space_constraint(x, pltpu.HBM) for x in (queries, fresh, lengths)
+        )
+        partial = jax.ShapeDtypeStruct((problems // 2, steps * heads, head_dim), f32)
         return pl.pallas_call(
-            functools.partial(old_kernel, factor=factor),
+            functools.partial(old_kernel, first=first, factor=factor),
             out_shape=(partial,) * 3 + (jax.ShapeDtypeStruct(partial.shape, bf16),),
-            in_specs=[SMEM, VMEM, VMEM, VMEM, HBM],
+            in_specs=[HBM, HBM, HBM, HBM],
             out_specs=(VMEM,) * 4,
             scratch_shapes=[
-                pltpu.VMEM((problems, 2, slots, head_dim), bf16),
-                pltpu.SemaphoreType.DMA((problems,)),
+                pltpu.SMEM(lengths.shape, jnp.int32),
+                pltpu.VMEM((problems // 2, *fresh.shape[1:]), bf16),
+                pltpu.VMEM((problems // 2, 2, slots, head_dim), bf16),
+                pltpu.SemaphoreType.DMA((problems // 2 + 3,)),
             ],
-            **params(8, 2**24, 2**21),
-        )(lengths, grouped, new_kv[:, :, 0, 0], new_kv[:, :, 0, 1], far_cache)
-
-    def fetch_weights(weights):
+            **params(8, 2**23, 2**20),
+        )(lengths, queries, fresh, far_cache)
+
+    def fetch_weights(weights, own):
         return pl.pallas_call(
-            fetch_kernel,
-            out_shape=jax.ShapeDtypeStruct(weights.shape, bf16),
-            in_specs=[HBM],
+            functools.partial(fetch_kernel, own=own),
+            out_shape=jax.ShapeDtypeStruct((weights.shape[0], half), bf16),
+            in_specs=[SMEM, HBM],
             out_specs=VMEM,
             scratch_shapes=[pltpu.SemaphoreType.DMA((8,))],
-            **params(12, 0, 2**24),
-        )(weights)
+            **params(8, 0, 2**23),
+        )(place, weights)
 
     block = keep + exchange(send, "cand", 32, 1)
-    block = block + exchange(block, "cand", 32, 8)
+    queries = queries.reshape(problems, steps * heads, head_dim)
+    fresh = new_kv.reshape(problems, 2 * steps, head_dim)
+    queries, fresh, lengths, block = lax.optimization_barrier((queries, fresh, lengths, block))
+    received, part = lax.optimization_barrier(
+        (exchange(block, "cand", 32, 8), attend_old(queries, fresh, lengths, 0))
+    )
+    block = block + received
+    queries, fresh, lengths, block = lax.optimization_barrier((queries, fresh, lengths, block))
+    received, rest = lax.optimization_barrier(
+        (exchange(block, "cand", 32, 24), attend_old(queries, fresh, lengths, problems // 2))
+    )
+    block = block + received
     far_values, block = lax.optimization_barrier((far_values, block))
-    received, weights = lax.optimization_barrier((exchange(block, "cand", 32, 24), fetch_weights(far_values)))
+    received, away_weights = lax.optimization_barrier(
+        (exchange(block, "cand", 32, 2), fetch_weights(far_values, False))
+    )
     block = block + received
-    queries, new_kv, lengths, block = lax.optimization_barrier((queries, new_kv, lengths, block))
-    received, partials = lax.optimization_barrier(
-        (exchange(block, "cand", 32, 2), attend_old(queries, new_kv, lengths))
+    far_values, block = lax.optimization_barrier((far_values, block))
+    received, home_weights = lax.optimization_barrier(
+        (exchange(block, "cand", 32, 6), fetch_weights(far_values, True))
     )
     block = block + received
-    block = block + exchange(block, "cand", 32, 6)
-    old, peak, total, grouped = partials
     other = exchange(block, "cand", 32, 1)
 
-    weights = pltpu.with_memory_space_constraint(weights, pltpu.VMEM)
+    away_weights, home_weights = (
+        pltpu.with_memory_space_constraint(x, pltpu.VMEM) for x in (away_weights, home_weights)
+    )
     flat = (problems * steps * heads, head_dim)
     half_shape = jax.ShapeDtypeStruct((problems * steps, half), bf16)
     scratch = [pltpu.SMEM(out_scales.shape, f32), pltpu.SemaphoreType.DMA]
     attended, away = pl.pallas_call(
         functools.partial(fork_kernel, factor=factor),
         out_shape=(jax.ShapeDtypeStruct(flat, f32), half_shape),
-        in_specs=[SMEM] + [VMEM] * 6 + [HBM, VMEM],
+        in_specs=[SMEM] + [VMEM] * 10 + [HBM, VMEM],
         out_specs=(VMEM, VMEM),
         scratch_shapes=scratch,
         **params(14, 2**26, 2**22),
     )(
         place,
-        grouped.reshape(flat),
         block,
         other,
-        old.reshape(flat),
-        peak.reshape(flat),
-        total.reshape(flat),
+        *(x.reshape(flat[0] // 2, head_dim) for x in (*part, *rest)),
         far_scales,
-        weights,
+        away_weights,
     )
     arrived = exchange(away, "tp", 8, 1)
     home = pl.pallas_call(
@@ -266,7 +291,7 @@
         out_specs=VMEM,
         scratch_shapes=scratch,
         **params(14, 2**26, 2**22),
-    )(place, attended, far_scales, weights)
+    )(place, attended, far_scales, home_weights)
 
     sums = home + arrived
     ahead, back, across = (exchange(sums, "tp", 8, bit) for bit in (2, 6, 4))

time: 61.1 us -> 58.8 us (0.962)
  the two profiles are of different devices: /device:TPU:64 before, /device:TPU:6 now
where the time goes in v4:
time: 58.8 us; the launch traced here: 58.5 us
  starting transfers between devices  20.5 us (35%)
  waiting for transfers between devices  19.9 us (34%)
  Pallas kernels  16.6 us (28%)
  local copies, waits for them, and re-layouts  0.99 us (2%)
    ppermute x11, starting transfers between devices, exchange(): return lax.ppermute(x, axis, [(i, i ^ bit) for i in range(size)])  20.5 us
    ppermute x11, waiting for transfers between devices, exchange(): return lax.ppermute(x, axis, [(i, i ^ bit) for i in range(size)])  19.9 us
    pallas_call x2, Pallas kernels, fetch_weights(): pl.pallas_call(functools.partial(fetch_kernel, own=own), out_shape=jax.Sh...  5.52 us
    pallas_call x2, Pallas kernels, attend_old(): pl.pallas_call(functools.partial(old_kernel, first=first, factor=factor),...  4.7 us
    pallas_call x1, Pallas kernels, local(): pl.pallas_call(extract_kernel, out_shape=(fork_shape, fork_shape), in_spe...  2.31 us
    pallas_call x1, Pallas kernels, local(): pl.pallas_call(functools.partial(fork_kernel, factor=factor), out_shape=(...  2.17 us
    pallas_call x1, Pallas kernels, local(): pl.pallas_call(project_kernel, out_shape=half_shape, in_specs=[SMEM, VMEM...  1.9 us
  transfers between devices with their start and end apart: 11, of which 10 were waited for; matrix products, arithmetic and copies ran while one was open for 0% of the time, Pallas kernels for 21%

profile of v4, /device:TPU:6, one launch (start us, length us, event | category | flops | bytes accessed | tf_op | source)
XLA Modules:
  0.0 58.5 jit_solution(8926091679229656131)
XLA Ops:
  0.1 2.3 %shard_map.82 = (bf16[2,256,128]{2,1,0:T(8,128)(2,1)S(1)}, bf16[2,256,128]{2,1,0:T(8,128)(2,1)S(1)}) custom-call(s32[3]{0:T(128)S(1)} %pad_add_fusion.place, s32[8]{0:T(128)} %lengths_in.3, s32[8]{0:T(128)} %winner_in.1, bf16[8,1,2,512,128]{4,3,2,1,0:T(8,128)(2,1)} %cache.5), custom_call_target="tpu_custom_call" | custom-call | bytes 524288 | tf_op jit(solution)/shard_map/pallas_call | solution.py:197
  2.5 1.3 %collective-permute-done = bf16[2,256,128]{2,1,0:T(8,128)(2,1)S(1)} collective-permute-done((bf16[2,256,128]{2,1,0:T(8,128)(2,1)S(1)}, bf16[2,256,128]{2,1,0:T(8,128)(2,1)S(1)}, u32[]{:S(2)}, u32[]{:S(2)}) %collective-permute-start) | collective-permute-done | bytes 131104 | tf_op jit(solution)/shard_map/ppermute | solution.py:21
  3.9 0.9 %collective-permute-start.1 = (bf16[2,256,128]{2,1,0:T(8,128)(2,1)S(1)}, bf16[2,256,128]{2,1,0:T(8,128)(2,1)S(1)}, u32[]{:S(2)}, u32[]{:S(2)}) collective-permute-start(bf16[2,256,128]{2,1,0:T(8,128)(2,1)S(1)} %add.45), channel_id=1, source_target_pairs={{0,64},{8,72},{16,80},{24,88},{32,96},{40,104},{48,112},{56,120},{... | collective-permute-start | bytes 393224 | tf_op jit(solution)/shard_map/ppermute | solution.py:21
  4.8 2.3 %shard_map.83 = (f32[4,8,128]{2,1,0:T(8,128)S(1)}, f32[4,8,128]{2,1,0:T(8,128)S(1)}, f32[4,8,128]{2,1,0:T(8,128)S(1)}, bf16[4,8,128]{2,1,0:T(8,128)(2,1)S(1)}) custom-call(s32[8]{0:T(128)} %lengths_in.3, bf16[8,8,128]{2,1,0:T(8,128)(2,1)} %bitcast.21, bf16[8,4,128]{2,1,0:T(4,128)(2,1)} %bitcast.23, bf16[8,1,2,512,128]{4,3,2,1,0:T(8,128)(2,1)} %cache.5), custom_call_target="tpu_custom_call" | custom-call | flops 8388608 | bytes 1048576 | tf_op jit(solution)/shard_map/pallas_call | solution.py:216
  7.1 2.4 %collective-permute-done.1 = bf16[2,256,128]{2,1,0:T(8,128)(2,1)S(1)} collective-permute-done((bf16[2,256,128]{2,1,0:T(8,128)(2,1)S(1)}, bf16[2,256,128]{2,1,0:T(8,128)(2,1)S(1)}, u32[]{:S(2)}, u32[]{:S(2)}) %collective-permute-start.1) | collective-permute-done | bytes 131104 | tf_op jit(solution)/shard_map/ppermute | solution.py:21
  9.5 2.3 %collective-permute-start.2 = (bf16[2,256,128]{2,1,0:T(8,128)(2,1)S(1)}, bf16[2,256,128]{2,1,0:T(8,128)(2,1)S(1)}, u32[]{:S(2)}, u32[]{:S(2)}) collective-permute-start(bf16[2,256,128]{2,1,0:T(8,128)(2,1)S(1)} %add.46), channel_id=1, source_target_pairs={{0,192},{8,200},{16,208},{24,216},{32,224},{40,232},{48,240},{56,2... | collective-permute-start | bytes 393224 | tf_op jit(solution)/shard_map/ppermute | solution.py:21
  11.8 2.3 %shard_map.84 = (f32[4,8,128]{2,1,0:T(8,128)S(1)}, f32[4,8,128]{2,1,0:T(8,128)S(1)}, f32[4,8,128]{2,1,0:T(8,128)S(1)}, bf16[4,8,128]{2,1,0:T(8,128)(2,1)S(1)}) custom-call(s32[8]{0:T(128)} %lengths_in.3, bf16[8,8,128]{2,1,0:T(8,128)(2,1)} %bitcast.22, bf16[8,4,128]{2,1,0:T(4,128)(2,1)} %bitcast.24, bf16[8,1,2,512,128]{4,3,2,1,0:T(8,128)(2,1)} %cache.5), custom_call_target="tpu_custom_call" | custom-call | flops 8388608 | bytes 1048576 | tf_op jit(solution)/shard_map/pallas_call | solution.py:216
  14.2 1.6 %collective-permute-done.2 = bf16[2,256,128]{2,1,0:T(8,128)(2,1)S(1)} collective-permute-done((bf16[2,256,128]{2,1,0:T(8,128)(2,1)S(1)}, bf16[2,256,128]{2,1,0:T(8,128)(2,1)S(1)}, u32[]{:S(2)}, u32[]{:S(2)}) %collective-permute-start.2) | collective-permute-done | bytes 131104 | tf_op jit(solution)/shard_map/ppermute | solution.py:21
  15.9 3.4 %collective-permute-start.3 = (bf16[2,256,128]{2,1,0:T(8,128)(2,1)S(1)}, bf16[2,256,128]{2,1,0:T(8,128)(2,1)S(1)}, u32[]{:S(2)}, u32[]{:S(2)}) collective-permute-start(bf16[2,256,128]{2,1,0:T(8,128)(2,1)S(1)} %add.47), channel_id=1, source_target_pairs={{0,16},{8,24},{16,0},{24,8},{32,48},{40,56},{48,32},{56,40},{64,80... | collective-permute-start | bytes 393224 | tf_op jit(solution)/shard_map/ppermute | solution.py:21
  19.2 2.8 %shard_map.85.refs_9_ = bf16[512,4096]{1,0:T(8,128)(2,1)S(1)} custom-call(s32[3]{0:T(128)S(1)} %pad_add_fusion.place, bf16[512,8192]{1,0:T(8,128)(2,1)} %far.1), custom_call_target="tpu_custom_call" | custom-call | bytes 8388608 | tf_op jit(solution)/shard_map/pallas_call | solution.py:231
  22.0 1.9 %collective-permute-done.3 = bf16[2,256,128]{2,1,0:T(8,128)(2,1)S(1)} collective-permute-done((bf16[2,256,128]{2,1,0:T(8,128)(2,1)S(1)}, bf16[2,256,128]{2,1,0:T(8,128)(2,1)S(1)}, u32[]{:S(2)}, u32[]{:S(2)}) %collective-permute-start.3) | collective-permute-done | bytes 131104 | tf_op jit(solution)/shard_map/ppermute | solution.py:21
  23.9 4.4 %collective-permute-start.4 = (bf16[2,256,128]{2,1,0:T(8,128)(2,1)S(1)}, bf16[2,256,128]{2,1,0:T(8,128)(2,1)S(1)}, u32[]{:S(2)}, u32[]{:S(2)}) collective-permute-start(bf16[2,256,128]{2,1,0:T(8,128)(2,1)S(1)} %add.48), channel_id=1, source_target_pairs={{0,48},{8,56},{16,32},{24,40},{32,16},{40,24},{48,0},{56,8},{64,11... | collective-permute-start | bytes 393224 | tf_op jit(solution)/shard_map/ppermute | solution.py:21
  28.3 2.8 %shard_map.86.weights = bf16[512,4096]{1,0:T(8,128)(2,1)S(1)} custom-call(s32[3]{0:T(128)S(1)} %pad_add_fusion.place, bf16[512,8192]{1,0:T(8,128)(2,1)} %far.1), custom_call_target="tpu_custom_call" | custom-call | bytes 8388608 | tf_op jit(solution)/shard_map/pallas_call | solution.py:231
  31.5 1.3 %collective-permute-done.5.other = bf16[2,256,128]{2,1,0:T(8,128)(2,1)S(1)} collective-permute-done((bf16[2,256,128]{2,1,0:T(8,128)(2,1)S(1)}, bf16[2,256,128]{2,1,0:T(8,128)(2,1)S(1)}, u32[]{:S(2)}, u32[]{:S(2)}) %collective-permute-start.5) | collective-permute-done | bytes 131104 | tf_op jit(solution)/shard_map/ppermute | solution.py:21
  32.8 2.2 %shard_map.87 = (f32[64,128]{1,0:T(8,128)S(1)}, bf16[16,4096]{1,0:T(8,128)(2,1)S(1)}) custom-call(s32[3]{0:T(128)S(1)} %pad_add_fusion.place, bf16[2,256,128]{2,1,0:T(8,128)(2,1)S(1)} %add.49.mine, bf16[2,256,128]{2,1,0:T(8,128)(2,1)S(1)} %collective-permute-done.5.other, f32[32,128]{1,0:T(8,128)S(1)} %bitcast.13, f32[32,128]{1,0:T(8,128)S(1)} %bitcast.14, ...), custom_call_target="tpu_custom_call" | custom-call | flops 67108864 | bytes 4194304 | tf_op jit(solution)/shard_map/pallas_call | solution.py:271
  35.0 2.9 %collective-permute-start.6 = (bf16[16,4096]{1,0:T(8,128)(2,1)S(1)}, bf16[16,4096]{1,0:T(8,128)(2,1)S(1)}, u32[]{:S(2)}, u32[]{:S(2)}) collective-permute-start(bf16[16,4096]{1,0:T(8,128)(2,1)S(1)} %get-tuple-element.80), channel_id=1, source_target_pairs={{0,1},{1,0},{2,3},{3,2},{4,5},{5,4},{6,7},{7,6},{8,9},{9,8},{10,11... | collective-permute-start | bytes 393224 | tf_op jit(solution)/shard_map/ppermute | solution.py:21
  37.9 1.9 %shard_map.88 = bf16[16,4096]{1,0:T(8,128)(2,1)S(1)} custom-call(s32[3]{0:T(128)S(1)} %pad_add_fusion.place, f32[64,128]{1,0:T(8,128)S(1)} %get-tuple-element.78.attended, f32[4,64]{1,0:T(4,128)} %scales_in.1, bf16[512,4096]{1,0:T(8,128)(2,1)S(1)} %shard_map.86.weights), custom_call_target="tpu_custom_call" | custom-call | flops 67108864 | bytes 4194304 | tf_op jit(solution)/shard_map/pallas_call | solution.py:287
  39.8 1.9 %collective-permute-done.6 = bf16[16,4096]{1,0:T(8,128)(2,1)S(1)} collective-permute-done((bf16[16,4096]{1,0:T(8,128)(2,1)S(1)}, bf16[16,4096]{1,0:T(8,128)(2,1)S(1)}, u32[]{:S(2)}, u32[]{:S(2)}) %collective-permute-start.6) | collective-permute-done | bytes 131104 | tf_op jit(solution)/shard_map/ppermute | solution.py:21
  41.7 1.7 %collective-permute-start.7 = (bf16[16,4096]{1,0:T(8,128)(2,1)S(1)}, bf16[16,4096]{1,0:T(8,128)(2,1)S(1)}, u32[]{:S(2)}, u32[]{:S(2)}) collective-permute-start(bf16[16,4096]{1,0:T(8,128)(2,1)S(1)} %add.50), channel_id=1, source_target_pairs={{0,2},{1,3},{2,0},{3,1},{4,6},{5,7},{6,4},{7,5},{8,10},{9,11},{10,... | collective-permute-start | bytes 393224 | tf_op jit(solution)/shard_map/ppermute | solution.py:21
  43.4 2.2 %collective-permute-start.8 = (bf16[16,4096]{1,0:T(8,128)(2,1)S(1)}, bf16[16,4096]{1,0:T(8,128)(2,1)S(1)}, u32[]{:S(2)}, u32[]{:S(2)}) collective-permute-start(bf16[16,4096]{1,0:T(8,128)(2,1)S(1)} %add.50), channel_id=1, source_target_pairs={{0,6},{1,7},{2,4},{3,5},{4,2},{5,3},{6,0},{7,1},{8,14},{9,15},{10,... | collective-permute-start | bytes 393224 | tf_op jit(solution)/shard_map/ppermute | solution.py:21
  46.9 5.5 %collective-permute-done.8 = bf16[16,4096]{1,0:T(8,128)(2,1)S(1)} collective-permute-done((bf16[16,4096]{1,0:T(8,128)(2,1)S(1)}, bf16[16,4096]{1,0:T(8,128)(2,1)S(1)}, u32[]{:S(2)}, u32[]{:S(2)}) %collective-permute-start.8) | collective-permute-done | bytes 131104 | tf_op jit(solution)/shard_map/ppermute | solution.py:21
  52.5 1.8 %collective-permute-start.10 = (bf16[16,4096]{1,0:T(8,128)(2,1)S(1)}, bf16[16,4096]{1,0:T(8,128)(2,1)S(1)}, u32[]{:S(2)}, u32[]{:S(2)}) collective-permute-start(bf16[16,4096]{1,0:T(8,128)(2,1)S(1)} %add_convert_fusion), channel_id=1, source_target_pairs={{0,1},{1,0},{2,3},{3,2},{4,5},{5,4},{6,7},{7,6},{8,9},{9,8},{10,11... | collective-permute-start | bytes 393224 | tf_op jit(solution)/shard_map/ppermute | solution.py:21
  54.3 3.2 %collective-permute-done.10 = bf16[16,4096]{1,0:T(8,128)(2,1)S(1)} collective-permute-done((bf16[16,4096]{1,0:T(8,128)(2,1)S(1)}, bf16[16,4096]{1,0:T(8,128)(2,1)S(1)}, u32[]{:S(2)}, u32[]{:S(2)}) %collective-permute-start.10) | collective-permute-done | bytes 131104 | tf_op jit(solution)/shard_map/ppermute | solution.py:21
  57.6 0.9 %reshape.47 = bf16[8,2,8192]{2,1,0:T(2,128)(2,1)} reshape(bf16[16,8192]{1,0:T(8,128)(2,1)S(1)} %pad_maximum_fusion) | data formatting | bytes 524288 | tf_op jit(solution)/shard_map/reshape | solution.py:307
  (19 shorter events, 2.1 us)
Async XLA Ops:
  2.4 1.4 %collective-permute-start = (bf16[2,256,128]{2,1,0:T(8,128)(2,1)S(1)}, bf16[2,256,128]{2,1,0:T(8,128)(2,1)S(1)}, u32[]{:S(2)}, u32[]{:S(2)}) collective-permute-start(bf16[2,256,128]{2,1,0:T(8,128)(2,1)S(1)} %get-tuple-element.44), channel_id=1, source_target_pairs={{0,8},{8,0},{16,24},{24,16},{32,40},{40,32},{48,56},{56,48},{64,72... | collective-permute-start | bytes 393224 | tf_op jit(solution)/shard_map/ppermute | solution.py:21
  3.9 5.6 %collective-permute-start.1 = (bf16[2,256,128]{2,1,0:T(8,128)(2,1)S(1)}, bf16[2,256,128]{2,1,0:T(8,128)(2,1)S(1)}, u32[]{:S(2)}, u32[]{:S(2)}) collective-permute-start(bf16[2,256,128]{2,1,0:T(8,128)(2,1)S(1)} %add.45), channel_id=1, source_target_pairs={{0,64},{8,72},{16,80},{24,88},{32,96},{40,104},{48,112},{56,120},{... | collective-permute-start | bytes 393224 | tf_op jit(solution)/shard_map/ppermute | solution.py:21
  9.5 6.3 %collective-permute-start.2 = (bf16[2,256,128]{2,1,0:T(8,128)(2,1)S(1)}, bf16[2,256,128]{2,1,0:T(8,128)(2,1)S(1)}, u32[]{:S(2)}, u32[]{:S(2)}) collective-permute-start(bf16[2,256,128]{2,1,0:T(8,128)(2,1)S(1)} %add.46), channel_id=1, source_target_pairs={{0,192},{8,200},{16,208},{24,216},{32,224},{40,232},{48,240},{56,2... | collective-permute-start | bytes 393224 | tf_op jit(solution)/shard_map/ppermute | solution.py:21
  15.9 8.0 %collective-permute-start.3 = (bf16[2,256,128]{2,1,0:T(8,128)(2,1)S(1)}, bf16[2,256,128]{2,1,0:T(8,128)(2,1)S(1)}, u32[]{:S(2)}, u32[]{:S(2)}) collective-permute-start(bf16[2,256,128]{2,1,0:T(8,128)(2,1)S(1)} %add.47), channel_id=1, source_target_pairs={{0,16},{8,24},{16,0},{24,8},{32,48},{40,56},{48,32},{56,40},{64,80... | collective-permute-start | bytes 393224 | tf_op jit(solution)/shard_map/ppermute | solution.py:21
  23.9 7.4 %collective-permute-start.4 = (bf16[2,256,128]{2,1,0:T(8,128)(2,1)S(1)}, bf16[2,256,128]{2,1,0:T(8,128)(2,1)S(1)}, u32[]{:S(2)}, u32[]{:S(2)}) collective-permute-start(bf16[2,256,128]{2,1,0:T(8,128)(2,1)S(1)} %add.48), channel_id=1, source_target_pairs={{0,48},{8,56},{16,32},{24,40},{32,16},{40,24},{48,0},{56,8},{64,11... | collective-permute-start | bytes 393224 | tf_op jit(solution)/shard_map/ppermute | solution.py:21
  31.4 1.4 %collective-permute-start.5 = (bf16[2,256,128]{2,1,0:T(8,128)(2,1)S(1)}, bf16[2,256,128]{2,1,0:T(8,128)(2,1)S(1)}, u32[]{:S(2)}, u32[]{:S(2)}) collective-permute-start(bf16[2,256,128]{2,1,0:T(8,128)(2,1)S(1)} %add.49.mine), channel_id=1, source_target_pairs={{0,8},{8,0},{16,24},{24,16},{32,40},{40,32},{48,56},{56,48},{64,72... | collective-permute-start | bytes 393224 | tf_op jit(solution)/shard_map/ppermute | solution.py:21
  32.8 13.5 %copy-start = (bf16[8,2,8192]{2,1,0:T(2,128)(2,1)S(1)}, bf16[8,2,8192]{2,1,0:T(2,128)(2,1)}, u32[]{:S(2)}) copy-start(bf16[8,2,8192]{2,1,0:T(2,128)(2,1)} %param.8) | copy-start | bytes 786436
  35.0 6.7 %collective-permute-start.6 = (bf16[16,4096]{1,0:T(8,128)(2,1)S(1)}, bf16[16,4096]{1,0:T(8,128)(2,1)S(1)}, u32[]{:S(2)}, u32[]{:S(2)}) collective-permute-start(bf16[16,4096]{1,0:T(8,128)(2,1)S(1)} %get-tuple-element.80), channel_id=1, source_target_pairs={{0,1},{1,0},{2,3},{3,2},{4,5},{5,4},{6,7},{7,6},{8,9},{9,8},{10,11... | collective-permute-start | bytes 393224 | tf_op jit(solution)/shard_map/ppermute | solution.py:21
  41.7 5.1 %collective-permute-start.7 = (bf16[16,4096]{1,0:T(8,128)(2,1)S(1)}, bf16[16,4096]{1,0:T(8,128)(2,1)S(1)}, u32[]{:S(2)}, u32[]{:S(2)}) collective-permute-start(bf16[16,4096]{1,0:T(8,128)(2,1)S(1)} %add.50), channel_id=1, source_target_pairs={{0,2},{1,3},{2,0},{3,1},{4,6},{5,7},{6,4},{7,5},{8,10},{9,11},{10,... | collective-permute-start | bytes 393224 | tf_op jit(solution)/shard_map/ppermute | solution.py:21
  43.4 9.0 %collective-permute-start.8 = (bf16[16,4096]{1,0:T(8,128)(2,1)S(1)}, bf16[16,4096]{1,0:T(8,128)(2,1)S(1)}, u32[]{:S(2)}, u32[]{:S(2)}) collective-permute-start(bf16[16,4096]{1,0:T(8,128)(2,1)S(1)} %add.50), channel_id=1, source_target_pairs={{0,6},{1,7},{2,4},{3,5},{4,2},{5,3},{6,0},{7,1},{8,14},{9,15},{10,... | collective-permute-start | bytes 393224 | tf_op jit(solution)/shard_map/ppermute | solution.py:21
  45.6 6.8 %collective-permute-start.9 = (bf16[16,4096]{1,0:T(8,128)(2,1)S(1)}, bf16[16,4096]{1,0:T(8,128)(2,1)S(1)}, u32[]{:S(2)}, u32[]{:S(2)}) collective-permute-start(bf16[16,4096]{1,0:T(8,128)(2,1)S(1)} %add.50), channel_id=1, source_target_pairs={{0,4},{1,5},{2,6},{3,7},{4,0},{5,1},{6,2},{7,3},{8,12},{9,13},{10,... | collective-permute-start | bytes 393224 | tf_op jit(solution)/shard_map/ppermute | solution.py:21
  52.5 5.1 %collective-permute-start.10 = (bf16[16,4096]{1,0:T(8,128)(2,1)S(1)}, bf16[16,4096]{1,0:T(8,128)(2,1)S(1)}, u32[]{:S(2)}, u32[]{:S(2)}) collective-permute-start(bf16[16,4096]{1,0:T(8,128)(2,1)S(1)} %add_convert_fusion), channel_id=1, source_target_pairs={{0,1},{1,0},{2,3},{3,2},{4,5},{5,4},{6,7},{7,6},{8,9},{9,8},{10,11... | collective-permute-start | bytes 393224 | tf_op jit(solution)/shard_map/ppermute | solution.py:21

commit v5 on v4

--- a/solution.py
+++ b/solution.py
@@ -49,7 +49,7 @@
         copies[p].wait()
     rows = lax.broadcasted_iota(jnp.int32, (16, 128), 0)
     for j in range(problems):
-        p = j ^ (place[1] * half)
+        p = j ^ (place[1] * half + place[3] * (half // 2))
         _, offset = start_of(p)
         mine = winner[p] == place[0]
         where = (keep if j < half else send, j % half)
@@ -150,7 +150,8 @@
     for half, ref in ((place[1], mine), (1 - place[1], other)):
         scores = lax.dot_general(queries, ref[0], NT, preferred_element_type=jnp.float32) * factor
         row = lax.broadcasted_iota(jnp.int32, scores.shape, 0) // per_row
-        owner = lax.broadcasted_iota(jnp.int32, scores.shape, 1) // BLOCK + half * (keys_here // BLOCK)
+        owner = lax.broadcasted_iota(jnp.int32, scores.shape, 1) // BLOCK
+        owner = (owner ^ (place[3] * (keys_here // BLOCK // 2))) + half * (keys_here // BLOCK)
         halves.append(jnp.where(row == owner, scores, -jnp.inf))
     top = jnp.maximum(jnp.max(halves[0], -1, keepdims=True), jnp.max(halves[1], -1, keepdims=True))
     top = jnp.maximum(peak, top)
@@ -189,7 +190,7 @@
     far_cache, far_lengths, winner, far_values, far_scales = (
         pltpu.with_memory_space_constraint(x, pltpu.HBM) for x in (kv_cache, lengths, winner, out_values, out_scales)
     )
-    place = jnp.stack([cand, cand % 2, tp % 2]).astype(jnp.int32)
+    place = jnp.stack([cand, cand % 2, tp % 2, (cand // 8 + cand // 16) % 2]).astype(jnp.int32)
     half = width // 2
     bf16, f32 = jnp.bfloat16, jnp.float32
 
@@ -240,26 +241,29 @@
     block = keep + exchange(send, "cand", 32, 1)
     queries = queries.reshape(problems, steps * heads, head_dim)
     fresh = new_kv.reshape(problems, 2 * steps, head_dim)
+    middle = block.shape[1] // 2
+    far_values, block = lax.optimization_barrier((far_values, block))
+    received, home_weights = lax.optimization_barrier(
+        (exchange(block[:, middle:], "cand", 32, 8), fetch_weights(far_values, True))
+    )
+    block = block[:, :middle] + received
     queries, fresh, lengths, block = lax.optimization_barrier((queries, fresh, lengths, block))
     received, part = lax.optimization_barrier(
-        (exchange(block, "cand", 32, 8), attend_old(queries, fresh, lengths, 0))
+        (exchange(block, "cand", 32, 24), attend_old(queries, fresh, lengths, 0))
     )
     block = block + received
     queries, fresh, lengths, block = lax.optimization_barrier((queries, fresh, lengths, block))
     received, rest = lax.optimization_barrier(
-        (exchange(block, "cand", 32, 24), attend_old(queries, fresh, lengths, problems // 2))
+        (exchange(block, "cand", 32, 2), attend_old(queries, fresh, lengths, problems // 2))
     )
     block = block + received
     far_values, block = lax.optimization_barrier((far_values, block))
     received, away_weights = lax.optimization_barrier(
-        (exchange(block, "cand", 32, 2), fetch_weights(far_values, False))
+        (exchange(block, "cand", 32, 6), fetch_weights(far_values, False))
     )
     block = block + received
-    far_values, block = lax.optimization_barrier((far_values, block))
-    received, home_weights = lax.optimization_barrier(
-        (exchange(block, "cand", 32, 6), fetch_weights(far_values, True))
-    )
-    block = block + received
+    received = exchange(block, "cand", 32, 8)
+    block = jnp.concatenate([block, received], axis=1)
     other = exchange(block, "cand", 32, 1)
 
     away_weights, home_weights = (

time: 58.8 us -> 58.6 us (level)
    ppermute x11 -> x12, waiting for transfers between devices: 19.9 us -> 19.5 us  [exchange(): return lax.ppermute(x, axis, [(i, i ^ bit) for i in range(size)])]
    ppermute x11 -> x12, starting transfers between devices: 20.5 us -> 20.6 us  [exchange(): return lax.ppermute(x, axis, [(i, i ^ bit) for i in range(size)])]
  transfers between devices with their start and end apart: 11 -> 12, of which waited for: 10 -> 10; matrix products, arithmetic and copies ran while one was open for 0% -> 0% of each run, Pallas kernels for 21% -> 21%
where the time goes in v5:
time: 58.6 us; the launch traced here: 58.3 us
  starting transfers between devices  20.6 us (35%)
  waiting for transfers between devices  19.5 us (33%)
  Pallas kernels  16.6 us (28%)
  local copies, waits for them, and re-layouts  1 us (2%)
    ppermute x12, starting transfers between devices, exchange(): return lax.ppermute(x, axis, [(i, i ^ bit) for i in range(size)])  20.6 us
    ppermute x12, waiting for transfers between devices, exchange(): return lax.ppermute(x, axis, [(i, i ^ bit) for i in range(size)])  19.5 us
    pallas_call x2, Pallas kernels, fetch_weights(): pl.pallas_call(functools.partial(fetch_kernel, own=own), out_shape=jax.Sh...  5.52 us
    pallas_call x2, Pallas kernels, attend_old(): pl.pallas_call(functools.partial(old_kernel, first=first, factor=factor),...  4.7 us
    pallas_call x1, Pallas kernels, local(): pl.pallas_call(extract_kernel, out_shape=(fork_shape, fork_shape), in_spe...  2.31 us
    pallas_call x1, Pallas kernels, local(): pl.pallas_call(functools.partial(fork_kernel, factor=factor), out_shape=(...  2.17 us
    pallas_call x1, Pallas kernels, local(): pl.pallas_call(project_kernel, out_shape=half_shape, in_specs=[SMEM, VMEM...  1.9 us
  transfers between devices with their start and end apart: 12, of which 10 were waited for; matrix products, arithmetic and copies ran while one was open for 0% of the time, Pallas kernels for 21%

profile of v5, /device:TPU:6, one launch (start us, length us, event | category | flops | bytes accessed | tf_op | source)
XLA Modules:
  0.0 58.3 jit_solution(9958044813218045231)
XLA Ops:
  0.1 2.3 %shard_map.82 = (bf16[2,256,128]{2,1,0:T(8,128)(2,1)S(1)}, bf16[2,256,128]{2,1,0:T(8,128)(2,1)S(1)}) custom-call(s32[4]{0:T(128)S(1)} %pad_add_fusion.place, s32[8]{0:T(128)} %lengths_in.3, s32[8]{0:T(128)} %winner_in.1, bf16[8,1,2,512,128]{4,3,2,1,0:T(8,128)(2,1)} %cache.5), custom_call_target="tpu_custom_call" | custom-call | bytes 524288 | tf_op jit(solution)/shard_map/pallas_call | solution.py:198
  2.5 1.3 %collective-permute-done = bf16[2,256,128]{2,1,0:T(8,128)(2,1)S(1)} collective-permute-done((bf16[2,256,128]{2,1,0:T(8,128)(2,1)S(1)}, bf16[2,256,128]{2,1,0:T(8,128)(2,1)S(1)}, u32[]{:S(2)}, u32[]{:S(2)}) %collective-permute-start) | collective-permute-done | bytes 131104 | tf_op jit(solution)/shard_map/ppermute | solution.py:21
  3.9 0.9 %collective-permute-start.1 = (bf16[2,128,128]{2,1,0:T(8,128)(2,1)S(1)}, bf16[2,128,128]{2,1,0:T(8,128)(2,1)S(1)}, u32[]{:S(2)}, u32[]{:S(2)}) collective-permute-start(bf16[2,128,128]{2,1,0:T(8,128)(2,1)S(1)} %slice.7), channel_id=1, source_target_pairs={{0,64},{8,72},{16,80},{24,88},{32,96},{40,104},{48,112},{56,120},{... | collective-permute-start | bytes 196616 | tf_op jit(solution)/shard_map/ppermute | solution.py:21
  4.8 2.8 %shard_map.83.weights = bf16[512,4096]{1,0:T(8,128)(2,1)S(1)} custom-call(s32[4]{0:T(128)S(1)} %pad_add_fusion.place, bf16[512,8192]{1,0:T(8,128)(2,1)} %far.1), custom_call_target="tpu_custom_call" | custom-call | bytes 8388608 | tf_op jit(solution)/shard_map/pallas_call | solution.py:232
  8.3 2.3 %collective-permute-start.2 = (bf16[2,128,128]{2,1,0:T(8,128)(2,1)S(1)}, bf16[2,128,128]{2,1,0:T(8,128)(2,1)S(1)}, u32[]{:S(2)}, u32[]{:S(2)}) collective-permute-start(bf16[2,128,128]{2,1,0:T(8,128)(2,1)S(1)} %slice_add_fusion), channel_id=1, source_target_pairs={{0,192},{8,200},{16,208},{24,216},{32,224},{40,232},{48,240},{56,2... | collective-permute-start | bytes 196616 | tf_op jit(solution)/shard_map/ppermute | solution.py:21
  10.6 2.3 %shard_map.84 = (f32[4,8,128]{2,1,0:T(8,128)S(1)}, f32[4,8,128]{2,1,0:T(8,128)S(1)}, f32[4,8,128]{2,1,0:T(8,128)S(1)}, bf16[4,8,128]{2,1,0:T(8,128)(2,1)S(1)}) custom-call(s32[8]{0:T(128)} %lengths_in.3, bf16[8,8,128]{2,1,0:T(8,128)(2,1)} %bitcast.22, bf16[8,4,128]{2,1,0:T(4,128)(2,1)} %bitcast.24, bf16[8,1,2,512,128]{4,3,2,1,0:T(8,128)(2,1)} %cache.5), custom_call_target="tpu_custom_call" | custom-call | flops 8388608 | bytes 1048576 | tf_op jit(solution)/shard_map/pallas_call | solution.py:217
  12.9 0.9 %collective-permute-done.2 = bf16[2,128,128]{2,1,0:T(8,128)(2,1)S(1)} collective-permute-done((bf16[2,128,128]{2,1,0:T(8,128)(2,1)S(1)}, bf16[2,128,128]{2,1,0:T(8,128)(2,1)S(1)}, u32[]{:S(2)}, u32[]{:S(2)}) %collective-permute-start.2) | collective-permute-done | bytes 65568 | tf_op jit(solution)/shard_map/ppermute | solution.py:21
  13.8 3.4 %collective-permute-start.3 = (bf16[2,128,128]{2,1,0:T(8,128)(2,1)S(1)}, bf16[2,128,128]{2,1,0:T(8,128)(2,1)S(1)}, u32[]{:S(2)}, u32[]{:S(2)}) collective-permute-start(bf16[2,128,128]{2,1,0:T(8,128)(2,1)S(1)} %add.57), channel_id=1, source_target_pairs={{0,16},{8,24},{16,0},{24,8},{32,48},{40,56},{48,32},{56,40},{64,80... | collective-permute-start | bytes 196616 | tf_op jit(solution)/shard_map/ppermute | solution.py:21
  17.2 2.3 %shard_map.85 = (f32[4,8,128]{2,1,0:T(8,128)S(1)}, f32[4,8,128]{2,1,0:T(8,128)S(1)}, f32[4,8,128]{2,1,0:T(8,128)S(1)}, bf16[4,8,128]{2,1,0:T(8,128)(2,1)S(1)}) custom-call(s32[8]{0:T(128)} %lengths_in.3, bf16[8,8,128]{2,1,0:T(8,128)(2,1)} %bitcast.23, bf16[8,4,128]{2,1,0:T(4,128)(2,1)} %bitcast.25, bf16[8,1,2,512,128]{4,3,2,1,0:T(8,128)(2,1)} %cache.5), custom_call_target="tpu_custom_call" | custom-call | flops 8388608 | bytes 1048576 | tf_op jit(solution)/shard_map/pallas_call | solution.py:217
  19.6 6.0 %collective-permute-start.4 = (bf16[2,128,128]{2,1,0:T(8,128)(2,1)S(1)}, bf16[2,128,128]{2,1,0:T(8,128)(2,1)S(1)}, u32[]{:S(2)}, u32[]{:S(2)}) collective-permute-start(bf16[2,128,128]{2,1,0:T(8,128)(2,1)S(1)} %add.58), channel_id=1, source_target_pairs={{0,48},{8,56},{16,32},{24,40},{32,16},{40,24},{48,0},{56,8},{64,11... | collective-permute-start | bytes 196616 | tf_op jit(solution)/shard_map/ppermute | solution.py:21
  25.6 2.8 %shard_map.86.refs_9_ = bf16[512,4096]{1,0:T(8,128)(2,1)S(1)} custom-call(s32[4]{0:T(128)S(1)} %pad_add_fusion.place, bf16[512,8192]{1,0:T(8,128)(2,1)} %far.1), custom_call_target="tpu_custom_call" | custom-call | bytes 8388608 | tf_op jit(solution)/shard_map/pallas_call | solution.py:232
  28.5 4.3 %collective-permute-done.5 = bf16[2,128,128]{2,1,0:T(8,128)(2,1)S(1)} collective-permute-done((bf16[2,128,128]{2,1,0:T(8,128)(2,1)S(1)}, bf16[2,128,128]{2,1,0:T(8,128)(2,1)S(1)}, u32[]{:S(2)}, u32[]{:S(2)}) %collective-permute-start.5) | collective-permute-done | bytes 65568 | tf_op jit(solution)/shard_map/ppermute | solution.py:21
  32.9 1.3 %collective-permute-done.6.other = bf16[2,256,128]{2,1,0:T(8,128)(2,1)S(1)} collective-permute-done((bf16[2,256,128]{2,1,0:T(8,128)(2,1)S(1)}, bf16[2,256,128]{2,1,0:T(8,128)(2,1)S(1)}, u32[]{:S(2)}, u32[]{:S(2)}) %collective-permute-start.6) | collective-permute-done | bytes 131104 | tf_op jit(solution)/shard_map/ppermute | solution.py:21
  34.2 2.2 %shard_map.87 = (f32[64,128]{1,0:T(8,128)S(1)}, bf16[16,4096]{1,0:T(8,128)(2,1)S(1)}) custom-call(s32[4]{0:T(128)S(1)} %pad_add_fusion.place, bf16[2,256,128]{2,1,0:T(8,128)(2,1)S(1)} %pad_maximum_fusion.1.mine, bf16[2,256,128]{2,1,0:T(8,128)(2,1)S(1)} %collective-permute-done.6.other, f32[32,128]{1,0:T(8,128)S(1)} %bitcast.14, f32[32,128]{1,0:T(8,128)S(1)} %bitcast.15, ...), custom_call_target="tpu_custom_call" | custom-call | flops 67108864 | bytes 4194304 | tf_op jit(solution)/shard_map/pallas_call | solution.py:275
  36.4 1.7 %collective-permute-start.7 = (bf16[16,4096]{1,0:T(8,128)(2,1)S(1)}, bf16[16,4096]{1,0:T(8,128)(2,1)S(1)}, u32[]{:S(2)}, u32[]{:S(2)}) collective-permute-start(bf16[16,4096]{1,0:T(8,128)(2,1)S(1)} %get-tuple-element.80), channel_id=1, source_target_pairs={{0,1},{1,0},{2,3},{3,2},{4,5},{5,4},{6,7},{7,6},{8,9},{9,8},{10,11... | collective-permute-start | bytes 393224 | tf_op jit(solution)/shard_map/ppermute | solution.py:21
  38.1 1.9 %shard_map.88 = bf16[16,4096]{1,0:T(8,128)(2,1)S(1)} custom-call(s32[4]{0:T(128)S(1)} %pad_add_fusion.place, f32[64,128]{1,0:T(8,128)S(1)} %get-tuple-element.78.attended, f32[4,64]{1,0:T(4,128)} %scales_in.1, bf16[512,4096]{1,0:T(8,128)(2,1)S(1)} %shard_map.83.weights), custom_call_target="tpu_custom_call" | custom-call | flops 67108864 | bytes 4194304 | tf_op jit(solution)/shard_map/pallas_call | solution.py:291
  40.0 2.0 %collective-permute-done.7 = bf16[16,4096]{1,0:T(8,128)(2,1)S(1)} collective-permute-done((bf16[16,4096]{1,0:T(8,128)(2,1)S(1)}, bf16[16,4096]{1,0:T(8,128)(2,1)S(1)}, u32[]{:S(2)}, u32[]{:S(2)}) %collective-permute-start.7) | collective-permute-done | bytes 131104 | tf_op jit(solution)/shard_map/ppermute | solution.py:21
  42.1 3.3 %collective-permute-start.10 = (bf16[16,4096]{1,0:T(8,128)(2,1)S(1)}, bf16[16,4096]{1,0:T(8,128)(2,1)S(1)}, u32[]{:S(2)}, u32[]{:S(2)}) collective-permute-start(bf16[16,4096]{1,0:T(8,128)(2,1)S(1)} %add.60), channel_id=1, source_target_pairs={{0,4},{1,5},{2,6},{3,7},{4,0},{5,1},{6,2},{7,3},{8,12},{9,13},{10,... | collective-permute-start | bytes 393224 | tf_op jit(solution)/shard_map/ppermute | solution.py:21
  45.4 0.7 %collective-permute-start.8 = (bf16[16,4096]{1,0:T(8,128)(2,1)S(1)}, bf16[16,4096]{1,0:T(8,128)(2,1)S(1)}, u32[]{:S(2)}, u32[]{:S(2)}) collective-permute-start(bf16[16,4096]{1,0:T(8,128)(2,1)S(1)} %add.60), channel_id=1, source_target_pairs={{0,2},{1,3},{2,0},{3,1},{4,6},{5,7},{6,4},{7,5},{8,10},{9,11},{10,... | collective-permute-start | bytes 393224 | tf_op jit(solution)/shard_map/ppermute | solution.py:21
  46.5 3.3 %collective-permute-done.10 = bf16[16,4096]{1,0:T(8,128)(2,1)S(1)} collective-permute-done((bf16[16,4096]{1,0:T(8,128)(2,1)S(1)}, bf16[16,4096]{1,0:T(8,128)(2,1)S(1)}, u32[]{:S(2)}, u32[]{:S(2)}) %collective-permute-start.10) | collective-permute-done | bytes 131104 | tf_op jit(solution)/shard_map/ppermute | solution.py:21
  49.8 1.8 %collective-permute-done.8 = bf16[16,4096]{1,0:T(8,128)(2,1)S(1)} collective-permute-done((bf16[16,4096]{1,0:T(8,128)(2,1)S(1)}, bf16[16,4096]{1,0:T(8,128)(2,1)S(1)}, u32[]{:S(2)}, u32[]{:S(2)}) %collective-permute-start.8) | collective-permute-done | bytes 131104 | tf_op jit(solution)/shard_map/ppermute | solution.py:21
  52.3 1.7 %collective-permute-start.11 = (bf16[16,4096]{1,0:T(8,128)(2,1)S(1)}, bf16[16,4096]{1,0:T(8,128)(2,1)S(1)}, u32[]{:S(2)}, u32[]{:S(2)}) collective-permute-start(bf16[16,4096]{1,0:T(8,128)(2,1)S(1)} %add_convert_fusion), channel_id=1, source_target_pairs={{0,1},{1,0},{2,3},{3,2},{4,5},{5,4},{6,7},{7,6},{8,9},{9,8},{10,11... | collective-permute-start | bytes 393224 | tf_op jit(solution)/shard_map/ppermute | solution.py:21
  54.0 3.3 %collective-permute-done.11 = bf16[16,4096]{1,0:T(8,128)(2,1)S(1)} collective-permute-done((bf16[16,4096]{1,0:T(8,128)(2,1)S(1)}, bf16[16,4096]{1,0:T(8,128)(2,1)S(1)}, u32[]{:S(2)}, u32[]{:S(2)}) %collective-permute-start.11) | collective-permute-done | bytes 131104 | tf_op jit(solution)/shard_map/ppermute | solution.py:21
  57.4 0.9 %reshape.47 = bf16[8,2,8192]{2,1,0:T(2,128)(2,1)} reshape(bf16[16,8192]{1,0:T(8,128)(2,1)S(1)} %pad_maximum_fusion) | data formatting | bytes 524288 | tf_op jit(solution)/shard_map/reshape | solution.py:311
  (23 shorter events, 2.5 us)
Async XLA Ops:
  2.4 1.4 %collective-permute-start = (bf16[2,256,128]{2,1,0:T(8,128)(2,1)S(1)}, bf16[2,256,128]{2,1,0:T(8,128)(2,1)S(1)}, u32[]{:S(2)}, u32[]{:S(2)}) collective-permute-start(bf16[2,256,128]{2,1,0:T(8,128)(2,1)S(1)} %get-tuple-element.44), channel_id=1, source_target_pairs={{0,8},{8,0},{16,24},{24,16},{32,40},{40,32},{48,56},{56,48},{64,72... | collective-permute-start | bytes 393224 | tf_op jit(solution)/shard_map/ppermute | solution.py:21
  3.9 4.4 %collective-permute-start.1 = (bf16[2,128,128]{2,1,0:T(8,128)(2,1)S(1)}, bf16[2,128,128]{2,1,0:T(8,128)(2,1)S(1)}, u32[]{:S(2)}, u32[]{:S(2)}) collective-permute-start(bf16[2,128,128]{2,1,0:T(8,128)(2,1)S(1)} %slice.7), channel_id=1, source_target_pairs={{0,64},{8,72},{16,80},{24,88},{32,96},{40,104},{48,112},{56,120},{... | collective-permute-start | bytes 196616 | tf_op jit(solution)/shard_map/ppermute | solution.py:21
  8.3 5.6 %collective-permute-start.2 = (bf16[2,128,128]{2,1,0:T(8,128)(2,1)S(1)}, bf16[2,128,128]{2,1,0:T(8,128)(2,1)S(1)}, u32[]{:S(2)}, u32[]{:S(2)}) collective-permute-start(bf16[2,128,128]{2,1,0:T(8,128)(2,1)S(1)} %slice_add_fusion), channel_id=1, source_target_pairs={{0,192},{8,200},{16,208},{24,216},{32,224},{40,232},{48,240},{56,2... | collective-permute-start | bytes 196616 | tf_op jit(solution)/shard_map/ppermute | solution.py:21
  13.8 5.7 %collective-permute-start.3 = (bf16[2,128,128]{2,1,0:T(8,128)(2,1)S(1)}, bf16[2,128,128]{2,1,0:T(8,128)(2,1)S(1)}, u32[]{:S(2)}, u32[]{:S(2)}) collective-permute-start(bf16[2,128,128]{2,1,0:T(8,128)(2,1)S(1)} %add.57), channel_id=1, source_target_pairs={{0,16},{8,24},{16,0},{24,8},{32,48},{40,56},{48,32},{56,40},{64,80... | collective-permute-start | bytes 196616 | tf_op jit(solution)/shard_map/ppermute | solution.py:21
  19.6 8.8 %collective-permute-start.4 = (bf16[2,128,128]{2,1,0:T(8,128)(2,1)S(1)}, bf16[2,128,128]{2,1,0:T(8,128)(2,1)S(1)}, u32[]{:S(2)}, u32[]{:S(2)}) collective-permute-start(bf16[2,128,128]{2,1,0:T(8,128)(2,1)S(1)} %add.58), channel_id=1, source_target_pairs={{0,48},{8,56},{16,32},{24,40},{32,16},{40,24},{48,0},{56,8},{64,11... | collective-permute-start | bytes 196616 | tf_op jit(solution)/shard_map/ppermute | solution.py:21
  28.4 4.4 %collective-permute-start.5 = (bf16[2,128,128]{2,1,0:T(8,128)(2,1)S(1)}, bf16[2,128,128]{2,1,0:T(8,128)(2,1)S(1)}, u32[]{:S(2)}, u32[]{:S(2)}) collective-permute-start(bf16[2,128,128]{2,1,0:T(8,128)(2,1)S(1)} %add.59), channel_id=1, source_target_pairs={{0,64},{8,72},{16,80},{24,88},{32,96},{40,104},{48,112},{56,120},{... | collective-permute-start | bytes 196616 | tf_op jit(solution)/shard_map/ppermute | solution.py:21
  32.8 1.4 %collective-permute-start.6 = (bf16[2,256,128]{2,1,0:T(8,128)(2,1)S(1)}, bf16[2,256,128]{2,1,0:T(8,128)(2,1)S(1)}, u32[]{:S(2)}, u32[]{:S(2)}) collective-permute-start(bf16[2,256,128]{2,1,0:T(8,128)(2,1)S(1)} %pad_maximum_fusion.1.mine), channel_id=1, source_target_pairs={{0,8},{8,0},{16,24},{24,16},{32,40},{40,32},{48,56},{56,48},{64,72... | collective-permute-start | bytes 393224 | tf_op jit(solution)/shard_map/ppermute | solution.py:21
  34.2 12.2 %copy-start = (bf16[8,2,8192]{2,1,0:T(2,128)(2,1)S(1)}, bf16[8,2,8192]{2,1,0:T(2,128)(2,1)}, u32[]{:S(2)}) copy-start(bf16[8,2,8192]{2,1,0:T(2,128)(2,1)} %param.8) | copy-start | bytes 786436
  36.4 5.6 %collective-permute-start.7 = (bf16[16,4096]{1,0:T(8,128)(2,1)S(1)}, bf16[16,4096]{1,0:T(8,128)(2,1)S(1)}, u32[]{:S(2)}, u32[]{:S(2)}) collective-permute-start(bf16[16,4096]{1,0:T(8,128)(2,1)S(1)} %get-tuple-element.80), channel_id=1, source_target_pairs={{0,1},{1,0},{2,3},{3,2},{4,5},{5,4},{6,7},{7,6},{8,9},{9,8},{10,11... | collective-permute-start | bytes 393224 | tf_op jit(solution)/shard_map/ppermute | solution.py:21
  42.1 7.7 %collective-permute-start.10 = (bf16[16,4096]{1,0:T(8,128)(2,1)S(1)}, bf16[16,4096]{1,0:T(8,128)(2,1)S(1)}, u32[]{:S(2)}, u32[]{:S(2)}) collective-permute-start(bf16[16,4096]{1,0:T(8,128)(2,1)S(1)} %add.60), channel_id=1, source_target_pairs={{0,4},{1,5},{2,6},{3,7},{4,0},{5,1},{6,2},{7,3},{8,12},{9,13},{10,... | collective-permute-start | bytes 393224 | tf_op jit(solution)/shard_map/ppermute | solution.py:21
  45.4 6.2 %collective-permute-start.8 = (bf16[16,4096]{1,0:T(8,128)(2,1)S(1)}, bf16[16,4096]{1,0:T(8,128)(2,1)S(1)}, u32[]{:S(2)}, u32[]{:S(2)}) collective-permute-start(bf16[16,4096]{1,0:T(8,128)(2,1)S(1)} %add.60), channel_id=1, source_target_pairs={{0,2},{1,3},{2,0},{3,1},{4,6},{5,7},{6,4},{7,5},{8,10},{9,11},{10,... | collective-permute-start | bytes 393224 | tf_op jit(solution)/shard_map/ppermute | solution.py:21
  46.0 6.2 %collective-permute-start.9 = (bf16[16,4096]{1,0:T(8,128)(2,1)S(1)}, bf16[16,4096]{1,0:T(8,128)(2,1)S(1)}, u32[]{:S(2)}, u32[]{:S(2)}) collective-permute-start(bf16[16,4096]{1,0:T(8,128)(2,1)S(1)} %add.60), channel_id=1, source_target_pairs={{0,6},{1,7},{2,4},{3,5},{4,2},{5,3},{6,0},{7,1},{8,14},{9,15},{10,... | collective-permute-start | bytes 393224 | tf_op jit(solution)/shard_map/ppermute | solution.py:21
  52.3 5.1 %collective-permute-start.11 = (bf16[16,4096]{1,0:T(8,128)(2,1)S(1)}, bf16[16,4096]{1,0:T(8,128)(2,1)S(1)}, u32[]{:S(2)}, u32[]{:S(2)}) collective-permute-start(bf16[16,4096]{1,0:T(8,128)(2,1)S(1)} %add_convert_fusion), channel_id=1, source_target_pairs={{0,1},{1,0},{2,3},{3,2},{4,5},{5,4},{6,7},{7,6},{8,9},{9,8},{10,11... | collective-permute-start | bytes 393224 | tf_op jit(solution)/shard_map/ppermute | solution.py:21

commit v6 on v5

--- a/solution.py
+++ b/solution.py
@@ -38,15 +38,24 @@
         start = jnp.minimum((first // 16) * 16, cache.shape[3] - WINDOW)
         return pl.multiple_of(start, 16), first - start
 
-    copies = []
+    def window_copy(p):
+        start, _ = start_of(p)
+        return pltpu.make_async_copy(
+            cache.at[p, 0, :, pl.ds(start, WINDOW), :], window.at[p], sems.at[p]
+        )
+
     for p in range(problems):
-        start, _ = start_of(p)
-        copies.append(
-            pltpu.make_async_copy(cache.at[p, 0, :, pl.ds(start, WINDOW), :], window.at[p], sems.at[p])
-        )
-        copies[-1].start()
+
+        @pl.when(winner[p] == place[0])
+        def _(p=p):
+            window_copy(p).start()
+
     for p in range(problems):
-        copies[p].wait()
+
+        @pl.when(winner[p] == place[0])
+        def _(p=p):
+            window_copy(p).wait()
+
     rows = lax.broadcasted_iota(jnp.int32, (16, 128), 0)
     for j in range(problems):
         p = j ^ (place[1] * half + place[3] * (half // 2))

time: 58.6 us -> 58.2 us (level)
  starting transfers between devices: 20.6 us -> 22 us
  Pallas kernels: 16.6 us -> 15.8 us
  waiting for transfers between devices: 19.5 us -> 18.9 us
    ppermute x12, starting transfers between devices: 20.6 us -> 22 us  [exchange(): return lax.ppermute(x, axis, [(i, i ^ bit) for i in range(size)])]
    pallas_call x1, Pallas kernels: 2.31 us -> 1.48 us  [local(): pl.pallas_call(extract_kernel, out_shape=(fork_shape, fork_shape), in_spe...]
    ppermute x12, waiting for transfers between devices: 19.5 us -> 18.9 us  [exchange(): return lax.ppermute(x, axis, [(i, i ^ bit) for i in range(size)])]
where the time goes in v6:
time: 58.2 us
  starting transfers between devices  22 us (38%)
  waiting for transfers between devices  18.9 us (32%)
  Pallas kernels  15.8 us (27%)
  local copies, waits for them, and re-layouts  1 us (2%)
    ppermute x12, starting transfers between devices, exchange(): return lax.ppermute(x, axis, [(i, i ^ bit) for i in range(size)])  22 us
    ppermute x12, waiting for transfers between devices, exchange(): return lax.ppermute(x, axis, [(i, i ^ bit) for i in range(size)])  18.9 us
    pallas_call x2, Pallas kernels, fetch_weights(): pl.pallas_call(functools.partial(fetch_kernel, own=own), out_shape=jax.Sh...  5.52 us
    pallas_call x2, Pallas kernels, attend_old(): pl.pallas_call(functools.partial(old_kernel, first=first, factor=factor),...  4.7 us
    pallas_call x1, Pallas kernels, local(): pl.pallas_call(functools.partial(fork_kernel, factor=factor), out_shape=(...  2.17 us
    pallas_call x1, Pallas kernels, local(): pl.pallas_call(project_kernel, out_shape=half_shape, in_specs=[SMEM, VMEM...  1.9 us
    pallas_call x1, Pallas kernels, local(): pl.pallas_call(extract_kernel, out_shape=(fork_shape, fork_shape), in_spe...  1.48 us
  transfers between devices with their start and end apart: 12, of which 10 were waited for; matrix products, arithmetic and copies ran while one was open for 0% of the time, Pallas kernels for 21%

profile of v6, /device:TPU:6, one launch (start us, length us, event | category | flops | bytes accessed | tf_op | source)
XLA Modules:
  0.0 58.2 jit_solution(5433865349901214477)
XLA Ops:
  0.1 1.5 %shard_map.82 = (bf16[2,256,128]{2,1,0:T(8,128)(2,1)S(1)}, bf16[2,256,128]{2,1,0:T(8,128)(2,1)S(1)}) custom-call(s32[4]{0:T(128)S(1)} %pad_add_fusion.place, s32[8]{0:T(128)} %lengths_in.3, s32[8]{0:T(128)} %winner_in.1, bf16[8,1,2,512,128]{4,3,2,1,0:T(8,128)(2,1)} %cache.5), custom_call_target="tpu_custom_call" | custom-call | bytes 524288 | tf_op jit(solution)/shard_map/pallas_call | solution.py:207
  1.7 1.3 %collective-permute-done = bf16[2,256,128]{2,1,0:T(8,128)(2,1)S(1)} collective-permute-done((bf16[2,256,128]{2,1,0:T(8,128)(2,1)S(1)}, bf16[2,256,128]{2,1,0:T(8,128)(2,1)S(1)}, u32[]{:S(2)}, u32[]{:S(2)}) %collective-permute-start) | collective-permute-done | bytes 131104 | tf_op jit(solution)/shard_map/ppermute | solution.py:21
  3.1 0.9 %collective-permute-start.1 = (bf16[2,128,128]{2,1,0:T(8,128)(2,1)S(1)}, bf16[2,128,128]{2,1,0:T(8,128)(2,1)S(1)}, u32[]{:S(2)}, u32[]{:S(2)}) collective-permute-start(bf16[2,128,128]{2,1,0:T(8,128)(2,1)S(1)} %slice.7), channel_id=1, source_target_pairs={{0,64},{8,72},{16,80},{24,88},{32,96},{40,104},{48,112},{56,120},{... | collective-permute-start | bytes 196616 | tf_op jit(solution)/shard_map/ppermute | solution.py:21
  4.0 2.8 %shard_map.83.weights = bf16[512,4096]{1,0:T(8,128)(2,1)S(1)} custom-call(s32[4]{0:T(128)S(1)} %pad_add_fusion.place, bf16[512,8192]{1,0:T(8,128)(2,1)} %far.1), custom_call_target="tpu_custom_call" | custom-call | bytes 8388608 | tf_op jit(solution)/shard_map/pallas_call | solution.py:241
  7.4 3.0 %collective-permute-start.2 = (bf16[2,128,128]{2,1,0:T(8,128)(2,1)S(1)}, bf16[2,128,128]{2,1,0:T(8,128)(2,1)S(1)}, u32[]{:S(2)}, u32[]{:S(2)}) collective-permute-start(bf16[2,128,128]{2,1,0:T(8,128)(2,1)S(1)} %slice_add_fusion), channel_id=1, source_target_pairs={{0,192},{8,200},{16,208},{24,216},{32,224},{40,232},{48,240},{56,2... | collective-permute-start | bytes 196616 | tf_op jit(solution)/shard_map/ppermute | solution.py:21
  10.4 2.3 %shard_map.84 = (f32[4,8,128]{2,1,0:T(8,128)S(1)}, f32[4,8,128]{2,1,0:T(8,128)S(1)}, f32[4,8,128]{2,1,0:T(8,128)S(1)}, bf16[4,8,128]{2,1,0:T(8,128)(2,1)S(1)}) custom-call(s32[8]{0:T(128)} %lengths_in.3, bf16[8,8,128]{2,1,0:T(8,128)(2,1)} %bitcast.22, bf16[8,4,128]{2,1,0:T(4,128)(2,1)} %bitcast.24, bf16[8,1,2,512,128]{4,3,2,1,0:T(8,128)(2,1)} %cache.5), custom_call_target="tpu_custom_call" | custom-call | flops 8388608 | bytes 1048576 | tf_op jit(solution)/shard_map/pallas_call | solution.py:226
  13.0 3.7 %collective-permute-start.3 = (bf16[2,128,128]{2,1,0:T(8,128)(2,1)S(1)}, bf16[2,128,128]{2,1,0:T(8,128)(2,1)S(1)}, u32[]{:S(2)}, u32[]{:S(2)}) collective-permute-start(bf16[2,128,128]{2,1,0:T(8,128)(2,1)S(1)} %add.57), channel_id=1, source_target_pairs={{0,16},{8,24},{16,0},{24,8},{32,48},{40,56},{48,32},{56,40},{64,80... | collective-permute-start | bytes 196616 | tf_op jit(solution)/shard_map/ppermute | solution.py:21
  16.7 2.3 %shard_map.85 = (f32[4,8,128]{2,1,0:T(8,128)S(1)}, f32[4,8,128]{2,1,0:T(8,128)S(1)}, f32[4,8,128]{2,1,0:T(8,128)S(1)}, bf16[4,8,128]{2,1,0:T(8,128)(2,1)S(1)}) custom-call(s32[8]{0:T(128)} %lengths_in.3, bf16[8,8,128]{2,1,0:T(8,128)(2,1)} %bitcast.23, bf16[8,4,128]{2,1,0:T(4,128)(2,1)} %bitcast.25, bf16[8,1,2,512,128]{4,3,2,1,0:T(8,128)(2,1)} %cache.5), custom_call_target="tpu_custom_call" | custom-call | flops 8388608 | bytes 1048576 | tf_op jit(solution)/shard_map/pallas_call | solution.py:226
  19.1 6.4 %collective-permute-start.4 = (bf16[2,128,128]{2,1,0:T(8,128)(2,1)S(1)}, bf16[2,128,128]{2,1,0:T(8,128)(2,1)S(1)}, u32[]{:S(2)}, u32[]{:S(2)}) collective-permute-start(bf16[2,128,128]{2,1,0:T(8,128)(2,1)S(1)} %add.58), channel_id=1, source_target_pairs={{0,48},{8,56},{16,32},{24,40},{32,16},{40,24},{48,0},{56,8},{64,11... | collective-permute-start | bytes 196616 | tf_op jit(solution)/shard_map/ppermute | solution.py:21
  25.5 2.8 %shard_map.86.refs_9_ = bf16[512,4096]{1,0:T(8,128)(2,1)S(1)} custom-call(s32[4]{0:T(128)S(1)} %pad_add_fusion.place, bf16[512,8192]{1,0:T(8,128)(2,1)} %far.1), custom_call_target="tpu_custom_call" | custom-call | bytes 8388608 | tf_op jit(solution)/shard_map/pallas_call | solution.py:241
  28.4 4.3 %collective-permute-done.5 = bf16[2,128,128]{2,1,0:T(8,128)(2,1)S(1)} collective-permute-done((bf16[2,128,128]{2,1,0:T(8,128)(2,1)S(1)}, bf16[2,128,128]{2,1,0:T(8,128)(2,1)S(1)}, u32[]{:S(2)}, u32[]{:S(2)}) %collective-permute-start.5) | collective-permute-done | bytes 65568 | tf_op jit(solution)/shard_map/ppermute | solution.py:21
  32.8 1.3 %collective-permute-done.6.other = bf16[2,256,128]{2,1,0:T(8,128)(2,1)S(1)} collective-permute-done((bf16[2,256,128]{2,1,0:T(8,128)(2,1)S(1)}, bf16[2,256,128]{2,1,0:T(8,128)(2,1)S(1)}, u32[]{:S(2)}, u32[]{:S(2)}) %collective-permute-start.6) | collective-permute-done | bytes 131104 | tf_op jit(solution)/shard_map/ppermute | solution.py:21
  34.1 2.2 %shard_map.87 = (f32[64,128]{1,0:T(8,128)S(1)}, bf16[16,4096]{1,0:T(8,128)(2,1)S(1)}) custom-call(s32[4]{0:T(128)S(1)} %pad_add_fusion.place, bf16[2,256,128]{2,1,0:T(8,128)(2,1)S(1)} %pad_maximum_fusion.1.mine, bf16[2,256,128]{2,1,0:T(8,128)(2,1)S(1)} %collective-permute-done.6.other, f32[32,128]{1,0:T(8,128)S(1)} %bitcast.14, f32[32,128]{1,0:T(8,128)S(1)} %bitcast.15, ...), custom_call_target="tpu_custom_call" | custom-call | flops 67108864 | bytes 4194304 | tf_op jit(solution)/shard_map/pallas_call | solution.py:284
  36.3 1.7 %collective-permute-start.7 = (bf16[16,4096]{1,0:T(8,128)(2,1)S(1)}, bf16[16,4096]{1,0:T(8,128)(2,1)S(1)}, u32[]{:S(2)}, u32[]{:S(2)}) collective-permute-start(bf16[16,4096]{1,0:T(8,128)(2,1)S(1)} %get-tuple-element.80), channel_id=1, source_target_pairs={{0,1},{1,0},{2,3},{3,2},{4,5},{5,4},{6,7},{7,6},{8,9},{9,8},{10,11... | collective-permute-start | bytes 393224 | tf_op jit(solution)/shard_map/ppermute | solution.py:21
  38.0 1.9 %shard_map.88 = bf16[16,4096]{1,0:T(8,128)(2,1)S(1)} custom-call(s32[4]{0:T(128)S(1)} %pad_add_fusion.place, f32[64,128]{1,0:T(8,128)S(1)} %get-tuple-element.78.attended, f32[4,64]{1,0:T(4,128)} %scales_in.1, bf16[512,4096]{1,0:T(8,128)(2,1)S(1)} %shard_map.83.weights), custom_call_target="tpu_custom_call" | custom-call | flops 67108864 | bytes 4194304 | tf_op jit(solution)/shard_map/pallas_call | solution.py:300
  39.9 2.0 %collective-permute-done.7 = bf16[16,4096]{1,0:T(8,128)(2,1)S(1)} collective-permute-done((bf16[16,4096]{1,0:T(8,128)(2,1)S(1)}, bf16[16,4096]{1,0:T(8,128)(2,1)S(1)}, u32[]{:S(2)}, u32[]{:S(2)}) %collective-permute-start.7) | collective-permute-done | bytes 131104 | tf_op jit(solution)/shard_map/ppermute | solution.py:21
  41.9 3.3 %collective-permute-start.10 = (bf16[16,4096]{1,0:T(8,128)(2,1)S(1)}, bf16[16,4096]{1,0:T(8,128)(2,1)S(1)}, u32[]{:S(2)}, u32[]{:S(2)}) collective-permute-start(bf16[16,4096]{1,0:T(8,128)(2,1)S(1)} %add.60), channel_id=1, source_target_pairs={{0,4},{1,5},{2,6},{3,7},{4,0},{5,1},{6,2},{7,3},{8,12},{9,13},{10,... | collective-permute-start | bytes 393224 | tf_op jit(solution)/shard_map/ppermute | solution.py:21
  45.2 0.7 %collective-permute-start.8 = (bf16[16,4096]{1,0:T(8,128)(2,1)S(1)}, bf16[16,4096]{1,0:T(8,128)(2,1)S(1)}, u32[]{:S(2)}, u32[]{:S(2)}) collective-permute-start(bf16[16,4096]{1,0:T(8,128)(2,1)S(1)} %add.60), channel_id=1, source_target_pairs={{0,2},{1,3},{2,0},{3,1},{4,6},{5,7},{6,4},{7,5},{8,10},{9,11},{10,... | collective-permute-start | bytes 393224 | tf_op jit(solution)/shard_map/ppermute | solution.py:21
  46.4 3.3 %collective-permute-done.10 = bf16[16,4096]{1,0:T(8,128)(2,1)S(1)} collective-permute-done((bf16[16,4096]{1,0:T(8,128)(2,1)S(1)}, bf16[16,4096]{1,0:T(8,128)(2,1)S(1)}, u32[]{:S(2)}, u32[]{:S(2)}) %collective-permute-start.10) | collective-permute-done | bytes 131104 | tf_op jit(solution)/shard_map/ppermute | solution.py:21
  49.7 1.8 %collective-permute-done.8 = bf16[16,4096]{1,0:T(8,128)(2,1)S(1)} collective-permute-done((bf16[16,4096]{1,0:T(8,128)(2,1)S(1)}, bf16[16,4096]{1,0:T(8,128)(2,1)S(1)}, u32[]{:S(2)}, u32[]{:S(2)}) %collective-permute-start.8) | collective-permute-done | bytes 131104 | tf_op jit(solution)/shard_map/ppermute | solution.py:21
  51.4 0.7 %collective-permute-done.9 = bf16[16,4096]{1,0:T(8,128)(2,1)S(1)} collective-permute-done((bf16[16,4096]{1,0:T(8,128)(2,1)S(1)}, bf16[16,4096]{1,0:T(8,128)(2,1)S(1)}, u32[]{:S(2)}, u32[]{:S(2)}) %collective-permute-start.9) | collective-permute-done | bytes 131104 | tf_op jit(solution)/shard_map/ppermute | solution.py:21
  52.2 1.7 %collective-permute-start.11 = (bf16[16,4096]{1,0:T(8,128)(2,1)S(1)}, bf16[16,4096]{1,0:T(8,128)(2,1)S(1)}, u32[]{:S(2)}, u32[]{:S(2)}) collective-permute-start(bf16[16,4096]{1,0:T(8,128)(2,1)S(1)} %add_convert_fusion), channel_id=1, source_target_pairs={{0,1},{1,0},{2,3},{3,2},{4,5},{5,4},{6,7},{7,6},{8,9},{9,8},{10,11... | collective-permute-start | bytes 393224 | tf_op jit(solution)/shard_map/ppermute | solution.py:21
  53.9 3.3 %collective-permute-done.11 = bf16[16,4096]{1,0:T(8,128)(2,1)S(1)} collective-permute-done((bf16[16,4096]{1,0:T(8,128)(2,1)S(1)}, bf16[16,4096]{1,0:T(8,128)(2,1)S(1)}, u32[]{:S(2)}, u32[]{:S(2)}) %collective-permute-start.11) | collective-permute-done | bytes 131104 | tf_op jit(solution)/shard_map/ppermute | solution.py:21
  57.3 0.9 %reshape.47 = bf16[8,2,8192]{2,1,0:T(2,128)(2,1)} reshape(bf16[16,8192]{1,0:T(8,128)(2,1)S(1)} %pad_maximum_fusion) | data formatting | bytes 524288 | tf_op jit(solution)/shard_map/reshape | solution.py:320
  (23 shorter events, 2.0 us)
Async XLA Ops:
  1.6 1.4 %collective-permute-start = (bf16[2,256,128]{2,1,0:T(8,128)(2,1)S(1)}, bf16[2,256,128]{2,1,0:T(8,128)(2,1)S(1)}, u32[]{:S(2)}, u32[]{:S(2)}) collective-permute-start(bf16[2,256,128]{2,1,0:T(8,128)(2,1)S(1)} %get-tuple-element.44), channel_id=1, source_target_pairs={{0,8},{8,0},{16,24},{24,16},{32,40},{40,32},{48,56},{56,48},{64,72... | collective-permute-start | bytes 393224 | tf_op jit(solution)/shard_map/ppermute | solution.py:21
  3.1 4.4 %collective-permute-start.1 = (bf16[2,128,128]{2,1,0:T(8,128)(2,1)S(1)}, bf16[2,128,128]{2,1,0:T(8,128)(2,1)S(1)}, u32[]{:S(2)}, u32[]{:S(2)}) collective-permute-start(bf16[2,128,128]{2,1,0:T(8,128)(2,1)S(1)} %slice.7), channel_id=1, source_target_pairs={{0,64},{8,72},{16,80},{24,88},{32,96},{40,104},{48,112},{56,120},{... | collective-permute-start | bytes 196616 | tf_op jit(solution)/shard_map/ppermute | solution.py:21
  7.4 5.6 %collective-permute-start.2 = (bf16[2,128,128]{2,1,0:T(8,128)(2,1)S(1)}, bf16[2,128,128]{2,1,0:T(8,128)(2,1)S(1)}, u32[]{:S(2)}, u32[]{:S(2)}) collective-permute-start(bf16[2,128,128]{2,1,0:T(8,128)(2,1)S(1)} %slice_add_fusion), channel_id=1, source_target_pairs={{0,192},{8,200},{16,208},{24,216},{32,224},{40,232},{48,240},{56,2... | collective-permute-start | bytes 196616 | tf_op jit(solution)/shard_map/ppermute | solution.py:21
  13.0 6.0 %collective-permute-start.3 = (bf16[2,128,128]{2,1,0:T(8,128)(2,1)S(1)}, bf16[2,128,128]{2,1,0:T(8,128)(2,1)S(1)}, u32[]{:S(2)}, u32[]{:S(2)}) collective-permute-start(bf16[2,128,128]{2,1,0:T(8,128)(2,1)S(1)} %add.57), channel_id=1, source_target_pairs={{0,16},{8,24},{16,0},{24,8},{32,48},{40,56},{48,32},{56,40},{64,80... | collective-permute-start | bytes 196616 | tf_op jit(solution)/shard_map/ppermute | solution.py:21
  19.1 9.2 %collective-permute-start.4 = (bf16[2,128,128]{2,1,0:T(8,128)(2,1)S(1)}, bf16[2,128,128]{2,1,0:T(8,128)(2,1)S(1)}, u32[]{:S(2)}, u32[]{:S(2)}) collective-permute-start(bf16[2,128,128]{2,1,0:T(8,128)(2,1)S(1)} %add.58), channel_id=1, source_target_pairs={{0,48},{8,56},{16,32},{24,40},{32,16},{40,24},{48,0},{56,8},{64,11... | collective-permute-start | bytes 196616 | tf_op jit(solution)/shard_map/ppermute | solution.py:21
  28.3 4.4 %collective-permute-start.5 = (bf16[2,128,128]{2,1,0:T(8,128)(2,1)S(1)}, bf16[2,128,128]{2,1,0:T(8,128)(2,1)S(1)}, u32[]{:S(2)}, u32[]{:S(2)}) collective-permute-start(bf16[2,128,128]{2,1,0:T(8,128)(2,1)S(1)} %add.59), channel_id=1, source_target_pairs={{0,64},{8,72},{16,80},{24,88},{32,96},{40,104},{48,112},{56,120},{... | collective-permute-start | bytes 196616 | tf_op jit(solution)/shard_map/ppermute | solution.py:21
  32.7 1.4 %collective-permute-start.6 = (bf16[2,256,128]{2,1,0:T(8,128)(2,1)S(1)}, bf16[2,256,128]{2,1,0:T(8,128)(2,1)S(1)}, u32[]{:S(2)}, u32[]{:S(2)}) collective-permute-start(bf16[2,256,128]{2,1,0:T(8,128)(2,1)S(1)} %pad_maximum_fusion.1.mine), channel_id=1, source_target_pairs={{0,8},{8,0},{16,24},{24,16},{32,40},{40,32},{48,56},{56,48},{64,72... | collective-permute-start | bytes 393224 | tf_op jit(solution)/shard_map/ppermute | solution.py:21
  34.1 12.2 %copy-start = (bf16[8,2,8192]{2,1,0:T(2,128)(2,1)S(1)}, bf16[8,2,8192]{2,1,0:T(2,128)(2,1)}, u32[]{:S(2)}) copy-start(bf16[8,2,8192]{2,1,0:T(2,128)(2,1)} %param.8) | copy-start | bytes 786436
  36.3 5.6 %collective-permute-start.7 = (bf16[16,4096]{1,0:T(8,128)(2,1)S(1)}, bf16[16,4096]{1,0:T(8,128)(2,1)S(1)}, u32[]{:S(2)}, u32[]{:S(2)}) collective-permute-start(bf16[16,4096]{1,0:T(8,128)(2,1)S(1)} %get-tuple-element.80), channel_id=1, source_target_pairs={{0,1},{1,0},{2,3},{3,2},{4,5},{5,4},{6,7},{7,6},{8,9},{9,8},{10,11... | collective-permute-start | bytes 393224 | tf_op jit(solution)/shard_map/ppermute | solution.py:21
  41.9 7.7 %collective-permute-start.10 = (bf16[16,4096]{1,0:T(8,128)(2,1)S(1)}, bf16[16,4096]{1,0:T(8,128)(2,1)S(1)}, u32[]{:S(2)}, u32[]{:S(2)}) collective-permute-start(bf16[16,4096]{1,0:T(8,128)(2,1)S(1)} %add.60), channel_id=1, source_target_pairs={{0,4},{1,5},{2,6},{3,7},{4,0},{5,1},{6,2},{7,3},{8,12},{9,13},{10,... | collective-permute-start | bytes 393224 | tf_op jit(solution)/shard_map/ppermute | solution.py:21
  45.2 6.2 %collective-permute-start.8 = (bf16[16,4096]{1,0:T(8,128)(2,1)S(1)}, bf16[16,4096]{1,0:T(8,128)(2,1)S(1)}, u32[]{:S(2)}, u32[]{:S(2)}) collective-permute-start(bf16[16,4096]{1,0:T(8,128)(2,1)S(1)} %add.60), channel_id=1, source_target_pairs={{0,2},{1,3},{2,0},{3,1},{4,6},{5,7},{6,4},{7,5},{8,10},{9,11},{10,... | collective-permute-start | bytes 393224 | tf_op jit(solution)/shard_map/ppermute | solution.py:21
  45.9 6.2 %collective-permute-start.9 = (bf16[16,4096]{1,0:T(8,128)(2,1)S(1)}, bf16[16,4096]{1,0:T(8,128)(2,1)S(1)}, u32[]{:S(2)}, u32[]{:S(2)}) collective-permute-start(bf16[16,4096]{1,0:T(8,128)(2,1)S(1)} %add.60), channel_id=1, source_target_pairs={{0,6},{1,7},{2,4},{3,5},{4,2},{5,3},{6,0},{7,1},{8,14},{9,15},{10,... | collective-permute-start | bytes 393224 | tf_op jit(solution)/shard_map/ppermute | solution.py:21
  52.2 5.1 %collective-permute-start.11 = (bf16[16,4096]{1,0:T(8,128)(2,1)S(1)}, bf16[16,4096]{1,0:T(8,128)(2,1)S(1)}, u32[]{:S(2)}, u32[]{:S(2)}) collective-permute-start(bf16[16,4096]{1,0:T(8,128)(2,1)S(1)} %add_convert_fusion), channel_id=1, source_target_pairs={{0,1},{1,0},{2,3},{3,2},{4,5},{5,4},{6,7},{7,6},{8,9},{9,8},{10,11... | collective-permute-start | bytes 393224 | tf_op jit(solution)/shard_map/ppermute | solution.py:21
